TPU v7x, 32 devices: a whole 2x2x4 slice. The times are simulated.
32 devices in a mesh: req: 4 (over y, core), exp: 8 (over z, x).
Axes of the slice: x: 2, y: 2, z: 4, core: 2. Of those that a mesh axis runs over, the one named last changes fastest.
Arguments:
- hidden_in: bfloat16 [4096, 2048], P(('req', 'exp')), may hold values from -6 to 6
- qkv: bfloat16 [4096, 6144], P(('req', 'exp'))
- q_gain: float32 [128], replicated, as said below
- k_gain: float32 [128], replicated, as said below
- query_pages: bfloat16 [4, 8, 128, 4096], P('req', None, None, 'exp'), may hold values from -6 to 6
- page_table: int32 [4, 8], P('req'), may hold values from 0 to 7, each once within a row
- doc_lengths: int32 [4, 32], P('req'), may hold values from 1 to 128, 1024 in all within a row
- doc_query: int32 [4, 32], P('req'), may hold values from 0 to 7
- out_weight: bfloat16 [2048, 2048], replicated, may hold values from -0.125 to 0.125
- moe_gain: float32 [2048], replicated, may hold values from 0.5 to 1.5
- routes: int32 [4096, 8], P(('req', 'exp')), may hold values from 0 to 15, all different within a row; in each aligned block of 128 rows (0 to 127, 128 to 255, ...) at most 96 rows name the same one
- route_weight: float32 [4096, 8], P(('req', 'exp')), may hold values from 0.02 to 0.25
- gate_weight: bfloat16 [32, 2048, 512], P(('req', 'exp')), may hold values from -0.125 to 0.125
- up_weight: bfloat16 [32, 2048, 512], P(('req', 'exp')), may hold values from -0.125 to 0.125
- down_weight: bfloat16 [32, 512, 2048], P(('req', 'exp')), may hold values from -0.1875 to 0.1875
- score_weight: float32 [2048], replicated, may hold values from -0.125 to 0.125
Outputs:
- layer_out: bfloat16 [4096, 2048], P(('req', 'exp'))
- doc_scores: float32 [4, 32], P('req')
Inputs may be any that keep to these rules, and one draw needn't show every extreme that they name: Among the routes of the rows of one device no expert is named more than 96 times; in every draw some device's rows name some expert exactly 96 times. `doc_lengths`: each group's 32 lengths sum to 1024; the longest of each group is exactly 128. `page_table`: each row is a permutation of the pages. `q_gain`: Positive. `k_gain`: Positive.
All inputs are finite; a program needn't handle non-finite values.
Results may differ from a plain program's by a relative error of at most 0.012.
Values may be sent and summed in bfloat16 or wider, within the bound.
No kernel may reach another device: no remote copies, remote signals or barrier semaphores. Data moves between devices by JAX's collectives and lax.ppermute only.
A program may use at most 128 MiB of HBM per device.

v0:
```python
import jax
import jax.numpy as jnp
from jax import lax
from jax.sharding import PartitionSpec as P

HEADS = 16
HD = 128
TOP = 8
NQ = 8
PAGE = 128


eps = 1e-06
rope_base = 50000.0
neg_fill = -1e30


def padded(block, sides, width):
    for axis, dim in sides:
        count = lax.axis_size(axis)
        forward = [(i, i + 1) for i in range(count - 1)]
        backward = [(target, source) for source, target in forward]
        low = lax.ppermute(
            lax.slice_in_dim(block, block.shape[dim] - width, None, axis=dim), axis, forward
        )
        high = lax.ppermute(lax.slice_in_dim(block, 0, width, axis=dim), axis, backward)
        block = jnp.concatenate([low, block, high], axis=dim)
    return block


def rms_scale(values, gain_vec):
    mean_sq = jnp.mean(values * values, axis=-1, keepdims=True)
    return values * lax.rsqrt(mean_sq + eps) * gain_vec


def rotate(values, positions):
    half_dim = values.shape[-1] // 2
    frequency = rope_base ** (-(jnp.arange(half_dim, dtype=jnp.float32) * 2.0 / values.shape[-1]))
    angles = positions.astype(jnp.float32)[:, None] * frequency[None, :]
    cosine = jnp.cos(angles)[:, None, :]
    sine_part = jnp.sin(angles)[:, None, :]
    lower_part = values[..., :half_dim]
    upper_part = values[..., half_dim:]
    return jnp.concatenate(
        [
            lower_part * cosine - upper_part * sine_part,
            upper_part * cosine + lower_part * sine_part,
        ],
        axis=-1,
    )


def doc_table(doc_len, positions):
    doc_ends = jnp.cumsum(doc_len, dtype=jnp.int32)
    starts = doc_ends - doc_len
    doc_ids = jnp.sum(
        (positions[:, None] >= doc_ends[None, :]).astype(jnp.int32), axis=1, dtype=jnp.int32
    )
    inside = (positions >= 0) & (positions < doc_ends[-1])
    doc_ids = jnp.where(inside, doc_ids, -1)
    member = doc_ids[:, None] == jnp.arange(doc_len.shape[0], dtype=jnp.int32)[None, :]
    doc_start = jnp.sum(jnp.where(member, starts[None, :], 0), axis=1, dtype=jnp.int32)
    return (doc_ids, member, doc_start)


def page_lookup(member, doc_query, page_table):
    query_ids = jnp.sum(jnp.where(member, doc_query[None, :], 0), axis=1, dtype=jnp.int32)
    query_hit = query_ids[:, None] == jnp.arange(page_table.shape[0], dtype=jnp.int32)[None, :]
    return jnp.sum(jnp.where(query_hit, page_table[None, :], 0), axis=1, dtype=jnp.int32)


def attend(query_rows, key_rows, value_rows, visible):
    score_scale = query_rows.shape[-1] ** (-0.5)
    scores = (
        jnp.einsum("nhd,khd->hnk", query_rows, key_rows, preferred_element_type=jnp.float32)
        * score_scale
    )
    scores = jnp.where(visible[None], scores, neg_fill)
    row_max = jnp.max(scores, axis=-1)
    probs = jnp.where(visible[None], jnp.exp(scores - row_max[..., None]), 0.0)
    row_total = jnp.sum(probs, axis=-1)
    weighted = jnp.einsum(
        "hnk,khd->nhd", probs.astype(jnp.bfloat16), value_rows, preferred_element_type=jnp.float32
    )
    return (weighted, row_max.T, row_total.T)


def slot_numbers(route_flat, bin_count):
    onehot = (route_flat[:, None] == jnp.arange(bin_count, dtype=jnp.int32)[None, :]).astype(
        jnp.int32
    )
    prior_count = jnp.cumsum(onehot, axis=0, dtype=jnp.int32) - onehot
    return jnp.sum(prior_count * onehot, axis=1, dtype=jnp.int32)


def expert_piece(rows_three, gate_weight, up_weight, down_weight):
    flat_rows = rows_three.reshape(-1, rows_three.shape[-1])
    gate_act = jnp.dot(flat_rows, gate_weight[0], preferred_element_type=jnp.float32)
    up_act = jnp.dot(flat_rows, up_weight[0], preferred_element_type=jnp.float32)
    hidden_act = (jax.nn.silu(gate_act) * up_act).astype(jnp.bfloat16)
    piece_out = jnp.dot(hidden_act, down_weight[0], preferred_element_type=jnp.float32)
    return piece_out.astype(jnp.bfloat16).reshape(rows_three.shape)


def local(
    hidden_in,
    qkv,
    q_gain,
    k_gain,
    query_pages,
    page_table,
    doc_lengths,
    doc_query,
    out_weight,
    moe_gain,
    routes,
    route_weight,
    gate_weight,
    up_weight,
    down_weight,
    score_weight,
):
    tok_count = hidden_in.shape[0]
    width = hidden_in.shape[1]
    exp_count = lax.axis_size("exp")
    devices = lax.axis_size("req") * exp_count
    experts = devices // 2
    capacity = 2 * max(1, 3 * tok_count * TOP // (4 * experts))
    exp_index = lax.axis_index("exp")
    doc_len = doc_lengths[0]
    own_pos = exp_index * tok_count + jnp.arange(tok_count, dtype=jnp.int32)
    own_doc, own_member, own_start = doc_table(doc_len, own_pos)
    own_page = page_lookup(own_member, doc_query[0], page_table[0])
    rope_pos = PAGE + own_pos - own_start
    query_rows = rotate(
        rms_scale(qkv[:, :width].astype(jnp.float32).reshape(tok_count, HEADS, HD), q_gain),
        rope_pos,
    ).astype(jnp.bfloat16)
    key_rows = rotate(
        rms_scale(
            qkv[:, width : 2 * width].astype(jnp.float32).reshape(tok_count, HEADS, HD), k_gain
        ),
        rope_pos,
    ).astype(jnp.bfloat16)
    kv_local = jnp.concatenate([key_rows.reshape(tok_count, width), qkv[:, 2 * width :]], axis=1)
    window = padded(kv_local, (("exp", 0),), tok_count)
    win_pos = (exp_index - 1) * tok_count + jnp.arange(3 * tok_count, dtype=jnp.int32)
    win_doc, win_member, win_start = doc_table(doc_len, win_pos)
    win_keys = window[:, :width].reshape(3 * tok_count, HEADS, HD)
    win_values = window[:, width:].reshape(3 * tok_count, HEADS, HD)
    win_visible = win_doc[None, :] == own_doc[:, None]
    key_page = jnp.arange(NQ * PAGE, dtype=jnp.int32) // PAGE
    page_rows = lax.all_gather(query_pages[0], "exp", axis=2, tiled=True).reshape(
        NQ * PAGE, HEADS, 2, HD
    )
    all_keys = jnp.concatenate([page_rows[:, :, 0], win_keys], axis=0)
    all_values = jnp.concatenate([page_rows[:, :, 1], win_values], axis=0)
    visible = jnp.concatenate([key_page[None, :] == own_page[:, None], win_visible], axis=1)
    weighted, row_max, row_total = attend(query_rows, all_keys, all_values, visible)
    attn = weighted / row_total[..., None]
    attn = attn.astype(jnp.bfloat16).reshape(tok_count, width)
    mixed = jnp.dot(attn, out_weight, preferred_element_type=jnp.float32)
    resid = (hidden_in.astype(jnp.float32) + mixed).astype(jnp.bfloat16)
    normed = rms_scale(resid.astype(jnp.float32), moe_gain).astype(jnp.bfloat16)
    route_flat = routes.reshape(-1)
    slots = slot_numbers(route_flat, experts)
    place = route_flat * capacity + slots
    token_ids = jnp.arange(tok_count * TOP, dtype=jnp.int32) // TOP
    slot_tokens = jnp.full((experts * capacity,), tok_count, jnp.int32).at[place].set(token_ids)
    padded_rows = jnp.concatenate([normed, jnp.zeros((1, width), jnp.bfloat16)], axis=0)
    outgoing = padded_rows[slot_tokens].reshape(experts, capacity, width)
    doubled = jnp.broadcast_to(outgoing[:, None], (experts, 2, capacity, width)).reshape(
        2 * experts, capacity, width
    )
    arrived = lax.all_to_all(doubled, ("req", "exp"), split_axis=0, concat_axis=0, tiled=True)
    partial_value = expert_piece(arrived, gate_weight, up_weight, down_weight)
    returned = lax.all_to_all(
        partial_value, ("req", "exp"), split_axis=0, concat_axis=0, tiled=True
    ).reshape(experts, 2, capacity, width)
    results = (returned[:, 0].astype(jnp.float32) + returned[:, 1].astype(jnp.float32)).astype(
        jnp.bfloat16
    )
    picked = results.reshape(experts * capacity, width)[place].reshape(tok_count, TOP, width)
    combined = jnp.einsum("tk,tkd->td", route_weight, picked.astype(jnp.float32))
    layer_out = (resid.astype(jnp.float32) + combined).astype(jnp.bfloat16)
    token_score = jnp.dot(
        layer_out.astype(jnp.float32), score_weight, precision=lax.Precision.HIGHEST
    )
    doc_partial = jnp.dot(
        token_score, own_member.astype(jnp.float32), precision=lax.Precision.HIGHEST
    )
    doc_sums = lax.psum(doc_partial, "exp")
    doc_scores = (doc_sums / doc_len.astype(jnp.float32))[None, :]
    return (layer_out, doc_scores)


def solution(mesh):
    in_specs = (
        P(("req", "exp"), None),
        P(("req", "exp"), None),
        P(),
        P(),
        P("req", None, None, "exp"),
        P("req", None),
        P("req", None),
        P("req", None),
        P(),
        P(),
        P(("req", "exp"), None),
        P(("req", "exp"), None),
        P(("req", "exp"), None, None),
        P(("req", "exp"), None, None),
        P(("req", "exp"), None, None),
        P(),
    )
    out_specs = (P(("req", "exp"), None), P("req", None))
    return jax.shard_map(local, mesh=mesh, in_specs=in_specs, out_specs=out_specs, check_vma=False)
```

profile of v0, /device:TPU:0, one launch (start us, length us, event | category | flops | bytes accessed | tf_op | source)
XLA Modules:
  0.0 918.6 jit_solution(15825828197544896715)
XLA Ops:
  7.3 0.7 all-gather.3.cloned.1.call-update
  8.0 0.7 copy.46
  8.9 0.5 slice.72
  9.4 2.5 fusion.57
  12.2 1.2 copy.45
  13.4 1.3 copy.68
  14.7 1.3 copy.50
  16.1 0.7 and_select_fusion.1
  17.2 0.3 multiply_cosine_fusion
  17.5 1.9 multiply_multiply_fusion
  19.4 1.7 subtract_convert_fusion
  21.7 1.3 copy.67
  23.0 1.1 pad_maximum_fusion.1
  24.2 5.9 collective-permute-start
  30.1 1.3 collective-permute-start.1
  31.7 4.5 reduce-window.11
  36.9 4.5 scatter_custom_fusion
  41.7 0.6 and_select_fusion
  42.6 35.4 %collective-permute-done = bf16[128,4096]{0,1:T(8,128)(2,1)} collective-permute-done((bf16[128,4096]{0,1:T(8,128)(2,1)}, bf16[128,4096]{0,1:T(8,128)(2,1)}, u32[]{:S(2)}, u32[]{:S(2)}) %collective-permute-start) | collective-permute-done | bytes 1048608 | tf_op jit(solution)/shard_map/ppermute | solution.py:23
  78.0 6.6 pad_maximum_fusion
  84.6 2.1 fusion.56
  86.7 2.6 copy.52
  89.3 75.8 %all-gather.3.cloned.1.call-done = bf16[1,8,128,4096]{3,2,1,0:T(8,128)(2,1)} async-done(((bf16[1,8,128,512]{3,2,1,0:T(8,128)(2,1)}), bf16[1,8,128,4096]{3,2,1,0:T(8,128)(2,1)}) %all-gather.3.cloned.1.call-update) | async-done | bytes 8388624 | tf_op jit(solution)/shard_map/all_gather | solution.py:153
  165.0 14.3 %reshape.297 = bf16[1024,16,2,128]{3,2,1,0:T(2,128)(2,1)} reshape(bf16[1,8,128,4096]{3,2,1,0:T(8,128)(2,1)} %all-gather.3.cloned.1.call-done) | data formatting | bytes 16777216 | tf_op jit(solution)/shard_map/reshape | solution.py:153
  179.4 17.2 %fusion.55 = (bf16[1024,16,1,128]{3,2,1,0:T(2,128)(2,1)}, bf16[1024,16,1,128]{3,2,1,0:T(2,128)(2,1)S(1)}) fusion(bf16[1024,16,2,128]{3,2,1,0:T(2,128)(2,1)} %reshape.297), kind=kLoop, calls=%fused_computation.114 | loop fusion | bytes 16777216 | tf_op jit(solution)/shard_map/slice | solution.py:157
  196.6 4.7 copy.76
  201.4 20.1 %copy.65 = bf16[1024,16,1,128]{0,3,1,2:T(8,128)(2,1)} copy(bf16[1024,16,1,128]{3,2,1,0:T(2,128)(2,1)} %get-tuple-element.4) | data formatting | bytes 8388608
  221.5 9.1 fusion.6
  230.5 14.1 %fusion.58 = (f32[16,128]{1,0:T(8,128)S(1)}, bf16[16,128,1408]{2,1,0:T(8,128)(2,1)}) fusion(f32[16,128,1408]{2,1,0:T(8,128)} %fusion.6, pred[128,1408]{1,0:T(8,128)(4,1)S(1)} %pad_add_fusion), kind=kOutput, calls=%fused_computation.117 | output fusion | flops 23070080 | bytes 17489920 | tf_op jit(solution)/shard_map/sub | solution.py:80
  244.6 6.3 divide_convert_fusion
  250.9 2.4 multiply_reduce_fusion
  253.4 1.0 copy-done.2
  254.5 7.1 gather_fusion
  261.6 5.2 broadcast_in_dim.129
  266.9 277.4 %all_to_all.10 = bf16[32,96,2048]{2,1,0:T(8,128)(2,1)S(1)} all-to-all(bf16[32,96,2048]{2,1,0:T(8,128)(2,1)S(1)} %bitcast.105), channel_id=1, replica_groups=mesh['req'=4,'exp'=8] {'req','exp'}, dimensions={0} | all-to-all | bytes 25165824 | tf_op jit(solution)/shard_map/all_to_all | solution.py:175
  544.2 4.5 copy-done.1
  548.7 8.8 fusion.21
  557.5 21.0 %convolution_convert_fusion = bf16[3072,2048]{1,0:T(8,128)(2,1)} fusion(bf16[1,512,2048]{2,1,0:T(8,128)(2,1)S(1)} %copy-done, f32[3072,512]{1,0:T(8,128)} %fusion.21, bf16[3072,2048]{1,0:T(8,128)(2,1)} %bitcast.112, bf16[1,2048,512]{2,1,0:T(8,128)(2,1)} %param.29), kind=kOutput, calls=%fused_computation.7 | convolution fusion | flops 12900630528 | bytes 35651584 | tf_op jit(solution)/shard_map/dot_general | solution.py:101
  578.5 4.2 all-to-all-start.1
  582.9 278.8 %all-to-all-done.1 = bf16[32,96,2048]{2,1,0:T(8,128)(2,1)} async-done(((bf16[32,96,2048]{2,1,0:T(8,128)(2,1)}), bf16[32,96,2048]{2,1,0:T(8,128)(2,1)}, u32[]{:S(2)}, u32[]{:S(2)}) %all-to-all-start.1) | async-done | bytes 12582944 | tf_op jit(solution)/shard_map/all_to_all | solution.py:177
  861.7 9.2 %add_convert_fusion = bf16[16,1,96,2048]{3,2,0,1:T(8,128)(2,1)} fusion(bf16[16,2,96,2048]{3,2,1,0:T(8,128)(2,1)} %bitcast.28), kind=kLoop, calls=%fused_computation.4 | loop fusion | flops 12582912 | bytes 18874368 | tf_op jit(solution)/shard_map/convert_element_type | solution.py:180
  870.9 12.5 %gather_fusion.1 = bf16[1024,2048]{1,0:T(8,128)(2,1)} fusion(bf16[1536,2048]{1,0:T(8,128)(2,1)} %bitcast.104, s32[1024]{0:T(1024)S(1)} %broadcast_clamp_fusion), kind=kCustom, calls=%fused_computation.1 | custom fusion | bytes 8392704 | tf_op jit(solution)/shard_map/gather | solution.py:183
  883.4 3.4 fusion.14
  886.8 0.5 fusion.28
  887.4 0.8 copy-done.6
  888.1 0.5 convolution_bitcast_fusion.1
  888.8 22.4 %psum.7 = f32[32]{0:T(128)S(1)} all-reduce(f32[32]{0:T(128)S(1)} %convolution_bitcast_fusion), channel_id=1, replica_groups=mesh['req'=4,'exp'=8] {'exp'}, use_global_device_ids=true, to_apply=%region_15.16 | all-reduce | flops 32 | bytes 256 | tf_op jit(solution)/shard_map/psum | solution.py:192
  911.2 0.5 fusion.49
  (84 shorter events, 3.5 us)
Async XLA Ops:
  7.2 550.3 %copy-start = (bf16[1,512,2048]{2,1,0:T(8,128)(2,1)S(1)}, bf16[1,512,2048]{2,1,0:T(8,128)(2,1)}, u32[]{:S(2)}) copy-start(bf16[1,512,2048]{2,1,0:T(8,128)(2,1)} %param.30) | copy-start | bytes 6291460
  7.2 9.6 %copy-start.14 = (s32[1,32]{1,0:T(1,128)S(1)}, s32[1,32]{1,0:T(1,128)}, u32[]{:S(2)}) copy-start(s32[1,32]{1,0:T(1,128)} %param.22) | copy-start | bytes 388
  7.2 9.6 %copy-start.13 = (s32[1,32]{1,0:T(1,128)S(1)}, s32[1,32]{1,0:T(1,128)}, u32[]{:S(2)}) copy-start(s32[1,32]{1,0:T(1,128)} %param.23) | copy-start | bytes 388
  7.2 10.3 %copy-start.11 = (f32[128]{0:T(128)S(1)}, f32[128]{0:T(128)}, u32[]{:S(2)}) copy-start(f32[128]{0:T(128)} %param.18) | copy-start | bytes 1540
  7.2 10.3 %copy-start.12 = (f32[128]{0:T(128)S(1)}, f32[128]{0:T(128)}, u32[]{:S(2)}) copy-start(f32[128]{0:T(128)} %param.19) | copy-start | bytes 1540
  7.2 157.8 %all-gather.3.cloned.1.call-start = ((), (), s32[]{:S(2)}) async-start(), calls=%async_computation.2 | async-start | bytes 9437184 | tf_op jit(solution)/shard_map/all_gather | solution.py:153
  19.4 12.0 %copy-start.7 = (s32[128,8]{0,1:T(8,128)S(1)}, s32[128,8]{0,1:T(8,128)}, u32[]{:S(2)}) copy-start(s32[128,8]{0,1:T(8,128)} %param.26) | copy-start | bytes 12292
  19.4 22.1 %copy-start.16 = (s32[1,8]{1,0:T(1,128)S(1)}, s32[1,8]{1,0:T(1,128)}, u32[]{:S(2)}) copy-start(s32[1,8]{1,0:T(1,128)} %param.21) | copy-start | bytes 100
  24.2 53.8 %collective-permute-start = (bf16[128,4096]{0,1:T(8,128)(2,1)}, bf16[128,4096]{0,1:T(8,128)(2,1)}, u32[]{:S(2)}, u32[]{:S(2)}) collective-permute-start(bf16[128,4096]{0,1:T(8,128)(2,1)} %pad_maximum_fusion.1), channel_id=1, source_target_pairs={{0,1},{1,2},{2,3},{3,4},{4,5},{5,6},{6,7},{8,9},{9,10},{10,11},{11... | collective-permute-start | bytes 3145736 | tf_op jit(solution)/shard_map/ppermute | solution.py:23
  30.1 47.9 %collective-permute-start.1 = (bf16[128,4096]{0,1:T(8,128)(2,1)}, bf16[128,4096]{0,1:T(8,128)(2,1)}, u32[]{:S(2)}, u32[]{:S(2)}) collective-permute-start(bf16[128,4096]{0,1:T(8,128)(2,1)} %pad_maximum_fusion.1), channel_id=1, source_target_pairs={{1,0},{2,1},{3,2},{4,3},{5,4},{6,5},{7,6},{9,8},{10,9},{11,10},{12... | collective-permute-start | bytes 3145736 | tf_op jit(solution)/shard_map/ppermute | solution.py:26
  201.3 20.1 %copy-start.4 = (bf16[128,16,64]{2,0,1:T(8,128)(2,1)S(1)}, bf16[128,16,64]{2,0,1:T(8,128)(2,1)}, u32[]{:S(2)}) copy-start(bf16[128,16,64]{2,0,1:T(8,128)(2,1)} %get-tuple-element.11) | copy-start | bytes 786436
  201.4 20.1 %copy-start.5 = (bf16[128,16,64]{2,0,1:T(8,128)(2,1)S(1)}, bf16[128,16,64]{2,0,1:T(8,128)(2,1)}, u32[]{:S(2)}) copy-start(bf16[128,16,64]{2,0,1:T(8,128)(2,1)} %get-tuple-element.12) | copy-start | bytes 786436
  221.4 29.4 %slice-start = ((s8[8388608]{0:T(1024)(128)(4,1)}), s8[4194304]{0:T(1024)(128)(4,1)S(1)}, s32[]{:S(2)}) async-start(s8[8388608]{0:T(1024)(128)(4,1)} %bitcast.106), calls=%async_computation.3 | async-start | bytes 8388608
  230.5 20.4 %slice-start.1 = ((s8[8388608]{0:T(1024)(128)(4,1)}), s8[4194304]{0:T(1024)(128)(4,1)S(1)}, s32[]{:S(2)}) async-start(s8[8388608]{0:T(1024)(128)(4,1)} %bitcast.106), calls=%async_computation.4 | async-start | bytes 8388608
  250.9 3.4 copy-start.8
  253.3 1.0 copy-start.2
  266.9 281.9 %copy-start.15 = (bf16[1,2048,512]{2,1,0:T(8,128)(2,1)S(1)}, bf16[1,2048,512]{2,1,0:T(8,128)(2,1)}, u32[]{:S(2)}) copy-start(bf16[1,2048,512]{2,1,0:T(8,128)(2,1)} %param.28) | copy-start | bytes 6291460
  544.2 4.5 copy-start.1
  578.5 4.2 copy-start.10
  578.5 283.2 %all-to-all-start.1 = ((bf16[32,96,2048]{2,1,0:T(8,128)(2,1)}), bf16[32,96,2048]{2,1,0:T(8,128)(2,1)}, u32[]{:S(2)}, u32[]{:S(2)}) async-start(bf16[32,96,2048]{2,1,0:T(8,128)(2,1)} %bitcast.110), calls=%async_computation.1 | async-start | bytes 25165824 | tf_op jit(solution)/shard_map/all_to_all | solution.py:177
  870.9 15.9 %copy-start.3 = (f32[128,2048]{1,0:T(8,128)S(1)}, f32[128,2048]{1,0:T(8,128)}, u32[]{:S(2)}) copy-start(f32[128,2048]{1,0:T(8,128)} %copy-done.2) | copy-start | bytes 3145732
  883.4 4.7 copy-start.9
  887.3 0.8 copy-start.6
Sparse Core Ops, SparseCore 0:
  10.1 154.8 all-gather.2
where the time goes:
time: 920 us; the launch traced here: 919 us
  waiting for transfers between devices  391 us (42%)
  blocking collectives  300 us (33%)
  local copies, waits for them, and re-layouts  107 us (12%)
  matrix products  51.6 us (6%)
  other arithmetic  43.5 us (5%)
  between operations  14.5 us (2%)
  starting transfers between devices  11.5 us (1%)
    all_to_all x1, waiting for transfers between devices, local(): lax.all_to_all(partial_value, ('req', 'exp'), split_axis=0, concat_axis=0...  279 us
    all_to_all x1, blocking collectives, local(): lax.all_to_all(doubled, ('req', 'exp'), split_axis=0, concat_axis=0, tile...  277 us
    all_gather x1, waiting for transfers between devices, local(): lax.all_gather(query_pages[0], 'exp', axis=2, tiled=True)  75.8 us
    ppermute x1, waiting for transfers between devices, padded(): lax.ppermute(lax.slice_in_dim(block, block.shape[dim] - width, None, axis...  35.4 us
    unnamed x45, local copies, waits for them, and re-layouts  34.3 us
    psum x1, blocking collectives, local(): doc_sums = lax.psum(doc_partial, 'exp')  22.4 us
    dot_general x1, matrix products, expert_piece(): jnp.dot(hidden_act, down_weight[0], preferred_element_type=jnp.float32)  21 us
  transfers between devices with their start and end apart: 4, of which 3 were waited for; matrix products, arithmetic and copies ran while one was open for 4% of the time, Pallas kernels for 0%

commit v1 on v0

v1 whole, which is shorter than its diff:
```python
import functools

import jax
import jax.numpy as jnp
import numpy as np
from jax import lax
from jax.experimental import pallas as pl
from jax.experimental.pallas import tpu as pltpu
from jax.sharding import PartitionSpec as P

HEADS = 16
HD = 128
TOP = 8
PAGE = 128
LANES = 128
ALL = ("req", "exp")


eps = 1e-06
rope_base = 50000.0
neg_fill = -1e30


def rms_scale(values, gain_vec):
    mean_sq = jnp.mean(values * values, axis=-1, keepdims=True)
    return values * lax.rsqrt(mean_sq + eps) * gain_vec


def rope_table():
    half_dim = HD // 2
    frequency = rope_base ** (-(np.arange(half_dim) * 2.0 / HD))
    angles = (PAGE + np.arange(PAGE))[:, None] * frequency[None, :]
    cosine, sine = np.cos(angles), np.sin(angles)
    rest = np.concatenate([cosine, cosine, -sine, sine], axis=1).astype(np.float32)
    terms = []
    for _ in range(3):
        term = rest.astype(jnp.bfloat16)
        terms.append(term)
        rest = rest - term.astype(np.float32)
    return np.concatenate(terms, axis=1)


def attention_kernel(
    qkv_ref, pages_ref, len_ref, query_ref, table_ref, q_gain_ref, k_gain_ref, rope_ref,
    out_ref, q_rows, k_rows,
):
    tokens = qkv_ref.shape[0]
    heads = qkv_ref.shape[1] // (3 * HD)
    blocks = tokens // LANES
    keys = pages_ref.shape[0]
    score_scale = HD ** (-0.5) * 1.4426950408889634

    row_ids = lax.broadcasted_iota(jnp.int32, (LANES, LANES), 0)
    lane_ids = lax.broadcasted_iota(jnp.int32, (LANES, LANES), 1)
    lane_f32 = lane_ids.astype(jnp.float32)
    upper = (row_ids <= lane_ids).astype(jnp.bfloat16)
    lens = jnp.broadcast_to(len_ref[...].astype(jnp.bfloat16), (16, LANES))
    ends = jnp.dot(lens, upper, preferred_element_type=jnp.float32)[0:1]
    slot = lax.broadcasted_iota(jnp.int32, (table_ref.shape[0], LANES), 0)
    doc_page = jnp.sum(
        jnp.where(slot == query_ref[...], table_ref[...], 0).astype(jnp.float32),
        axis=0, keepdims=True,
    )

    def places(block):
        own = (row_ids + block * LANES).astype(jnp.float32)
        passed = own >= ends
        start = jnp.max(jnp.where(passed, ends, 0.0), axis=1, keepdims=True)
        stop = jnp.min(jnp.where(passed, 1e9, ends), axis=1, keepdims=True)
        doc = jnp.sum(passed.astype(jnp.float32), axis=1, keepdims=True)
        page = jnp.sum(jnp.where(lane_f32 == doc, doc_page, 0.0), axis=1, keepdims=True)
        return own, start, stop, page

    @pl.loop(0, blocks)
    def _(block):
        rows = pl.ds(pl.multiple_of(block * LANES, LANES), LANES)
        own, start, _, _ = places(block)
        onehot = (lane_f32 == own - start).astype(jnp.bfloat16)
        terms = jnp.dot(onehot, rope_ref[...], preferred_element_type=jnp.float32)
        both = terms[:, : 2 * HD] + (terms[:, 2 * HD : 4 * HD] + terms[:, 4 * HD :])
        cosine, sine = both[:, :HD], both[:, HD:]
        for part, gain_ref, kept in ((0, q_gain_ref, q_rows), (1, k_gain_ref, k_rows)):
            for head in range(heads):
                at = (part * heads + head) * HD
                values = qkv_ref[rows, at : at + HD].astype(jnp.float32)
                values = rms_scale(values, gain_ref[...])
                swapped = pltpu.roll(values, HD // 2, 1)
                kept[rows, head * HD : (head + 1) * HD] = (
                    values * cosine + swapped * sine
                ).astype(jnp.bfloat16)

    page_of_key = (
        lax.broadcasted_iota(jnp.int32, (LANES, keys), 1) // PAGE
    ).astype(jnp.float32)
    wide = 3 * LANES
    key_at = lax.broadcasted_iota(jnp.int32, (LANES, wide), 1)

    @pl.loop(0, blocks)
    def _(block):
        rows = pl.ds(pl.multiple_of(block * LANES, LANES), LANES)
        first = pl.multiple_of(jnp.clip(block - 1, 0, blocks - 3) * LANES, LANES)
        window = pl.ds(first, wide)
        _, start, stop, page = places(block)
        position = (key_at + first).astype(jnp.float32)
        in_page = page_of_key == page
        in_doc = (position >= start) & (position < stop)
        for head in range(heads):
            cols = slice(head * HD, (head + 1) * HD)
            query = q_rows[rows, cols]
            page_keys = pages_ref[:, 2 * head * HD : (2 * head + 1) * HD]
            page_values = pages_ref[:, (2 * head + 1) * HD : (2 * head + 2) * HD]
            at = (2 * heads + head) * HD
            contract = (((1,), (1,)), ((), ()))
            far = lax.dot_general(
                query, page_keys, contract, preferred_element_type=jnp.float32
            )
            near = lax.dot_general(
                query, k_rows[window, cols], contract, preferred_element_type=jnp.float32
            )
            far = jnp.where(in_page, far, neg_fill)
            near = jnp.where(in_doc, near, neg_fill)
            top = jnp.maximum(
                jnp.max(far, axis=1, keepdims=True), jnp.max(near, axis=1, keepdims=True)
            )
            far = jnp.exp2((far - top) * score_scale)
            near = jnp.exp2((near - top) * score_scale)
            total = jnp.sum(far, axis=1, keepdims=True) + jnp.sum(near, axis=1, keepdims=True)
            weighted = jnp.dot(
                far.astype(jnp.bfloat16), page_values, preferred_element_type=jnp.float32
            ) + jnp.dot(
                near.astype(jnp.bfloat16),
                qkv_ref[window, at : at + HD],
                preferred_element_type=jnp.float32,
            )
            out_ref[rows, cols] = (weighted / total).astype(jnp.bfloat16)


def column_block(exp_count, part, index):
    return (0, part * exp_count + index)


def pack_kernel(q_ref, k_ref, v_ref, out_ref):
    out_ref[...] = jnp.concatenate([q_ref[...], k_ref[...], v_ref[...]], axis=1)


def attention(qkv, q_gain, k_gain, pages, page_table, doc_len, doc_query):
    tok_count, width = qkv.shape[0], qkv.shape[1] // 3
    exp_count = lax.axis_size("exp")
    own = width // exp_count
    tokens = exp_count * tok_count
    parts = pl.pallas_call(
        pack_kernel,
        grid=(exp_count,),
        out_shape=jax.ShapeDtypeStruct((tokens, 3 * own), jnp.bfloat16),
        in_specs=[
            pl.BlockSpec((tok_count, own), functools.partial(column_block, exp_count, part))
            for part in range(3)
        ],
        out_specs=pl.BlockSpec((tok_count, 3 * own), lambda i: (i, 0)),
        name="pack_heads",
    )(qkv, qkv, qkv)
    group = lax.all_to_all(parts, "exp", split_axis=0, concat_axis=0, tiled=True)
    docs = doc_len.shape[1]
    spare = ((0, 0), (0, LANES - docs))
    out = pl.pallas_call(
        attention_kernel,
        out_shape=jax.ShapeDtypeStruct((tokens, own), jnp.bfloat16),
        scratch_shapes=[
            pltpu.VMEM((tokens, own), jnp.bfloat16),
            pltpu.VMEM((tokens, own), jnp.bfloat16),
        ],
        compiler_params=pltpu.CompilerParams(vmem_limit_bytes=32 * 1024 * 1024),
        name="paged_attention",
    )(
        group,
        pages.reshape(-1, 2 * own),
        jnp.pad(doc_len, spare),
        jnp.pad(doc_query, spare, constant_values=-1),
        page_table.reshape(-1, 1),
        q_gain.reshape(1, HD),
        k_gain.reshape(1, HD),
        jnp.asarray(rope_table()),
    )
    back = lax.all_to_all(out, "exp", split_axis=0, concat_axis=0, tiled=True)
    return back.reshape(exp_count, tok_count, own)


def expert_kernel(rows_ref, scale_ref, gate_ref, up_ref, down_ref, out_ref):
    rows = rows_ref[...]
    gate_act = jnp.dot(rows, gate_ref[0], preferred_element_type=jnp.float32)
    up_act = jnp.dot(rows, up_ref[0], preferred_element_type=jnp.float32)
    hidden_act = jax.nn.silu(gate_act) * (up_act * scale_ref[...])
    out_ref[...] = jnp.dot(
        hidden_act.astype(jnp.bfloat16), down_ref[0], preferred_element_type=jnp.float32
    ).astype(jnp.bfloat16)


def weighted_piece(rows, scale, gate_weight, up_weight, down_weight):
    count, width = rows.shape
    hidden = gate_weight.shape[2]
    tile = 256
    once = pl.Buffered(1)
    return pl.pallas_call(
        expert_kernel,
        grid=(count // tile,),
        out_shape=jax.ShapeDtypeStruct(rows.shape, jnp.bfloat16),
        in_specs=[
            pl.BlockSpec((tile, width), lambda i: (i, 0)),
            pl.BlockSpec((tile, 1), lambda i: (i, 0)),
            pl.BlockSpec((1, width, hidden), lambda i: (0, 0, 0), pipeline_mode=once),
            pl.BlockSpec((1, width, hidden), lambda i: (0, 0, 0), pipeline_mode=once),
            pl.BlockSpec((1, hidden, width), lambda i: (0, 0, 0), pipeline_mode=once),
        ],
        out_specs=pl.BlockSpec((tile, width), lambda i: (i, 0)),
        compiler_params=pltpu.CompilerParams(vmem_limit_bytes=24 * 1024 * 1024),
        cost_estimate=pl.CostEstimate(
            flops=6 * count * width * hidden,
            bytes_accessed=4 * count * width + 6 * width * hidden,
            transcendentals=count * hidden,
        ),
        name="expert_half",
    )(rows, scale, gate_weight, up_weight, down_weight)


def expert_piece(rows, gate_weight, up_weight, down_weight):
    gate_act = jnp.dot(rows, gate_weight[0], preferred_element_type=jnp.float32)
    up_act = jnp.dot(rows, up_weight[0], preferred_element_type=jnp.float32)
    hidden_act = jax.nn.silu(gate_act) * up_act
    piece_out = jnp.dot(
        hidden_act.astype(jnp.bfloat16), down_weight[0], preferred_element_type=jnp.float32
    )
    return piece_out.astype(jnp.bfloat16)


def slot_numbers(route_flat, bin_count):
    onehot = (route_flat[:, None] == jnp.arange(bin_count, dtype=jnp.int32)[None, :]).astype(
        jnp.int32
    )
    prior_count = jnp.cumsum(onehot, axis=0, dtype=jnp.int32) - onehot
    return jnp.sum(prior_count * onehot, axis=1, dtype=jnp.int32)


def experts_by_slots(normed, routes, route_weight, gate_weight, up_weight, down_weight):
    tok_count, width = normed.shape
    devices = lax.axis_size("req") * lax.axis_size("exp")
    experts = devices // 2
    capacity = 2 * max(1, 3 * tok_count * TOP // (4 * experts))
    route_flat = routes.reshape(-1)
    slots = slot_numbers(route_flat, experts)
    place = route_flat * capacity + slots
    token_ids = jnp.arange(tok_count * TOP, dtype=jnp.int32) // TOP
    slot_tokens = jnp.full((experts * capacity,), tok_count, jnp.int32).at[place].set(token_ids)
    padded_rows = jnp.concatenate([normed, jnp.zeros((1, width), jnp.bfloat16)], axis=0)
    outgoing = padded_rows[slot_tokens].reshape(experts, capacity, width)
    doubled = jnp.broadcast_to(outgoing[:, None], (experts, 2, capacity, width)).reshape(
        2 * experts, capacity, width
    )
    arrived = lax.all_to_all(doubled, ALL, split_axis=0, concat_axis=0, tiled=True)
    pieces = expert_piece(arrived.reshape(-1, width), gate_weight, up_weight, down_weight)
    returned = lax.all_to_all(
        pieces.reshape(arrived.shape), ALL, split_axis=0, concat_axis=0, tiled=True
    ).reshape(experts, 2, capacity, width)
    results = (returned[:, 0].astype(jnp.float32) + returned[:, 1].astype(jnp.float32)).astype(
        jnp.bfloat16
    )
    picked = results.reshape(experts * capacity, width)[place].reshape(tok_count, TOP, width)
    return jnp.einsum("tk,tkd->td", route_weight, picked.astype(jnp.float32))


GRID = (2, 2, 4)


def device_number(x, y, z, core):
    return ((y * 2 + core) * GRID[2] + z) * GRID[0] + x


def pairs(target):
    found = []
    for y in range(GRID[1]):
        for core in range(2):
            for z in range(GRID[2]):
                for x in range(GRID[0]):
                    to = target(x, y, z, core)
                    if to is not None:
                        found.append((device_number(x, y, z, core), device_number(*to)))
    return found


def move(block, target):
    return lax.ppermute(block, ALL, pairs(target))


def over_x(x, y, z, core):
    return (1 - x, y, z, core)


def over_y(x, y, z, core):
    return (x, 1 - y, z, core)


def over_core(x, y, z, core):
    return (x, y, z, 1 - core)


def z_pair(x, y, z, core):
    return (x, y, z ^ 1, core)


def z_far(x, y, z, core):
    return (x, y, z ^ 2, core)


def z_middle(x, y, z, core):
    return (x, y, 3 - z, core) if z in (1, 2) else None


def z_outward(x, y, z, core):
    return (x, y, {1: 0, 2: 3}[z], core) if z in (1, 2) else None


def z_inward(x, y, z, core):
    return (x, y, {0: 1, 3: 2}[z], core) if z in (0, 3) else None


def experts_dense(normed, routes, route_weight, gate_weight, up_weight, down_weight):
    f32 = jnp.float32
    tok_count = normed.shape[0]
    req, exp = lax.axis_index("req"), lax.axis_index("exp")
    z = exp // GRID[0]
    devices = lax.axis_size("req") * lax.axis_size("exp")
    experts = devices // 2
    chosen = routes.T[None] == jnp.arange(experts, dtype=jnp.int32)[:, None, None]
    dense = jnp.sum(jnp.where(chosen, route_weight.T[None], 0.0), axis=1)
    for target in (z_pair, z_far, over_x, over_y, over_core):
        dense = jnp.stack([dense, move(dense, target)])
    own_expert = (req * lax.axis_size("exp") + exp) // 2
    weights = lax.dynamic_index_in_dim(dense, own_expert, 5, False)

    is_middle = (z == 1) | (z == 2)
    slot_0 = normed
    slot_1 = move(slot_0, z_pair)
    middle = move(slot_0, z_middle)
    slot_2 = jnp.where(is_middle, move(slot_1, z_middle), move(middle, z_outward))
    slot_3 = jnp.where(is_middle, middle, move(slot_2, z_outward))

    partials = []
    for low, near, far in ((0, slot_0, slot_1), (2, slot_2, slot_3)):
        own = jnp.concatenate([near, far], axis=0)
        by_x = move(own, over_x)
        by_y = move(own, over_y)
        diagonal_near = move(by_x[:tok_count], over_y)
        diagonal_far = move(by_y[tok_count:], over_x)
        rows = jnp.concatenate([own, by_x, by_y, diagonal_near, diagonal_far], axis=0)
        other_rows = move(rows, over_core)
        results = []
        for side, held in ((1, other_rows), (0, rows)):
            scale = weights[side, :, :, low // 2].reshape(-1, 1)
            results.append(weighted_piece(held, scale, gate_weight, up_weight, down_weight))
        partials.append(results)

    def total(*terms):
        result = terms[0].astype(f32)
        for term in terms[1:]:
            result = result + term.astype(f32)
        return result

    def to_wire(value):
        return value.astype(jnp.bfloat16)

    sums = {}
    n = tok_count
    for low, (theirs, mine) in ((2, partials[1]), (0, partials[0])):
        came = move(theirs, over_core)

        def both(first, last):
            return total(mine[first * n : last * n], came[first * n : last * n])

        from_y = move(to_wire(both(6, 7)), over_y)
        from_x = move(to_wire(both(7, 8)), over_x)
        to_x = jnp.concatenate([to_wire(both(2, 3) + total(from_y)), to_wire(both(3, 4))], axis=0)
        to_y = jnp.concatenate([to_wire(both(4, 5)), to_wire(both(5, 6) + total(from_x))], axis=0)
        back_x, back_y = move(to_x, over_x), move(to_y, over_y)
        own = both(0, 2) + total(back_x) + total(back_y)
        sums[low], sums[low + 1] = own[:n], own[n:]

    sum_2 = sums[2] + total(move(to_wire(sums[3]), z_inward))
    sum_3 = sums[3] + total(move(to_wire(sums[2]), z_inward))
    sum_1 = sums[1] + total(move(to_wire(sum_2), z_middle))
    return sums[0] + total(move(to_wire(sum_3), z_middle)) + total(move(to_wire(sum_1), z_pair))


def local(
    hidden_in,
    qkv,
    q_gain,
    k_gain,
    query_pages,
    page_table,
    doc_lengths,
    doc_query,
    out_weight,
    moe_gain,
    routes,
    route_weight,
    gate_weight,
    up_weight,
    down_weight,
    score_weight,
):
    tok_count = hidden_in.shape[0]
    exp_index = lax.axis_index("exp")
    attn = attention(qkv, q_gain, k_gain, query_pages, page_table, doc_lengths, doc_query)
    attn = attn.transpose(1, 0, 2).reshape(hidden_in.shape)
    mixed = jnp.dot(attn, out_weight, preferred_element_type=jnp.float32)
    resid = (hidden_in.astype(jnp.float32) + mixed).astype(jnp.bfloat16)
    normed = rms_scale(resid.astype(jnp.float32), moe_gain).astype(jnp.bfloat16)
    is_small = (lax.axis_size("req"), lax.axis_size("exp")) == (2 * GRID[1], GRID[0] * GRID[2])
    moe = experts_dense if is_small else experts_by_slots
    combined = moe(normed, routes, route_weight, gate_weight, up_weight, down_weight)
    layer_out = (resid.astype(jnp.float32) + combined).astype(jnp.bfloat16)
    token_score = jnp.dot(
        layer_out.astype(jnp.float32), score_weight, precision=lax.Precision.HIGHEST
    )
    doc_len = doc_lengths[0]
    doc_ends = jnp.cumsum(doc_len, dtype=jnp.int32)
    own_pos = exp_index * tok_count + jnp.arange(tok_count, dtype=jnp.int32)
    member = (own_pos[:, None] < doc_ends[None, :]) & (
        own_pos[:, None] >= (doc_ends - doc_len)[None, :]
    )
    doc_partial = jnp.dot(
        token_score, member.astype(jnp.float32), precision=lax.Precision.HIGHEST
    )
    doc_sums = lax.psum(doc_partial, "exp")
    doc_scores = (doc_sums / doc_len.astype(jnp.float32))[None, :]
    return (layer_out, doc_scores)


def solution(mesh):
    in_specs = (
        P(("req", "exp"), None),
        P(("req", "exp"), None),
        P(),
        P(),
        P("req", None, None, "exp"),
        P("req", None),
        P("req", None),
        P("req", None),
        P(),
        P(),
        P(("req", "exp"), None),
        P(("req", "exp"), None),
        P(("req", "exp"), None, None),
        P(("req", "exp"), None, None),
        P(("req", "exp"), None, None),
        P(),
    )
    out_specs = (P(("req", "exp"), None), P("req", None))
    return jax.shard_map(local, mesh=mesh, in_specs=in_specs, out_specs=out_specs, check_vma=False)
```

time: 920 us -> 406 us (0.44)
  blocking collectives: 300 us -> 38.5 us
  waiting for transfers between devices: 391 us -> 209 us
  local copies, waits for them, and re-layouts: 107 us -> 21.4 us
  Pallas kernels: 0 us -> 54.2 us
  matrix products: 51.6 us -> 5.53 us
  starting transfers between devices: 11.5 us -> 54.8 us
  other arithmetic: 43.5 us -> 20.5 us
  between operations: 14.5 us -> 1.28 us
    all_to_all x1, blocking collectives: 277 us -> 18.1 us  [attention(): back = lax.all_to_all(out, 'exp', split_axis=0, concat_axis=0, tiled=True)]
    all_to_all x1, waiting for transfers between devices: 279 us -> 36.9 us  [attention(): lax.all_to_all(parts, 'exp', split_axis=0, concat_axis=0, tiled=True)]
    ppermute x2 -> x35, waiting for transfers between devices: 35.4 us -> 172 us  [move(): return lax.ppermute(block, ALL, pairs(target))]
    all_gather x1 -> x0, waiting for transfers between devices: 75.8 us -> none  [local(): lax.all_gather(query_pages[0], 'exp', axis=2, tiled=True)]
    pallas_call x0 -> x6, Pallas kernels: none -> 54.2 us  [the longest x4 37.3 us: weighted_piece(): pl.pallas_call(expert_kernel, grid=(count // tile,), out_shape=jax.ShapeD...]
    dot_general x6 -> x1, matrix products: 48.7 us -> 0.21 us  [local(): jnp.dot(token_score, member.astype(jnp.float32), precision=lax.Precision....]
    ppermute x2 -> x35, starting transfers between devices: 7.22 us -> 47.5 us  [move(): return lax.ppermute(block, ALL, pairs(target))]
    slice x6, local copies, waits for them, and re-layouts: 22.6 us -> 0.32 us  [the longest x1 0.14 us: experts_dense(): sums[low], sums[low + 1] = (own[:n], own[n:])]
  transfers between devices with their start and end apart: 4 -> 36, of which waited for: 3 -> 21; matrix products, arithmetic and copies ran while one was open for 4% -> 6% of each run, Pallas kernels for 0% -> 9%
where the time goes in v1:
time: 406 us; the launch traced here: 405 us
  waiting for transfers between devices  209 us (51%)
  starting transfers between devices  54.8 us (13%)
  Pallas kernels  54.2 us (13%)
  blocking collectives  38.5 us (9%)
  local copies, waits for them, and re-layouts  21.4 us (5%)
  other arithmetic  20.5 us (5%)
  matrix products  5.53 us (1%)
    ppermute x35, waiting for transfers between devices, move(): return lax.ppermute(block, ALL, pairs(target))  172 us
    ppermute x35, starting transfers between devices, move(): return lax.ppermute(block, ALL, pairs(target))  47.5 us
    pallas_call x4, Pallas kernels, weighted_piece(): pl.pallas_call(expert_kernel, grid=(count // tile,), out_shape=jax.ShapeD...  37.3 us
    all_to_all x1, waiting for transfers between devices, attention(): lax.all_to_all(parts, 'exp', split_axis=0, concat_axis=0, tiled=True)  36.9 us
    psum x1, blocking collectives, local(): doc_sums = lax.psum(doc_partial, 'exp')  20.4 us
    all_to_all x1, blocking collectives, attention(): back = lax.all_to_all(out, 'exp', split_axis=0, concat_axis=0, tiled=True)  18.1 us
    unnamed x49, local copies, waits for them, and re-layouts  18 us
    pallas_call x1, Pallas kernels, attention(): pl.pallas_call(attention_kernel, out_shape=jax.ShapeDtypeStruct((tokens,...  11.5 us
  transfers between devices with their start and end apart: 36, of which 21 were waited for; matrix products, arithmetic and copies ran while one was open for 6% of the time, Pallas kernels for 9%

profile of v1, /device:TPU:0, one launch (start us, length us, event | category | flops | bytes accessed | tf_op | source)
XLA Modules:
  0.0 404.9 jit_solution(11044515492271990095)
XLA Ops:
  0.7 5.5 %pack_heads.1 = bf16[1024,768]{1,0:T(8,128)(2,1)} custom-call(bf16[128,6144]{1,0:T(8,128)(2,1)} %v_ref.1, bf16[128,6144]{1,0:T(8,128)(2,1)} %v_ref.1, bf16[128,6144]{1,0:T(8,128)(2,1)} %v_ref.1), custom_call_target="tpu_custom_call" | custom-call | tf_op jit(solution)/shard_map/pack_heads/pallas_call | solution.py:151
  6.2 7.3 %all-to-all-start = ((bf16[8,128,768]{2,1,0:T(8,128)(2,1)}), bf16[8,128,768]{2,1,0:T(8,128)(2,1)S(1)}, u32[]{:S(2)}, u32[]{:S(2)}) async-start(bf16[8,128,768]{2,1,0:T(8,128)(2,1)} %bitcast.61), calls=%async_computation | async-start | bytes 3145728 | tf_op jit(solution)/shard_map/all_to_all | solution.py:162
  13.6 36.9 %all-to-all-done = bf16[8,128,768]{2,1,0:T(8,128)(2,1)S(1)} async-done(((bf16[8,128,768]{2,1,0:T(8,128)(2,1)}), bf16[8,128,768]{2,1,0:T(8,128)(2,1)S(1)}, u32[]{:S(2)}, u32[]{:S(2)}) %all-to-all-start) | async-done | bytes 1572896 | tf_op jit(solution)/shard_map/all_to_all | solution.py:162
  50.5 11.5 %paged_attention.1 = bf16[1024,256]{1,0:T(8,128)(2,1)S(1)} custom-call(bf16[1024,768]{1,0:T(8,128)(2,1)S(1)} %bitcast.56, bf16[1024,512]{1,0:T(8,128)(2,1)S(1)} %bitcast.58, s32[1,128]{1,0:T(1,128)S(1)} %pad.7.len_ref, s32[1,128]{1,0:T(1,128)S(1)} %pad.8.query_ref, s32[8,1]{1,0:T(8,128)S(1)} %copy.45.table_ref, f32[1,128]{1,0:T(1,128)S(1)} %bitcast.59, ...), custom_call_target="tpu_custom_call" | custom-call | tf_op jit(solution)/shard_map/paged_attention/pallas_call | solution.py:165
  62.3 18.1 %all_to_all.20 = bf16[8,128,256]{1,2,0:T(8,128)(2,1)S(1)} all-to-all(bf16[8,128,256]{1,2,0:T(8,128)(2,1)S(1)} %copy.46), channel_id=1, replica_groups=mesh['req'=4,'exp'=8] {'exp'}, dimensions={0} | all-to-all | bytes 1048576 | tf_op jit(solution)/shard_map/all_to_all | solution.py:184
  80.4 4.8 %multiply_reduce_fusion = (f32[128]{0:T(128)S(1)}, f32[128,2048]{1,0:T(8,128)S(1)}) fusion(bf16[128,2048]{0,1:T(8,128)(2,1)S(1)} %bitcast.62, bf16[2048,2048]{1,0:T(8,128)(2,1)} %param.25, bf16[128,2048]{1,0:T(8,128)(2,1)} %param.17), kind=kOutput, calls=%fused_computation.34 | convolution fusion | flops 1075314560 | bytes 10486272 | tf_op jit(solution)/shard_map/dot_general | solution.py:414
  88.9 10.8 %collective-permute-done = bf16[128,2048]{1,0:T(8,128)(2,1)S(1)} collective-permute-done((bf16[128,2048]{1,0:T(8,128)(2,1)S(1)}, bf16[128,2048]{1,0:T(8,128)(2,1)S(1)}, u32[]{:S(2)}, u32[]{:S(2)}) %collective-permute-start) | collective-permute-done | bytes 524320 | tf_op jit(solution)/shard_map/ppermute | solution.py:290
  101.7 13.1 %collective-permute-done.18 = bf16[128,2048]{1,0:T(8,128)(2,1)S(1)} collective-permute-done((bf16[128,2048]{1,0:T(8,128)(2,1)S(1)}, bf16[128,2048]{1,0:T(8,128)(2,1)S(1)}, u32[]{:S(2)}, u32[]{:S(2)}) %collective-permute-start.18) | collective-permute-done | bytes 524320 | tf_op jit(solution)/shard_map/ppermute | solution.py:290
  117.3 11.1 %collective-permute-done.19 = bf16[128,2048]{1,0:T(8,128)(2,1)S(1)} collective-permute-done((bf16[128,2048]{1,0:T(8,128)(2,1)S(1)}, bf16[128,2048]{1,0:T(8,128)(2,1)S(1)}, u32[]{:S(2)}, u32[]{:S(2)}) %collective-permute-start.19) | collective-permute-done | bytes 524320 | tf_op jit(solution)/shard_map/ppermute | solution.py:290
  129.4 2.4 collective-permute-start.20
  133.3 18.3 %collective-permute-done.20 = bf16[256,2048]{1,0:T(8,128)(2,1)S(1)} collective-permute-done((bf16[256,2048]{1,0:T(8,128)(2,1)S(1)}, bf16[256,2048]{1,0:T(8,128)(2,1)S(1)}, u32[]{:S(2)}, u32[]{:S(2)}) %collective-permute-start.20) | collective-permute-done | bytes 1048608 | tf_op jit(solution)/shard_map/ppermute | solution.py:290
  151.6 2.6 collective-permute-start.22
  154.3 2.1 collective-permute-start.1
  158.7 8.4 %collective-permute-done.22 = bf16[128,2048]{1,0:T(8,128)(2,1)S(1)} collective-permute-done((bf16[128,2048]{1,0:T(8,128)(2,1)S(1)}, bf16[128,2048]{1,0:T(8,128)(2,1)S(1)}, u32[]{:S(2)}, u32[]{:S(2)}) %collective-permute-start.22) | collective-permute-done | bytes 524320 | tf_op jit(solution)/shard_map/ppermute | solution.py:290
  168.0 17.3 %collective-permute-done.23 = bf16[128,2048]{1,0:T(8,128)(2,1)S(1)} collective-permute-done((bf16[128,2048]{1,0:T(8,128)(2,1)S(1)}, bf16[128,2048]{1,0:T(8,128)(2,1)S(1)}, u32[]{:S(2)}, u32[]{:S(2)}) %collective-permute-start.23) | collective-permute-done | bytes 524320 | tf_op jit(solution)/shard_map/ppermute | solution.py:290
  186.2 1.6 collective-permute-start.3
  188.7 1.8 collective-permute-start.4
  192.6 8.0 %collective-permute-done.3 = bf16[128,2048]{1,0:T(8,128)(2,1)S(1)} collective-permute-done((bf16[128,2048]{1,0:T(8,128)(2,1)S(1)}, bf16[128,2048]{1,0:T(8,128)(2,1)S(1)}, u32[]{:S(2)}, u32[]{:S(2)}) %collective-permute-start.3) | collective-permute-done | bytes 524320 | tf_op jit(solution)/shard_map/ppermute | solution.py:290
  203.8 3.6 collective-permute-done.5
  208.7 3.3 collective-permute-done.6
  212.1 1.7 collective-permute-start.7
  213.8 2.2 collective-permute-done.7
  216.6 3.8 collective-permute-done.8
  223.7 1.6 copy-done.9
  225.2 9.8 %expert_half.7 = bf16[1024,2048]{1,0:T(8,128)(2,1)} custom-call(bf16[1024,2048]{1,0:T(8,128)(2,1)} %collective-permute-done.24.rows_ref, f32[1024,1]{1,0:T(8,128)S(1)} %copy.50.scale_ref, bf16[1,2048,512]{2,1,0:T(8,128)(2,1)S(1)} %copy-done.5, bf16[1,2048,512]{2,1,0:T(8,128)(2,1)S(1)} %copy-done.6, bf16[1,512,2048]{2,1,0:T(8,128)(2,1)S(1)} %copy-done.9), custom_call_target="tpu_custom_call" | custom-call | flops 6442450944 | bytes 14680064 | tf_op jit(solution)/shard_map/expert_half/pallas_call | solution.py:203
  235.5 1.6 copy-done.7
  237.0 1.6 copy-done.10
  238.6 9.7 %expert_half.5 = bf16[1024,2048]{1,0:T(8,128)(2,1)} custom-call(bf16[1024,2048]{1,0:T(8,128)(2,1)} %collective-permute-done.10.rows_ref, f32[1024,1]{1,0:T(8,128)S(1)} %copy.48.scale_ref, bf16[1,2048,512]{2,1,0:T(8,128)(2,1)S(1)} %copy-done.5, bf16[1,2048,512]{2,1,0:T(8,128)(2,1)S(1)} %copy-done.7, bf16[1,512,2048]{2,1,0:T(8,128)(2,1)S(1)} %copy-done.10), custom_call_target="tpu_custom_call" | custom-call | flops 6442450944 | bytes 14680064 | tf_op jit(solution)/shard_map/expert_half/pallas_call | solution.py:203
  249.2 1.6 copy-done.8
  250.8 1.6 copy-done.11
  252.4 8.8 %expert_half.6 = bf16[1024,2048]{1,0:T(8,128)(2,1)S(1)} custom-call(bf16[1024,2048]{1,0:T(8,128)(2,1)} %constant_dynamic-update-slice_fusion.6.rows_ref, f32[1024,1]{1,0:T(8,128)S(1)} %copy.49.scale_ref, bf16[1,2048,512]{2,1,0:T(8,128)(2,1)S(1)} %copy-done.5, bf16[1,2048,512]{2,1,0:T(8,128)(2,1)S(1)} %copy-done.8, bf16[1,512,2048]{2,1,0:T(8,128)(2,1)S(1)} %copy-done.11), custom_call_target="tpu_custom_call" | custom-call | flops 6442450944 | bytes 14680064 | tf_op jit(solution)/shard_map/expert_half/pallas_call | solution.py:203
  263.0 8.9 %expert_half.4 = bf16[1024,2048]{1,0:T(8,128)(2,1)S(1)} custom-call(bf16[1024,2048]{1,0:T(8,128)(2,1)} %constant_dynamic-update-slice_fusion.rows_ref, f32[1024,1]{1,0:T(8,128)S(1)} %copy.47.scale_ref, bf16[1,2048,512]{2,1,0:T(8,128)(2,1)S(1)} %copy-done.5, bf16[1,2048,512]{2,1,0:T(8,128)(2,1)S(1)} %copy-done.8, bf16[1,512,2048]{2,1,0:T(8,128)(2,1)S(1)} %copy-done.11), custom_call_target="tpu_custom_call" | custom-call | flops 6442450944 | bytes 14680064 | tf_op jit(solution)/shard_map/expert_half/pallas_call | solution.py:203
  271.9 4.6 %collective-permute-done.26 = bf16[128,2048]{1,0:T(8,128)(2,1)S(1)} collective-permute-done((bf16[128,2048]{1,0:T(8,128)(2,1)S(1)}, bf16[128,2048]{1,0:T(8,128)(2,1)S(1)}, u32[]{:S(2)}, u32[]{:S(2)}) %collective-permute-start.26) | collective-permute-done | bytes 524320 | tf_op jit(solution)/shard_map/ppermute | solution.py:290
  276.5 2.3 add_convert_fusion.6
  278.7 1.8 collective-permute-start.28
  282.7 10.9 %collective-permute-done.28 = bf16[128,2048]{1,0:T(8,128)(2,1)S(1)} collective-permute-done((bf16[128,2048]{1,0:T(8,128)(2,1)S(1)}, bf16[128,2048]{1,0:T(8,128)(2,1)S(1)}, u32[]{:S(2)}, u32[]{:S(2)}) %collective-permute-start.28) | collective-permute-done | bytes 524320 | tf_op jit(solution)/shard_map/ppermute | solution.py:290
  295.6 2.3 add_convert_fusion.12
  297.8 1.8 collective-permute-start.14
  300.1 27.3 %collective-permute-done.14 = bf16[128,2048]{1,0:T(8,128)(2,1)S(1)} collective-permute-done((bf16[128,2048]{1,0:T(8,128)(2,1)S(1)}, bf16[128,2048]{1,0:T(8,128)(2,1)S(1)}, u32[]{:S(2)}, u32[]{:S(2)}) %collective-permute-start.14) | collective-permute-done | bytes 524320 | tf_op jit(solution)/shard_map/ppermute | solution.py:290
  328.6 1.8 convert_add_fusion
  330.6 2.3 collective-permute-start.30
  334.8 10.4 %collective-permute-done.30 = bf16[128,2048]{1,0:T(8,128)(2,1)S(1)} collective-permute-done((bf16[128,2048]{1,0:T(8,128)(2,1)S(1)}, bf16[128,2048]{1,0:T(8,128)(2,1)S(1)}, u32[]{:S(2)}, u32[]{:S(2)}) %collective-permute-start.30) | collective-permute-done | bytes 524320 | tf_op jit(solution)/shard_map/ppermute | solution.py:290
  345.2 6.9 %collective-permute-done.32 = bf16[128,2048]{1,0:T(8,128)(2,1)S(1)} collective-permute-done((bf16[128,2048]{1,0:T(8,128)(2,1)S(1)}, bf16[128,2048]{1,0:T(8,128)(2,1)S(1)}, u32[]{:S(2)}, u32[]{:S(2)}) %collective-permute-start.32) | collective-permute-done | bytes 524320 | tf_op jit(solution)/shard_map/ppermute | solution.py:290
  354.1 1.8 collective-permute-done.15
  355.9 1.7 convert_add_fusion.1
  360.0 13.5 %collective-permute-start.34 = (bf16[128,2048]{1,0:T(8,128)(2,1)}, bf16[128,2048]{1,0:T(8,128)(2,1)}, u32[]{:S(2)}, u32[]{:S(2)}) collective-permute-start(bf16[128,2048]{1,0:T(8,128)(2,1)} %fusion.2), channel_id=1, source_target_pairs={{0,2},{1,3},{2,0},{3,1},{4,6},{5,7},{6,4},{7,5},{8,10},{9,11},{10,... | collective-permute-start | bytes 1572872 | tf_op jit(solution)/shard_map/ppermute | solution.py:290
  373.8 7.2 %collective-permute-done.34 = bf16[128,2048]{1,0:T(8,128)(2,1)} collective-permute-done((bf16[128,2048]{1,0:T(8,128)(2,1)}, bf16[128,2048]{1,0:T(8,128)(2,1)}, u32[]{:S(2)}, u32[]{:S(2)}) %collective-permute-start.34) | collective-permute-done | bytes 524320 | tf_op jit(solution)/shard_map/ppermute | solution.py:290
  384.1 20.4 %psum.7 = f32[32]{0:T(128)S(1)} all-reduce(f32[32]{0:T(128)S(1)} %convolution_bitcast_fusion), channel_id=1, replica_groups=mesh['req'=4,'exp'=8] {'exp'}, use_global_device_ids=true, to_apply=%region_3.4 | all-reduce | flops 32 | bytes 256 | tf_op jit(solution)/shard_map/psum | solution.py:433
  (133 shorter events, 45.4 us)
Async XLA Ops:
  0.6 381.9 %copy-start = (f32[2048]{0:T(1024)S(1)}, f32[2048]{0:T(1024)}, u32[]{:S(2)}) copy-start(f32[2048]{0:T(1024)} %param.32) | copy-start | bytes 24580
  0.6 49.8 %copy-start.2 = (bf16[128,768]{1,0:T(8,128)(2,1)S(1)}, bf16[128,768]{1,0:T(8,128)(2,1)}, u32[]{:S(2)}) copy-start(bf16[128,768]{1,0:T(8,128)(2,1)} %constant.54.clone.rope_ref) | copy-start | bytes 589828
  0.7 12.8 %copy-start.18 = (s32[1,8]{1,0:T(1,128)S(1)}, s32[1,8]{1,0:T(1,128)}, u32[]{:S(2)}) copy-start(s32[1,8]{1,0:T(1,128)} %param.22) | copy-start | bytes 100
  0.7 12.9 %copy-start.19 = (s32[1,32]{1,0:T(1,128)S(1)}, s32[1,32]{1,0:T(1,128)}, u32[]{:S(2)}) copy-start(s32[1,32]{1,0:T(1,128)} %param.23) | copy-start | bytes 388
  0.7 12.9 %copy-start.20 = (s32[1,32]{1,0:T(1,128)S(1)}, s32[1,32]{1,0:T(1,128)}, u32[]{:S(2)}) copy-start(s32[1,32]{1,0:T(1,128)} %param.24) | copy-start | bytes 388
  0.7 49.8 %copy-start.1 = (bf16[1,8,128,512]{3,2,1,0:T(8,128)(2,1)S(1)}, bf16[1,8,128,512]{3,2,1,0:T(8,128)(2,1)}, u32[]{:S(2)}) copy-start(bf16[1,8,128,512]{3,2,1,0:T(8,128)(2,1)} %param.21) | copy-start | bytes 3145732
  0.7 49.8 %copy-start.3 = (f32[128]{0:T(128)S(1)}, f32[128]{0:T(128)}, u32[]{:S(2)}) copy-start(f32[128]{0:T(128)} %param.19) | copy-start | bytes 1540
  0.7 49.8 %copy-start.4 = (f32[128]{0:T(128)S(1)}, f32[128]{0:T(128)}, u32[]{:S(2)}) copy-start(f32[128]{0:T(128)} %param.20) | copy-start | bytes 1540
  6.2 44.3 %all-to-all-start = ((bf16[8,128,768]{2,1,0:T(8,128)(2,1)}), bf16[8,128,768]{2,1,0:T(8,128)(2,1)S(1)}, u32[]{:S(2)}, u32[]{:S(2)}) async-start(bf16[8,128,768]{2,1,0:T(8,128)(2,1)} %bitcast.61), calls=%async_computation | async-start | bytes 3145728 | tf_op jit(solution)/shard_map/all_to_all | solution.py:162
  87.1 12.6 %collective-permute-start = (bf16[128,2048]{1,0:T(8,128)(2,1)S(1)}, bf16[128,2048]{1,0:T(8,128)(2,1)S(1)}, u32[]{:S(2)}, u32[]{:S(2)}) collective-permute-start(bf16[128,2048]{1,0:T(8,128)(2,1)S(1)} %get-tuple-element.7), channel_id=1, source_target_pairs={{0,2},{1,3},{2,0},{3,1},{4,6},{5,7},{6,4},{7,5},{8,10},{9,11},{10,... | collective-permute-start | bytes 1572872 | tf_op jit(solution)/shard_map/ppermute | solution.py:290
  88.2 12.2 %collective-permute-start.17 = (bf16[128,2048]{1,0:T(8,128)(2,1)S(1)}, bf16[128,2048]{1,0:T(8,128)(2,1)S(1)}, u32[]{:S(2)}, u32[]{:S(2)}) collective-permute-start(bf16[128,2048]{1,0:T(8,128)(2,1)S(1)} %get-tuple-element.7), channel_id=1, source_target_pairs={{2,4},{3,5},{4,2},{5,3},{10,12},{11,13},{12,10},{13,11},{18,20},{1... | collective-permute-start | bytes 1572872 | tf_op jit(solution)/shard_map/ppermute | solution.py:290
  99.7 2.0 collective-permute-start.16
  100.4 14.4 %collective-permute-start.18 = (bf16[128,2048]{1,0:T(8,128)(2,1)S(1)}, bf16[128,2048]{1,0:T(8,128)(2,1)S(1)}, u32[]{:S(2)}, u32[]{:S(2)}) collective-permute-start(bf16[128,2048]{1,0:T(8,128)(2,1)S(1)} %collective-permute-done.17), channel_id=1, source_target_pairs={{2,0},{3,1},{4,6},{5,7},{10,8},{11,9},{12,14},{13,15},{18,16},{19,... | collective-permute-start | bytes 1572872 | tf_op jit(solution)/shard_map/ppermute | solution.py:290
  115.8 12.6 %collective-permute-start.19 = (bf16[128,2048]{1,0:T(8,128)(2,1)S(1)}, bf16[128,2048]{1,0:T(8,128)(2,1)S(1)}, u32[]{:S(2)}, u32[]{:S(2)}) collective-permute-start(bf16[128,2048]{1,0:T(8,128)(2,1)S(1)} %get-tuple-element.5), channel_id=1, source_target_pairs={{2,0},{3,1},{4,6},{5,7},{10,8},{11,9},{12,14},{13,15},{18,16},{19,... | collective-permute-start | bytes 1572872 | tf_op jit(solution)/shard_map/ppermute | solution.py:290
  129.4 22.2 %collective-permute-start.20 = (bf16[256,2048]{1,0:T(8,128)(2,1)S(1)}, bf16[256,2048]{1,0:T(8,128)(2,1)S(1)}, u32[]{:S(2)}, u32[]{:S(2)}) collective-permute-start(bf16[256,2048]{1,0:T(8,128)(2,1)S(1)} %pad_maximum_fusion.3), channel_id=1, source_target_pairs={{0,1},{1,0},{2,3},{3,2},{4,5},{5,4},{6,7},{7,6},{8,9},{9,8},{10,11... | collective-permute-start | bytes 3145736 | tf_op jit(solution)/shard_map/ppermute | solution.py:290
  131.7 24.6 %collective-permute-start.21 = (bf16[256,2048]{1,0:T(8,128)(2,1)S(1)}, bf16[256,2048]{1,0:T(8,128)(2,1)S(1)}, u32[]{:S(2)}, u32[]{:S(2)}) collective-permute-start(bf16[256,2048]{1,0:T(8,128)(2,1)S(1)} %pad_maximum_fusion.3), channel_id=1, source_target_pairs={{0,16},{1,17},{2,18},{3,19},{4,20},{5,21},{6,22},{7,23},{8,24},{9,... | collective-permute-start | bytes 3145736 | tf_op jit(solution)/shard_map/ppermute | solution.py:290
  151.6 15.5 %collective-permute-start.22 = (bf16[128,2048]{1,0:T(8,128)(2,1)S(1)}, bf16[128,2048]{1,0:T(8,128)(2,1)S(1)}, u32[]{:S(2)}, u32[]{:S(2)}) collective-permute-start(bf16[128,2048]{1,0:T(8,128)(2,1)S(1)} %slice.179), channel_id=1, source_target_pairs={{0,16},{1,17},{2,18},{3,19},{4,20},{5,21},{6,22},{7,23},{8,24},{9,... | collective-permute-start | bytes 1572872 | tf_op jit(solution)/shard_map/ppermute | solution.py:290
  154.3 31.9 %collective-permute-start.1 = (bf16[256,2048]{1,0:T(8,128)(2,1)S(1)}, bf16[256,2048]{1,0:T(8,128)(2,1)S(1)}, u32[]{:S(2)}, u32[]{:S(2)}) collective-permute-start(bf16[256,2048]{1,0:T(8,128)(2,1)S(1)} %pad_maximum_fusion), channel_id=1, source_target_pairs={{0,1},{1,0},{2,3},{3,2},{4,5},{5,4},{6,7},{7,6},{8,9},{9,8},{10,11... | collective-permute-start | bytes 3145736 | tf_op jit(solution)/shard_map/ppermute | solution.py:290
  156.4 32.3 %collective-permute-start.2 = (bf16[256,2048]{1,0:T(8,128)(2,1)S(1)}, bf16[256,2048]{1,0:T(8,128)(2,1)S(1)}, u32[]{:S(2)}, u32[]{:S(2)}) collective-permute-start(bf16[256,2048]{1,0:T(8,128)(2,1)S(1)} %pad_maximum_fusion), channel_id=1, source_target_pairs={{0,16},{1,17},{2,18},{3,19},{4,20},{5,21},{6,22},{7,23},{8,24},{9,... | collective-permute-start | bytes 3145736 | tf_op jit(solution)/shard_map/ppermute | solution.py:290
  156.4 28.8 %collective-permute-start.23 = (bf16[128,2048]{1,0:T(8,128)(2,1)S(1)}, bf16[128,2048]{1,0:T(8,128)(2,1)S(1)}, u32[]{:S(2)}, u32[]{:S(2)}) collective-permute-start(bf16[128,2048]{1,0:T(8,128)(2,1)S(1)} %slice.180), channel_id=1, source_target_pairs={{0,1},{1,0},{2,3},{3,2},{4,5},{5,4},{6,7},{7,6},{8,9},{9,8},{10,11... | collective-permute-start | bytes 1572872 | tf_op jit(solution)/shard_map/ppermute | solution.py:290
  186.2 35.9 %collective-permute-start.24 = (bf16[1024,2048]{1,0:T(8,128)(2,1)}, bf16[1024,2048]{1,0:T(8,128)(2,1)}, u32[]{:S(2)}, u32[]{:S(2)}) collective-permute-start(bf16[1024,2048]{1,0:T(8,128)(2,1)} %constant_dynamic-update-slice_fusion.6.rows_ref), channel_id=1, source_target_pairs={{0,8},{1,9},{2,10},{3,11},{4,12},{5,13},{6,14},{7,15},{8,0},{9,1},... | collective-permute-start | bytes 12582920 | tf_op jit(solution)/shard_map/ppermute | solution.py:290
  186.2 14.4 %collective-permute-start.3 = (bf16[128,2048]{1,0:T(8,128)(2,1)S(1)}, bf16[128,2048]{1,0:T(8,128)(2,1)S(1)}, u32[]{:S(2)}, u32[]{:S(2)}) collective-permute-start(bf16[128,2048]{1,0:T(8,128)(2,1)S(1)} %slice.160), channel_id=1, source_target_pairs={{0,16},{1,17},{2,18},{3,19},{4,20},{5,21},{6,22},{7,23},{8,24},{9,... | collective-permute-start | bytes 1572872 | tf_op jit(solution)/shard_map/ppermute | solution.py:290
  187.8 15.9 %copy-start.16 = (f32[128,8]{0,1:T(8,128)S(1)}, f32[128,8]{0,1:T(8,128)}, u32[]{:S(2)}) copy-start(f32[128,8]{0,1:T(8,128)} %param.28) | copy-start | bytes 12292
  187.8 15.9 %copy-start.17 = (s32[128,8]{0,1:T(8,128)S(1)}, s32[128,8]{0,1:T(8,128)}, u32[]{:S(2)}) copy-start(s32[128,8]{0,1:T(8,128)} %param.27) | copy-start | bytes 12292
  188.7 33.4 %copy-start.5 = (bf16[1,2048,512]{2,1,0:T(8,128)(2,1)S(1)}, bf16[1,2048,512]{2,1,0:T(8,128)(2,1)}, u32[]{:S(2)}) copy-start(bf16[1,2048,512]{2,1,0:T(8,128)(2,1)} %gate_ref.7) | copy-start | bytes 6291460
  188.7 14.1 %collective-permute-start.4 = (bf16[128,2048]{1,0:T(8,128)(2,1)S(1)}, bf16[128,2048]{1,0:T(8,128)(2,1)S(1)}, u32[]{:S(2)}, u32[]{:S(2)}) collective-permute-start(bf16[128,2048]{1,0:T(8,128)(2,1)S(1)} %slice.161), channel_id=1, source_target_pairs={{0,1},{1,0},{2,3},{3,2},{4,5},{5,4},{6,7},{7,6},{8,9},{9,8},{10,11... | collective-permute-start | bytes 1572872 | tf_op jit(solution)/shard_map/ppermute | solution.py:290
  203.7 31.8 %collective-permute-start.10 = (bf16[1024,2048]{1,0:T(8,128)(2,1)}, bf16[1024,2048]{1,0:T(8,128)(2,1)}, u32[]{:S(2)}, u32[]{:S(2)}) collective-permute-start(bf16[1024,2048]{1,0:T(8,128)(2,1)} %constant_dynamic-update-slice_fusion.rows_ref), channel_id=1, source_target_pairs={{0,8},{1,9},{2,10},{3,11},{4,12},{5,13},{6,14},{7,15},{8,0},{9,1},... | collective-permute-start | bytes 12582920 | tf_op jit(solution)/shard_map/ppermute | solution.py:290
  203.7 3.7 collective-permute-start.5
  207.4 4.6 %collective-permute-start.6 = (f32[2,16,128]{2,1,0:T(8,128)S(1)}, f32[2,16,128]{2,1,0:T(8,128)S(1)}, u32[]{:S(2)}, u32[]{:S(2)}) collective-permute-start(f32[2,16,128]{2,1,0:T(8,128)S(1)} %get-tuple-element.31), channel_id=1, source_target_pairs={{0,4},{1,5},{2,6},{3,7},{4,0},{5,1},{6,2},{7,3},{8,12},{9,13},{10,... | collective-permute-start | bytes 49160 | tf_op jit(solution)/shard_map/ppermute | solution.py:290
  212.1 3.9 collective-permute-start.7
  216.0 4.3 %collective-permute-start.8 = (f32[2,2,2,16,128]{4,3,2,1,0:T(8,128)S(1)}, f32[2,2,2,16,128]{4,3,2,1,0:T(8,128)S(1)}, u32[]{:S(2)}, u32[]{:S(2)}) collective-permute-start(f32[2,2,2,16,128]{4,3,2,1,0:T(8,128)S(1)} %get-tuple-element.23), channel_id=1, source_target_pairs={{0,16},{1,17},{2,18},{3,19},{4,20},{5,21},{6,22},{7,23},{8,24},{9,... | collective-permute-start | bytes 196616 | tf_op jit(solution)/shard_map/ppermute | solution.py:290
  220.4 1.4 collective-permute-start.9
  235.1 26.2 %collective-permute-start.25 = (bf16[1024,2048]{1,0:T(8,128)(2,1)}, bf16[1024,2048]{1,0:T(8,128)(2,1)}, u32[]{:S(2)}, u32[]{:S(2)}) collective-permute-start(bf16[1024,2048]{1,0:T(8,128)(2,1)} %expert_half.7), channel_id=1, source_target_pairs={{0,8},{1,9},{2,10},{3,11},{4,12},{5,13},{6,14},{7,15},{8,0},{9,1},... | collective-permute-start | bytes 12582920 | tf_op jit(solution)/shard_map/ppermute | solution.py:290
  248.4 32.2 %collective-permute-start.11 = (bf16[1024,2048]{1,0:T(8,128)(2,1)}, bf16[1024,2048]{1,0:T(8,128)(2,1)}, u32[]{:S(2)}, u32[]{:S(2)}) collective-permute-start(bf16[1024,2048]{1,0:T(8,128)(2,1)} %expert_half.5), channel_id=1, source_target_pairs={{0,8},{1,9},{2,10},{3,11},{4,12},{5,13},{6,14},{7,15},{8,0},{9,1},... | collective-permute-start | bytes 12582920 | tf_op jit(solution)/shard_map/ppermute | solution.py:290
  262.4 14.0 %collective-permute-start.26 = (bf16[128,2048]{1,0:T(8,128)(2,1)S(1)}, bf16[128,2048]{1,0:T(8,128)(2,1)S(1)}, u32[]{:S(2)}, u32[]{:S(2)}) collective-permute-start(bf16[128,2048]{1,0:T(8,128)(2,1)S(1)} %add_convert_fusion.7), channel_id=1, source_target_pairs={{0,16},{1,17},{2,18},{3,19},{4,20},{5,21},{6,22},{7,23},{8,24},{9,... | collective-permute-start | bytes 1572872 | tf_op jit(solution)/shard_map/ppermute | solution.py:290
  278.7 14.9 %collective-permute-start.28 = (bf16[128,2048]{1,0:T(8,128)(2,1)S(1)}, bf16[128,2048]{1,0:T(8,128)(2,1)S(1)}, u32[]{:S(2)}, u32[]{:S(2)}) collective-permute-start(bf16[128,2048]{1,0:T(8,128)(2,1)S(1)} %get-tuple-element.9), channel_id=1, source_target_pairs={{0,1},{1,0},{2,3},{3,2},{4,5},{5,4},{6,7},{7,6},{8,9},{9,8},{10,11... | collective-permute-start | bytes 1572872 | tf_op jit(solution)/shard_map/ppermute | solution.py:290
  281.7 13.8 %collective-permute-start.12 = (bf16[128,2048]{1,0:T(8,128)(2,1)S(1)}, bf16[128,2048]{1,0:T(8,128)(2,1)S(1)}, u32[]{:S(2)}, u32[]{:S(2)}) collective-permute-start(bf16[128,2048]{1,0:T(8,128)(2,1)S(1)} %add_convert_fusion.13), channel_id=1, source_target_pairs={{0,16},{1,17},{2,18},{3,19},{4,20},{5,21},{6,22},{7,23},{8,24},{9,... | collective-permute-start | bytes 1572872 | tf_op jit(solution)/shard_map/ppermute | solution.py:290
  282.4 46.2 %collective-permute-start.27 = (bf16[256,2048]{1,0:T(8,128)(2,1)S(1)}, bf16[256,2048]{1,0:T(8,128)(2,1)S(1)}, u32[]{:S(2)}, u32[]{:S(2)}) collective-permute-start(bf16[256,2048]{1,0:T(8,128)(2,1)S(1)} %pad_maximum_fusion.4), channel_id=1, source_target_pairs={{0,1},{1,0},{2,3},{3,2},{4,5},{5,4},{6,7},{7,6},{8,9},{9,8},{10,11... | collective-permute-start | bytes 3145736 | tf_op jit(solution)/shard_map/ppermute | solution.py:290
  295.0 33.6 %collective-permute-start.29 = (bf16[256,2048]{1,0:T(8,128)(2,1)S(1)}, bf16[256,2048]{1,0:T(8,128)(2,1)S(1)}, u32[]{:S(2)}, u32[]{:S(2)}) collective-permute-start(bf16[256,2048]{1,0:T(8,128)(2,1)S(1)} %pad_maximum_fusion.5), channel_id=1, source_target_pairs={{0,16},{1,17},{2,18},{3,19},{4,20},{5,21},{6,22},{7,23},{8,24},{9,... | collective-permute-start | bytes 3145736 | tf_op jit(solution)/shard_map/ppermute | solution.py:290
  297.8 29.5 %collective-permute-start.14 = (bf16[128,2048]{1,0:T(8,128)(2,1)S(1)}, bf16[128,2048]{1,0:T(8,128)(2,1)S(1)}, u32[]{:S(2)}, u32[]{:S(2)}) collective-permute-start(bf16[128,2048]{1,0:T(8,128)(2,1)S(1)} %get-tuple-element.13), channel_id=1, source_target_pairs={{0,1},{1,0},{2,3},{3,2},{4,5},{5,4},{6,7},{7,6},{8,9},{9,8},{10,11... | collective-permute-start | bytes 1572872 | tf_op jit(solution)/shard_map/ppermute | solution.py:290
  299.7 54.3 %collective-permute-start.13 = (bf16[256,2048]{1,0:T(8,128)(2,1)S(1)}, bf16[256,2048]{1,0:T(8,128)(2,1)S(1)}, u32[]{:S(2)}, u32[]{:S(2)}) collective-permute-start(bf16[256,2048]{1,0:T(8,128)(2,1)S(1)} %pad_maximum_fusion.1), channel_id=1, source_target_pairs={{0,1},{1,0},{2,3},{3,2},{4,5},{5,4},{6,7},{7,6},{8,9},{9,8},{10,11... | collective-permute-start | bytes 3145736 | tf_op jit(solution)/shard_map/ppermute | solution.py:290
  330.6 14.7 %collective-permute-start.30 = (bf16[128,2048]{1,0:T(8,128)(2,1)S(1)}, bf16[128,2048]{1,0:T(8,128)(2,1)S(1)}, u32[]{:S(2)}, u32[]{:S(2)}) collective-permute-start(bf16[128,2048]{1,0:T(8,128)(2,1)S(1)} %get-tuple-element.18), channel_id=1, source_target_pairs={{0,2},{1,3},{6,4},{7,5},{8,10},{9,11},{14,12},{15,13},{16,18},{17,... | collective-permute-start | bytes 1572872 | tf_op jit(solution)/shard_map/ppermute | solution.py:290
  332.9 19.2 %collective-permute-start.32 = (bf16[128,2048]{1,0:T(8,128)(2,1)S(1)}, bf16[128,2048]{1,0:T(8,128)(2,1)S(1)}, u32[]{:S(2)}, u32[]{:S(2)}) collective-permute-start(bf16[128,2048]{1,0:T(8,128)(2,1)S(1)} %get-tuple-element.19), channel_id=1, source_target_pairs={{0,2},{1,3},{6,4},{7,5},{8,10},{9,11},{14,12},{15,13},{16,18},{17,... | collective-permute-start | bytes 1572872 | tf_op jit(solution)/shard_map/ppermute | solution.py:290
  334.3 21.5 %collective-permute-start.15 = (bf16[256,2048]{1,0:T(8,128)(2,1)S(1)}, bf16[256,2048]{1,0:T(8,128)(2,1)S(1)}, u32[]{:S(2)}, u32[]{:S(2)}) collective-permute-start(bf16[256,2048]{1,0:T(8,128)(2,1)S(1)} %pad_maximum_fusion.2), channel_id=1, source_target_pairs={{0,16},{1,17},{2,18},{3,19},{4,20},{5,21},{6,22},{7,23},{8,24},{9,... | collective-permute-start | bytes 3145736 | tf_op jit(solution)/shard_map/ppermute | solution.py:290
  353.2 27.8 %copy-start.13 = (f32[128,2048]{1,0:T(8,128)S(1)}, f32[128,2048]{1,0:T(8,128)}, u32[]{:S(2)}) copy-start(f32[128,2048]{1,0:T(8,128)} %copy-done.12) | copy-start | bytes 3145732
  353.2 5.9 %collective-permute-start.33 = (bf16[128,2048]{1,0:T(8,128)(2,1)S(1)}, bf16[128,2048]{1,0:T(8,128)(2,1)S(1)}, u32[]{:S(2)}, u32[]{:S(2)}) collective-permute-start(bf16[128,2048]{1,0:T(8,128)(2,1)S(1)} %get-tuple-element.17), channel_id=1, source_target_pairs={{2,4},{3,5},{4,2},{5,3},{10,12},{11,13},{12,10},{13,11},{18,20},{1... | collective-permute-start | bytes 1572872 | tf_op jit(solution)/shard_map/ppermute | solution.py:290
  357.6 16.2 %collective-permute-start.31 = (bf16[128,2048]{1,0:T(8,128)(2,1)}, bf16[128,2048]{1,0:T(8,128)(2,1)}, u32[]{:S(2)}, u32[]{:S(2)}) collective-permute-start(bf16[128,2048]{1,0:T(8,128)(2,1)} %get-tuple-element.16), channel_id=1, source_target_pairs={{2,4},{3,5},{4,2},{5,3},{10,12},{11,13},{12,10},{13,11},{18,20},{1... | collective-permute-start | bytes 1572872 | tf_op jit(solution)/shard_map/ppermute | solution.py:290
  360.0 21.0 %collective-permute-start.34 = (bf16[128,2048]{1,0:T(8,128)(2,1)}, bf16[128,2048]{1,0:T(8,128)(2,1)}, u32[]{:S(2)}, u32[]{:S(2)}) collective-permute-start(bf16[128,2048]{1,0:T(8,128)(2,1)} %fusion.2), channel_id=1, source_target_pairs={{0,2},{1,3},{2,0},{3,1},{4,6},{5,7},{6,4},{7,5},{8,10},{9,11},{10,... | collective-permute-start | bytes 1572872 | tf_op jit(solution)/shard_map/ppermute | solution.py:290
  (9 other events, 17.1 us)

commit v2 on v1

--- a/solution.py
+++ b/solution.py
@@ -135,12 +135,15 @@
             out_ref[rows, cols] = (weighted / total).astype(jnp.bfloat16)
 
 
-def column_block(exp_count, part, index):
-    return (0, part * exp_count + index)
-
-
-def pack_kernel(q_ref, k_ref, v_ref, out_ref):
-    out_ref[...] = jnp.concatenate([q_ref[...], k_ref[...], v_ref[...]], axis=1)
+def pack_kernel(exp_count, qkv_ref, out_ref):
+    rows = qkv_ref.shape[0]
+    own = qkv_ref.shape[1] // (3 * exp_count)
+    for index in range(exp_count):
+        for part in range(3):
+            at = (part * exp_count + index) * own
+            out_ref[index * rows : (index + 1) * rows, part * own : (part + 1) * own] = qkv_ref[
+                :, at : at + own
+            ]
 
 
 def attention(qkv, q_gain, k_gain, pages, page_table, doc_len, doc_query):
@@ -149,16 +152,10 @@
     own = width // exp_count
     tokens = exp_count * tok_count
     parts = pl.pallas_call(
-        pack_kernel,
-        grid=(exp_count,),
+        functools.partial(pack_kernel, exp_count),
         out_shape=jax.ShapeDtypeStruct((tokens, 3 * own), jnp.bfloat16),
-        in_specs=[
-            pl.BlockSpec((tok_count, own), functools.partial(column_block, exp_count, part))
-            for part in range(3)
-        ],
-        out_specs=pl.BlockSpec((tok_count, 3 * own), lambda i: (i, 0)),
         name="pack_heads",
-    )(qkv, qkv, qkv)
+    )(qkv)
     group = lax.all_to_all(parts, "exp", split_axis=0, concat_axis=0, tiled=True)
     docs = doc_len.shape[1]
     spare = ((0, 0), (0, LANES - docs))
@@ -185,41 +182,79 @@
     return back.reshape(exp_count, tok_count, own)
 
 
-def expert_kernel(rows_ref, scale_ref, gate_ref, up_ref, down_ref, out_ref):
-    rows = rows_ref[...]
-    gate_act = jnp.dot(rows, gate_ref[0], preferred_element_type=jnp.float32)
-    up_act = jnp.dot(rows, up_ref[0], preferred_element_type=jnp.float32)
-    hidden_act = jax.nn.silu(gate_act) * (up_act * scale_ref[...])
-    out_ref[...] = jnp.dot(
-        hidden_act.astype(jnp.bfloat16), down_ref[0], preferred_element_type=jnp.float32
-    ).astype(jnp.bfloat16)
-
-
-def weighted_piece(rows, scale, gate_weight, up_weight, down_weight):
+def expert_kernel(
+    steps, other_ref, rows_ref, scale_ref, gate_ref, up_ref, down_ref, relevance_ref,
+    theirs_ref, mine_ref, their_score_ref, my_score_ref,
+):
+    def work(held_ref, out_ref, score_ref):
+        held = held_ref[...]
+        gate_act = jnp.dot(held, gate_ref[0], preferred_element_type=jnp.float32)
+        up_act = jnp.dot(held, up_ref[0], preferred_element_type=jnp.float32)
+        hidden_act = jax.nn.silu(gate_act) * (up_act * scale_ref[...])
+        out_ref[...] = jnp.dot(
+            hidden_act.astype(jnp.bfloat16), down_ref[0], preferred_element_type=jnp.float32
+        ).astype(jnp.bfloat16)
+        score_ref[...] = jnp.sum(hidden_act * relevance_ref[...], axis=1, keepdims=True)
+
+    step = pl.program_id(0)
+
+    @pl.when(step < steps)
+    def _():
+        work(other_ref, theirs_ref, their_score_ref)
+
+    @pl.when(step >= steps)
+    def _():
+        work(rows_ref, mine_ref, my_score_ref)
+
+
+def weighted_pieces(other, rows, scale, at, gate_weight, up_weight, down_weight, relevance):
     count, width = rows.shape
     hidden = gate_weight.shape[2]
-    tile = 256
+    tile = 256 if count % 256 == 0 else 128
+    steps = count // tile
     once = pl.Buffered(1)
+
+    def early(i):
+        return (jnp.minimum(i, steps - 1), 0)
+
+    def late(i):
+        return (jnp.maximum(i - steps, 0), 0)
+
+    def place(i):
+        return (jnp.where(i < steps, at[0] // tile + i, at[1] // tile + i - steps), 0)
+
     return pl.pallas_call(
-        expert_kernel,
-        grid=(count // tile,),
-        out_shape=jax.ShapeDtypeStruct(rows.shape, jnp.bfloat16),
+        functools.partial(expert_kernel, steps),
+        grid=(2 * steps,),
+        out_shape=(
+            jax.ShapeDtypeStruct(rows.shape, jnp.bfloat16),
+            jax.ShapeDtypeStruct(rows.shape, jnp.bfloat16),
+            jax.ShapeDtypeStruct((count, 1), jnp.float32),
+            jax.ShapeDtypeStruct((count, 1), jnp.float32),
+        ),
         in_specs=[
-            pl.BlockSpec((tile, width), lambda i: (i, 0)),
-            pl.BlockSpec((tile, 1), lambda i: (i, 0)),
+            pl.BlockSpec((tile, width), early),
+            pl.BlockSpec((tile, width), late),
+            pl.BlockSpec((tile, 1), place),
             pl.BlockSpec((1, width, hidden), lambda i: (0, 0, 0), pipeline_mode=once),
             pl.BlockSpec((1, width, hidden), lambda i: (0, 0, 0), pipeline_mode=once),
             pl.BlockSpec((1, hidden, width), lambda i: (0, 0, 0), pipeline_mode=once),
+            pl.BlockSpec((1, hidden), lambda i: (0, 0)),
         ],
-        out_specs=pl.BlockSpec((tile, width), lambda i: (i, 0)),
+        out_specs=(
+            pl.BlockSpec((tile, width), early),
+            pl.BlockSpec((tile, width), late),
+            pl.BlockSpec((tile, 1), early),
+            pl.BlockSpec((tile, 1), late),
+        ),
         compiler_params=pltpu.CompilerParams(vmem_limit_bytes=24 * 1024 * 1024),
         cost_estimate=pl.CostEstimate(
-            flops=6 * count * width * hidden,
-            bytes_accessed=4 * count * width + 6 * width * hidden,
-            transcendentals=count * hidden,
+            flops=12 * count * width * hidden,
+            bytes_accessed=8 * count * width + 6 * width * hidden,
+            transcendentals=2 * count * hidden,
         ),
         name="expert_half",
-    )(rows, scale, gate_weight, up_weight, down_weight)
+    )(other, rows, scale, gate_weight, up_weight, down_weight, relevance)
 
 
 def expert_piece(rows, gate_weight, up_weight, down_weight):
@@ -322,41 +357,92 @@
     return (x, y, {0: 1, 3: 2}[z], core) if z in (0, 3) else None
 
 
-def experts_dense(normed, routes, route_weight, gate_weight, up_weight, down_weight):
-    f32 = jnp.float32
-    tok_count = normed.shape[0]
-    req, exp = lax.axis_index("req"), lax.axis_index("exp")
-    z = exp // GRID[0]
-    devices = lax.axis_size("req") * lax.axis_size("exp")
-    experts = devices // 2
+def together(*values):
+    return lax.optimization_barrier(values)
+
+
+def route_table(routes, route_weight):
+    exp_count = lax.axis_size("exp")
+    experts = lax.axis_size("req") * exp_count // 2
     chosen = routes.T[None] == jnp.arange(experts, dtype=jnp.int32)[:, None, None]
     dense = jnp.sum(jnp.where(chosen, route_weight.T[None], 0.0), axis=1)
     for target in (z_pair, z_far, over_x, over_y, over_core):
         dense = jnp.stack([dense, move(dense, target)])
-    own_expert = (req * lax.axis_size("exp") + exp) // 2
-    weights = lax.dynamic_index_in_dim(dense, own_expert, 5, False)
-
-    is_middle = (z == 1) | (z == 2)
-    slot_0 = normed
-    slot_1 = move(slot_0, z_pair)
-    middle = move(slot_0, z_middle)
-    slot_2 = jnp.where(is_middle, move(slot_1, z_middle), move(middle, z_outward))
-    slot_3 = jnp.where(is_middle, middle, move(slot_2, z_outward))
-
-    partials = []
-    for low, near, far in ((0, slot_0, slot_1), (2, slot_2, slot_3)):
-        own = jnp.concatenate([near, far], axis=0)
-        by_x = move(own, over_x)
-        by_y = move(own, over_y)
-        diagonal_near = move(by_x[:tok_count], over_y)
-        diagonal_far = move(by_y[tok_count:], over_x)
-        rows = jnp.concatenate([own, by_x, by_y, diagonal_near, diagonal_far], axis=0)
-        other_rows = move(rows, over_core)
-        results = []
-        for side, held in ((1, other_rows), (0, rows)):
-            scale = weights[side, :, :, low // 2].reshape(-1, 1)
-            results.append(weighted_piece(held, scale, gate_weight, up_weight, down_weight))
-        partials.append(results)
+    own_expert = (lax.axis_index("req") * exp_count + lax.axis_index("exp")) // 2
+    return lax.dynamic_index_in_dim(dense, own_expert, 5, False)
+
+
+def member_table(doc_len, tok_count):
+    ends = jnp.cumsum(doc_len, dtype=jnp.int32)
+    bounds = jnp.stack([ends - doc_len, ends])
+    for target in (over_y, over_core):
+        bounds = jnp.stack([bounds, move(bounds, target)])
+    exp = lax.axis_index("exp")
+    flips = np.array([[[k1 * 4 + k0 * 2 + dx for k0 in (0, 1)] for k1 in (0, 1)] for dx in (0, 1)])
+    blocks = jnp.bitwise_xor(exp, jnp.asarray(flips, jnp.int32))
+    position = blocks[..., None] * tok_count + jnp.arange(tok_count, dtype=jnp.int32)
+    position = position[None, None, ..., None]
+
+    def spread(side):
+        return bounds[:, :, side][:, :, None, None, None, None, :]
+
+    return ((position >= spread(0)) & (position < spread(1))).astype(jnp.float32)
+
+
+def experts_dense(resid, normed, weights, member, gate_weight, up_weight, down_weight, score_weight):
+    f32 = jnp.float32
+    n = normed.shape[0]
+    h = n // 2
+    z = lax.axis_index("exp") // GRID[0]
+    middle = (z == 1) | (z == 2)
+    relevance = jnp.dot(
+        down_weight[0].astype(f32), score_weight, precision=lax.Precision.HIGHEST
+    )[None]
+    scale = weights.transpose(3, 4, 0, 1, 2, 5).reshape(-1, 1)
+    normed, scale, member, relevance = together(normed, scale, member, relevance)
+
+    def join(*blocks):
+        return jnp.concatenate(blocks, axis=0)
+
+    def work(slot, first, other, rows):
+        at = [(slot * 2 + side) * 4 * n + first for side in (1, 0)]
+        return weighted_pieces(
+            other, rows, scale, at, gate_weight, up_weight, down_weight, relevance
+        )
+
+    p, m = move(normed, z_pair), move(normed, z_middle)
+    x0, y0 = move(normed, over_x), move(normed, over_y)
+    p, m, x0, y0 = together(p, m, x0, y0)
+
+    by_x, by_y = move(join(p, y0[h:]), over_x), move(join(p, x0[:h]), over_y)
+    q_middle, q_end = move(p, z_middle), move(m, z_outward)
+    by_x, by_y, q_middle, q_end = together(by_x, by_y, q_middle, q_end)
+    q = jnp.where(middle, q_middle, q_end)
+    xp, yp = by_x[:n], by_y[:n]
+    rows_0 = join(normed, x0, y0, by_y[n:], by_x[n:])
+
+    by_x, by_y = move(join(q, yp[h:]), over_x), move(join(q, xp[:h]), over_y)
+    r_end = move(q, z_outward)
+    out_0 = work(0, 0, move(rows_0, over_core), rows_0)
+    by_x, by_y, r_end, out_0 = together(by_x, by_y, r_end, out_0)
+    r = jnp.where(middle, m, r_end)
+    xq, yq = by_x[:n], by_y[:n]
+    rows_p = join(p, xp, yp, by_y[n:], by_x[n:])
+
+    by_x, by_y = move(join(r, yq[h:]), over_x), move(join(r, xq[:h]), over_y)
+    out_p = work(1, 0, move(rows_p, over_core), rows_p)
+    by_x, by_y, out_p = together(by_x, by_y, out_p)
+    xr, yr = by_x[:n], by_y[:n]
+    rows_q = join(q, xq, yq, by_y[n:], by_x[n:])
+
+    by_x, by_y = move(yr[h:], over_x), move(xr[:h], over_y)
+    rows_r = join(r, xr, yr)
+    other_q, other_r = move(rows_q, over_core), move(rows_r, over_core)
+    by_x, by_y, other_r = together(by_x, by_y, other_r)
+    rows_d = join(by_y, by_x)
+    out_d = work(3, 3 * n, move(rows_d, over_core), rows_d)
+    out_q = work(2, 0, other_q, rows_q)
+    out_r = work(3, 0, other_r, rows_r)
 
     def total(*terms):
         result = terms[0].astype(f32)
@@ -367,26 +453,80 @@
     def to_wire(value):
         return value.astype(jnp.bfloat16)
 
-    sums = {}
-    n = tok_count
-    for low, (theirs, mine) in ((2, partials[1]), (0, partials[0])):
-        came = move(theirs, over_core)
-
-        def both(first, last):
-            return total(mine[first * n : last * n], came[first * n : last * n])
-
-        from_y = move(to_wire(both(6, 7)), over_y)
-        from_x = move(to_wire(both(7, 8)), over_x)
-        to_x = jnp.concatenate([to_wire(both(2, 3) + total(from_y)), to_wire(both(3, 4))], axis=0)
-        to_y = jnp.concatenate([to_wire(both(4, 5)), to_wire(both(5, 6) + total(from_x))], axis=0)
-        back_x, back_y = move(to_x, over_x), move(to_y, over_y)
-        own = both(0, 2) + total(back_x) + total(back_y)
-        sums[low], sums[low + 1] = own[:n], own[n:]
-
-    sum_2 = sums[2] + total(move(to_wire(sums[3]), z_inward))
-    sum_3 = sums[3] + total(move(to_wire(sums[2]), z_inward))
-    sum_1 = sums[1] + total(move(to_wire(sum_2), z_middle))
-    return sums[0] + total(move(to_wire(sum_3), z_middle)) + total(move(to_wire(sum_1), z_pair))
+    class Plane:
+        def __init__(self, mine, came):
+            self.mine, self.came = mine, came
+
+        def part(self, first, last):
+            return total(self.mine[first:last], self.came[first:last])
+
+        def diagonal(self, at=3):
+            ends = to_wire(self.part(at * n, (at + 1) * n))
+            return ends[:h], ends[h:]
+
+        def sides(self, from_y, from_x):
+            of_x = join(self.part(n, n + h) + total(from_y), self.part(n + h, 2 * n))
+            of_y = join(self.part(2 * n, 2 * n + h), self.part(2 * n + h, 3 * n) + total(from_x))
+            return to_wire(of_x), to_wire(of_y)
+
+        def own(self, *terms):
+            return self.part(0, n) + total(*terms)
+
+    d = Plane(out_d[1], move(out_d[0], over_core))
+    to_y, to_x = d.diagonal(0)
+    from_y, from_x = move(to_y, over_y), move(to_x, over_x)
+    r = Plane(out_r[1], move(out_r[0], over_core))
+    q = Plane(out_q[1], move(out_q[0], over_core))
+    from_y, from_x, r.came, q.came = together(from_y, from_x, r.came, q.came)
+
+    of_x, of_y = r.sides(from_y, from_x)
+    to_y, to_x = q.diagonal()
+    by_x, by_y = move(join(of_x, to_x), over_x), move(join(of_y, to_y), over_y)
+    p = Plane(out_p[1], move(out_p[0], over_core))
+    by_x, by_y, p.came = together(by_x, by_y, p.came)
+    sum_r = r.own(by_x[:n], by_y[:n])
+
+    of_x, of_y = q.sides(by_y[n:], by_x[n:])
+    to_y, to_x = p.diagonal()
+    by_x, by_y = move(join(of_x, to_x), over_x), move(join(of_y, to_y), over_y)
+    q_more = move(to_wire(sum_r), z_inward)
+    own = Plane(out_0[1], move(out_0[0], over_core))
+    by_x, by_y, q_more, own.came = together(by_x, by_y, q_more, own.came)
+    sum_q = to_wire(q.own(by_x[:n], by_y[:n], q_more))
+
+    of_x, of_y = p.sides(by_y[n:], by_x[n:])
+    to_y, to_x = own.diagonal()
+    by_x, by_y = move(join(of_x, to_x), over_x), move(join(of_y, to_y), over_y)
+    p_more, r_more = move(sum_q, z_middle), move(sum_q, z_inward)
+    by_x, by_y, p_more, r_more = together(by_x, by_y, p_more, r_more)
+    sum_p = p.own(by_x[:n], by_y[:n], p_more)
+    sum_r = sum_r + total(r_more)
+
+    of_x, of_y = own.sides(by_y[n:], by_x[n:])
+    by_x, by_y = move(of_x, over_x), move(of_y, over_y)
+    from_p, from_r = move(to_wire(sum_p), z_pair), move(to_wire(sum_r), z_middle)
+
+    def score(out):
+        return out[3], out[2]
+
+    scores = jnp.stack(
+        [jnp.stack(score(out)) for out in (out_0, out_p, out_q)]
+        + [jnp.stack([join(*pair) for pair in zip(score(out_r), score(out_d))])]
+    ).reshape(2, 2, 2, 2, 2, n)
+    scores = scores.transpose(2, 3, 4, 0, 1, 5)
+    own_score = jnp.dot(resid.astype(f32), score_weight, precision=lax.Precision.HIGHEST)
+    doc_sums = jnp.sum(member * scores[..., None], axis=(2, 3, 4, 5))
+    doc_sums = doc_sums.at[0, 0].add(jnp.sum(member[0, 0, 0, 0, 0] * own_score[:, None], axis=0))
+    for target in (over_core, over_y):
+        doc_sums = doc_sums[0] + move(doc_sums[1], target)
+    for target in (over_x, z_pair, z_far):
+        doc_sums = doc_sums + move(doc_sums, target)
+    combined = own.own(by_x, by_y, from_p, from_r)
+    return (resid.astype(f32) + combined).astype(jnp.bfloat16), doc_sums
+
+
+def is_small():
+    return (lax.axis_size("req"), lax.axis_size("exp")) == (2 * GRID[1], GRID[0] * GRID[2])
 
 
 def local(
@@ -409,19 +549,31 @@
 ):
     tok_count = hidden_in.shape[0]
     exp_index = lax.axis_index("exp")
+    doc_len = doc_lengths[0]
     attn = attention(qkv, q_gain, k_gain, query_pages, page_table, doc_lengths, doc_query)
     attn = attn.transpose(1, 0, 2).reshape(hidden_in.shape)
     mixed = jnp.dot(attn, out_weight, preferred_element_type=jnp.float32)
     resid = (hidden_in.astype(jnp.float32) + mixed).astype(jnp.bfloat16)
     normed = rms_scale(resid.astype(jnp.float32), moe_gain).astype(jnp.bfloat16)
-    is_small = (lax.axis_size("req"), lax.axis_size("exp")) == (2 * GRID[1], GRID[0] * GRID[2])
-    moe = experts_dense if is_small else experts_by_slots
-    combined = moe(normed, routes, route_weight, gate_weight, up_weight, down_weight)
+    if is_small():
+        layer_out, doc_sums = experts_dense(
+            resid,
+            normed,
+            route_table(routes, route_weight),
+            member_table(doc_len, tok_count),
+            gate_weight,
+            up_weight,
+            down_weight,
+            score_weight,
+        )
+        return (layer_out, (doc_sums / doc_len.astype(jnp.float32))[None, :])
+    combined = experts_by_slots(
+        normed, routes, route_weight, gate_weight, up_weight, down_weight
+    )
     layer_out = (resid.astype(jnp.float32) + combined).astype(jnp.bfloat16)
     token_score = jnp.dot(
         layer_out.astype(jnp.float32), score_weight, precision=lax.Precision.HIGHEST
     )
-    doc_len = doc_lengths[0]
     doc_ends = jnp.cumsum(doc_len, dtype=jnp.int32)
     own_pos = exp_index * tok_count + jnp.arange(tok_count, dtype=jnp.int32)
     member = (own_pos[:, None] < doc_ends[None, :]) & (

time: 406 us -> 310 us (0.76)
  waiting for transfers between devices: 209 us -> 128 us
  blocking collectives: 38.5 us -> 0 us
  starting transfers between devices: 54.8 us -> 72.8 us
  other arithmetic: 20.5 us -> 31.8 us
  local copies, waits for them, and re-layouts: 21.4 us -> 17.2 us
    ppermute x35 -> x52, waiting for transfers between devices: 172 us -> 118 us  [move(): return lax.ppermute(block, ALL, pairs(target))]
    all_to_all x1, waiting for transfers between devices: 36.9 us -> 7.14 us  [attention(): lax.all_to_all(parts, 'exp', split_axis=0, concat_axis=0, tiled=True)]
    psum x1 -> x0, blocking collectives: 20.4 us -> none  [local(): doc_sums = lax.psum(doc_partial, 'exp')]
    all_to_all x1 -> x0, blocking collectives: 18.1 us -> none  [attention(): back = lax.all_to_all(out, 'exp', split_axis=0, concat_axis=0, tiled=True)]
    ppermute x35 -> x52, starting transfers between devices: 47.5 us -> 61.8 us  [move(): return lax.ppermute(block, ALL, pairs(target))]
    unnamed x49 -> x108, local copies, waits for them, and re-layouts: 18 us -> 10.3 us
    concatenate x6 -> x12, other arithmetic: 0.53 us -> 6.52 us  [join(): return jnp.concatenate(blocks, axis=0)]
    another operation x7 -> x20, other arithmetic: 0.22 us -> 6.03 us
  transfers between devices with their start and end apart: 36 -> 54, of which waited for: 21 -> 30; matrix products, arithmetic and copies ran while one was open for 6% -> 12% of each run, Pallas kernels for 9% -> 16%
where the time goes in v2:
time: 310 us; the launch traced here: 309 us
  waiting for transfers between devices  128 us (41%)
  starting transfers between devices  72.8 us (23%)
  Pallas kernels  50.9 us (16%)
  other arithmetic  31.8 us (10%)
  local copies, waits for them, and re-layouts  17.2 us (6%)
  matrix products  7.02 us (2%)
    ppermute x52, waiting for transfers between devices, move(): return lax.ppermute(block, ALL, pairs(target))  118 us
    ppermute x52, starting transfers between devices, move(): return lax.ppermute(block, ALL, pairs(target))  61.8 us
    pallas_call x5, Pallas kernels, weighted_pieces(): pl.pallas_call(functools.partial(expert_kernel, steps), grid=(2 * steps,)...  35.2 us
    pallas_call x1, Pallas kernels, attention(): pl.pallas_call(attention_kernel, out_shape=jax.ShapeDtypeStruct((tokens,...  13 us
    convert_element_type x8, other arithmetic, to_wire(): return value.astype(jnp.bfloat16)  11.1 us
    unnamed x108, local copies, waits for them, and re-layouts  10.3 us
    all_to_all x1, starting transfers between devices, attention(): lax.all_to_all(parts, 'exp', split_axis=0, concat_axis=0, tiled=True)  7.4 us
    all_to_all x1, waiting for transfers between devices, attention(): lax.all_to_all(parts, 'exp', split_axis=0, concat_axis=0, tiled=True)  7.14 us
  transfers between devices with their start and end apart: 54, of which 30 were waited for; matrix products, arithmetic and copies ran while one was open for 12% of the time, Pallas kernels for 16%

profile of v2, /device:TPU:0, one launch (start us, length us, event | category | flops | bytes accessed | tf_op | source)
XLA Modules:
  0.0 309.0 jit_solution(18141515790214920577)
XLA Ops:
  0.6 2.7 pack_heads.1
  3.4 7.4 %all-to-all-start = ((bf16[8,128,768]{2,1,0:T(8,128)(2,1)}), bf16[8,128,768]{2,1,0:T(8,128)(2,1)}, u32[]{:S(2)}, u32[]{:S(2)}) async-start(bf16[8,128,768]{2,1,0:T(8,128)(2,1)} %bitcast.113), calls=%async_computation | async-start | bytes 3145728 | tf_op jit(solution)/shard_map/all_to_all | solution.py:159
  10.9 2.1 collective-permute-start
  14.8 1.7 fusion.1.relevance_ref
  16.5 20.7 %collective-permute-done = f32[16,128]{1,0:T(8,128)S(1)} collective-permute-done((f32[16,128]{1,0:T(8,128)S(1)}, f32[16,128]{1,0:T(8,128)S(1)}, u32[]{:S(2)}, u32[]{:S(2)}) %collective-permute-start) | collective-permute-done | bytes 8224 | tf_op jit(solution)/shard_map/ppermute | solution.py:325
  37.2 3.9 %collective-permute-start.1 = (f32[2,16,128]{2,1,0:T(8,128)S(1)}, f32[2,16,128]{2,1,0:T(8,128)S(1)}, u32[]{:S(2)}, u32[]{:S(2)}) collective-permute-start(f32[2,16,128]{2,1,0:T(8,128)S(1)} %get-tuple-element.191), channel_id=1, source_target_pairs={{0,4},{1,5},{2,6},{3,7},{4,0},{5,1},{6,2},{7,3},{8,12},{9,13},{10,... | collective-permute-start | bytes 49160 | tf_op jit(solution)/shard_map/ppermute | solution.py:325
  41.3 7.1 %all-to-all-done = bf16[8,128,768]{2,1,0:T(8,128)(2,1)} async-done(((bf16[8,128,768]{2,1,0:T(8,128)(2,1)}), bf16[8,128,768]{2,1,0:T(8,128)(2,1)}, u32[]{:S(2)}, u32[]{:S(2)}) %all-to-all-start) | async-done | bytes 1572896 | tf_op jit(solution)/shard_map/all_to_all | solution.py:159
  49.7 13.0 %paged_attention.1 = bf16[1024,256]{1,0:T(8,128)(2,1)S(1)} custom-call(bf16[1024,768]{1,0:T(8,128)(2,1)} %bitcast.1.qkv_ref, bf16[1024,512]{1,0:T(8,128)(2,1)S(1)} %bitcast.110, s32[1,128]{1,0:T(1,128)S(1)} %pad.10.len_ref, s32[1,128]{1,0:T(1,128)S(1)} %pad.11.query_ref, s32[8,1]{1,0:T(8,128)S(1)} %copy.105.table_ref, f32[1,128]{1,0:T(1,128)S(1)} %bitcast.111, ...), custom_call_target="tpu_custom_call" | custom-call | tf_op jit(solution)/shard_map/paged_attention/pallas_call | solution.py:162
  63.7 3.6 %all-to-all-start.1 = ((bf16[8,128,256]{1,2,0:T(8,128)(2,1)}), bf16[8,128,256]{1,2,0:T(8,128)(2,1)S(1)}, u32[]{:S(2)}, u32[]{:S(2)}) async-start(bf16[8,128,256]{1,2,0:T(8,128)(2,1)} %copy.106), calls=%async_computation.1 | async-start | bytes 1048576 | tf_op jit(solution)/shard_map/all_to_all | solution.py:181
  67.2 2.1 collective-permute-start.2
  69.4 4.5 %collective-permute-done.2 = f32[2,2,16,128]{3,2,1,0:T(8,128)S(1)} collective-permute-done((f32[2,2,16,128]{3,2,1,0:T(8,128)S(1)}, f32[2,2,16,128]{3,2,1,0:T(8,128)S(1)}, u32[]{:S(2)}, u32[]{:S(2)}) %collective-permute-start.2) | collective-permute-done | bytes 32800 | tf_op jit(solution)/shard_map/ppermute | solution.py:325
  75.5 2.7 collective-permute-done.3
  79.7 2.1 all-to-all-done.1
  81.8 4.8 %fusion.3 = (f32[128]{0:T(128)S(1)}, bf16[128,2048]{1,0:T(8,128)(2,1)S(1)}) fusion(bf16[128,2048]{0,1:T(8,128)(2,1)S(1)} %bitcast.114, bf16[2048,2048]{1,0:T(8,128)(2,1)} %param.28, bf16[128,2048]{1,0:T(8,128)(2,1)S(1)} %copy-done.31), kind=kOutput, calls=%fused_computation.9 | convolution fusion | flops 1075314560 | bytes 9961984 | tf_op jit(solution)/shard_map/dot_general | solution.py:555
  90.6 8.6 %collective-permute-done.10 = bf16[128,2048]{1,0:T(8,128)(2,1)S(1)} collective-permute-done((bf16[128,2048]{1,0:T(8,128)(2,1)S(1)}, bf16[128,2048]{1,0:T(8,128)(2,1)S(1)}, u32[]{:S(2)}, u32[]{:S(2)}) %collective-permute-start.10) | collective-permute-done | bytes 524320 | tf_op jit(solution)/shard_map/ppermute | solution.py:325
  101.8 1.8 collective-permute-start.11
  108.9 12.5 %collective-permute-done.14 = bf16[128,2048]{1,0:T(8,128)(2,1)S(1)} collective-permute-done((bf16[128,2048]{1,0:T(8,128)(2,1)S(1)}, bf16[128,2048]{1,0:T(8,128)(2,1)S(1)}, u32[]{:S(2)}, u32[]{:S(2)}) %collective-permute-start.14) | collective-permute-done | bytes 524320 | tf_op jit(solution)/shard_map/ppermute | solution.py:325
  123.3 2.0 copy.108.scale_ref
  130.0 1.9 slice_dynamic-update-slice_fusion.1
  131.9 1.9 slice_dynamic-update-slice_fusion
  133.8 9.6 %expert_half.5 = (bf16[512,2048]{1,0:T(8,128)(2,1)S(1)}, bf16[512,2048]{1,0:T(8,128)(2,1)S(1)}, f32[512,1]{1,0:T(8,128)S(1)}, f32[512,1]{1,0:T(8,128)S(1)}) custom-call(bf16[512,2048]{1,0:T(8,128)(2,1)} %collective-permute-done.18.other_ref, bf16[512,2048]{1,0:T(8,128)(2,1)} %get-tuple-element.166.rows_ref, f32[4096,1]{1,0:T(8,128)S(1)} %copy-done.2, ...), custom_call_target="tpu_custom_call" | custom-call | flops 6442450944 | bytes 14680064 | tf_op jit(solution)/shard_map/expert_half/pallas_call | solution.py:226
  144.0 4.1 %collective-permute-done.15 = bf16[192,2048]{1,0:T(8,128)(2,1)S(1)} collective-permute-done((bf16[192,2048]{1,0:T(8,128)(2,1)S(1)}, bf16[192,2048]{1,0:T(8,128)(2,1)S(1)}, u32[]{:S(2)}, u32[]{:S(2)}) %collective-permute-start.15) | collective-permute-done | bytes 786464 | tf_op jit(solution)/shard_map/ppermute | solution.py:325
  148.6 1.7 collective-permute-start.19
  152.5 8.7 %expert_half.6 = (bf16[512,2048]{1,0:T(8,128)(2,1)}, bf16[512,2048]{1,0:T(8,128)(2,1)S(1)}, f32[512,1]{1,0:T(8,128)S(1)}, f32[512,1]{1,0:T(8,128)S(1)}) custom-call(bf16[512,2048]{1,0:T(8,128)(2,1)S(1)} %collective-permute-done.21.other_ref, bf16[512,2048]{1,0:T(8,128)(2,1)S(1)} %get-tuple-element.162.rows_ref, f32[4096,1]{1,0:T(8,128)S(1)} %copy-done.2, ...), custom_call_target="tpu_custom_call" | custom-call | flops 6442450944 | bytes 14680064 | tf_op jit(solution)/shard_map/expert_half/pallas_call | solution.py:226
  161.2 7.5 %collective-permute-done.19 = bf16[192,2048]{1,0:T(8,128)(2,1)S(1)} collective-permute-done((bf16[192,2048]{1,0:T(8,128)(2,1)S(1)}, bf16[192,2048]{1,0:T(8,128)(2,1)S(1)}, u32[]{:S(2)}, u32[]{:S(2)}) %collective-permute-start.19) | collective-permute-done | bytes 786464 | tf_op jit(solution)/shard_map/ppermute | solution.py:325
  172.8 6.4 %collective-permute-done.24 = bf16[64,2048]{1,0:T(8,128)(2,1)S(1)} collective-permute-done((bf16[64,2048]{1,0:T(8,128)(2,1)S(1)}, bf16[64,2048]{1,0:T(8,128)(2,1)S(1)}, u32[]{:S(2)}, u32[]{:S(2)}) %collective-permute-start.24) | collective-permute-done | bytes 262176 | tf_op jit(solution)/shard_map/ppermute | solution.py:325
  180.6 7.7 %expert_half.7 = (bf16[512,2048]{1,0:T(8,128)(2,1)S(1)}, bf16[512,2048]{1,0:T(8,128)(2,1)S(1)}, f32[512,1]{1,0:T(8,128)S(1)}, f32[512,1]{1,0:T(8,128)S(1)}) custom-call(bf16[512,2048]{1,0:T(8,128)(2,1)S(1)} %collective-permute-done.22.other_ref, bf16[512,2048]{1,0:T(8,128)(2,1)S(1)} %get-tuple-element.158.rows_ref, f32[4096,1]{1,0:T(8,128)S(1)} %copy-done.2, ...), custom_call_target="tpu_custom_call" | custom-call | flops 6442450944 | bytes 14680064 | tf_op jit(solution)/shard_map/expert_half/pallas_call | solution.py:226
  188.9 2.5 expert_half.8
  191.5 6.8 %expert_half.9 = (bf16[384,2048]{1,0:T(8,128)(2,1)S(1)}, bf16[384,2048]{1,0:T(8,128)(2,1)S(1)}, f32[384,1]{1,0:T(8,128)S(1)}, f32[384,1]{1,0:T(8,128)S(1)}) custom-call(bf16[384,2048]{1,0:T(8,128)(2,1)S(1)} %collective-permute-done.25.other_ref, bf16[384,2048]{1,0:T(8,128)(2,1)S(1)} %pad_maximum_fusion.rows_ref, f32[4096,1]{1,0:T(8,128)S(1)} %copy-done.2, ...), custom_call_target="tpu_custom_call" | custom-call | flops 4831838208 | bytes 12582912 | tf_op jit(solution)/shard_map/expert_half/pallas_call | solution.py:226
  200.0 7.4 %collective-permute-done.28 = bf16[64,2048]{1,0:T(8,128)(2,1)S(1)} collective-permute-done((bf16[64,2048]{1,0:T(8,128)(2,1)S(1)}, bf16[64,2048]{1,0:T(8,128)(2,1)S(1)}, u32[]{:S(2)}, u32[]{:S(2)}) %collective-permute-start.28) | collective-permute-done | bytes 262176 | tf_op jit(solution)/shard_map/ppermute | solution.py:325
  218.5 10.6 %collective-permute-done.33 = bf16[192,2048]{1,0:T(8,128)(2,1)} collective-permute-done((bf16[192,2048]{1,0:T(8,128)(2,1)}, bf16[192,2048]{1,0:T(8,128)(2,1)}, u32[]{:S(2)}, u32[]{:S(2)}) %collective-permute-start.33) | collective-permute-done | bytes 786464 | tf_op jit(solution)/shard_map/ppermute | solution.py:325
  229.1 2.1 collective-permute-done.32
  238.6 6.3 %collective-permute-start.37 = (bf16[128,2048]{1,0:T(8,128)(2,1)S(1)}, bf16[128,2048]{1,0:T(8,128)(2,1)}, u32[]{:S(2)}, u32[]{:S(2)}) collective-permute-start(bf16[128,2048]{1,0:T(8,128)(2,1)S(1)} %fusion.7), channel_id=1, source_target_pairs={{0,2},{1,3},{6,4},{7,5},{8,10},{9,11},{14,12},{15,13},{16,18},{17,... | collective-permute-start | bytes 1572872 | tf_op jit(solution)/shard_map/ppermute | solution.py:325
  245.5 7.1 %collective-permute-done.37 = bf16[128,2048]{1,0:T(8,128)(2,1)} collective-permute-done((bf16[128,2048]{1,0:T(8,128)(2,1)S(1)}, bf16[128,2048]{1,0:T(8,128)(2,1)}, u32[]{:S(2)}, u32[]{:S(2)}) %collective-permute-start.37) | collective-permute-done | bytes 524320 | tf_op jit(solution)/shard_map/ppermute | solution.py:325
  260.6 3.0 add_convert_fusion.2
  264.2 7.0 %collective-permute-start.42 = (bf16[128,2048]{1,0:T(8,128)(2,1)}, bf16[128,2048]{1,0:T(8,128)(2,1)S(1)}, u32[]{:S(2)}, u32[]{:S(2)}) collective-permute-start(bf16[128,2048]{1,0:T(8,128)(2,1)} %add_convert_fusion.2), channel_id=1, source_target_pairs={{0,2},{1,3},{6,4},{7,5},{8,10},{9,11},{14,12},{15,13},{16,18},{17,... | collective-permute-start | bytes 1572872 | tf_op jit(solution)/shard_map/ppermute | solution.py:325
  272.5 6.0 %collective-permute-done.42 = bf16[128,2048]{1,0:T(8,128)(2,1)S(1)} collective-permute-done((bf16[128,2048]{1,0:T(8,128)(2,1)}, bf16[128,2048]{1,0:T(8,128)(2,1)S(1)}, u32[]{:S(2)}, u32[]{:S(2)}) %collective-permute-start.42) | collective-permute-done | bytes 524320 | tf_op jit(solution)/shard_map/ppermute | solution.py:325
  278.5 2.1 add_convert_fusion.10
  280.6 1.8 collective-permute-start.43
  283.4 1.8 add_convert_fusion.1
  285.1 2.4 collective-permute-start.45
  287.6 1.8 add_convert_fusion
  291.3 2.4 collective-permute-done.48
  294.4 2.9 collective-permute-done.49
  297.3 2.7 collective-permute-start.50
  301.5 2.1 collective-permute-start.51
  303.6 2.4 collective-permute-done.51
  306.5 2.5 fusion.6
  (269 shorter events, 71.2 us)
Async XLA Ops:
  3.4 45.0 %all-to-all-start = ((bf16[8,128,768]{2,1,0:T(8,128)(2,1)}), bf16[8,128,768]{2,1,0:T(8,128)(2,1)}, u32[]{:S(2)}, u32[]{:S(2)}) async-start(bf16[8,128,768]{2,1,0:T(8,128)(2,1)} %bitcast.113), calls=%async_computation | async-start | bytes 3145728 | tf_op jit(solution)/shard_map/all_to_all | solution.py:159
  10.9 26.4 %collective-permute-start = (f32[16,128]{1,0:T(8,128)S(1)}, f32[16,128]{1,0:T(8,128)S(1)}, u32[]{:S(2)}, u32[]{:S(2)}) collective-permute-start(f32[16,128]{1,0:T(8,128)S(1)} %select_reduce_fusion), channel_id=1, source_target_pairs={{0,2},{1,3},{2,0},{3,1},{4,6},{5,7},{6,4},{7,5},{8,10},{9,11},{10,... | collective-permute-start | bytes 24584 | tf_op jit(solution)/shard_map/ppermute | solution.py:325
  13.2 56.2 %collective-permute-start.5 = (s32[2,32]{1,0:T(2,128)S(1)}, s32[2,32]{1,0:T(2,128)S(1)}, u32[]{:S(2)}, u32[]{:S(2)}) collective-permute-start(s32[2,32]{1,0:T(2,128)S(1)} %get-tuple-element.197), channel_id=1, source_target_pairs={{0,16},{1,17},{2,18},{3,19},{4,20},{5,21},{6,22},{7,23},{8,24},{9,... | collective-permute-start | bytes 776 | tf_op jit(solution)/shard_map/ppermute | solution.py:325
  37.2 30.0 %collective-permute-start.1 = (f32[2,16,128]{2,1,0:T(8,128)S(1)}, f32[2,16,128]{2,1,0:T(8,128)S(1)}, u32[]{:S(2)}, u32[]{:S(2)}) collective-permute-start(f32[2,16,128]{2,1,0:T(8,128)S(1)} %get-tuple-element.191), channel_id=1, source_target_pairs={{0,4},{1,5},{2,6},{3,7},{4,0},{5,1},{6,2},{7,3},{8,12},{9,13},{10,... | collective-permute-start | bytes 49160 | tf_op jit(solution)/shard_map/ppermute | solution.py:325
  63.7 18.1 %all-to-all-start.1 = ((bf16[8,128,256]{1,2,0:T(8,128)(2,1)}), bf16[8,128,256]{1,2,0:T(8,128)(2,1)S(1)}, u32[]{:S(2)}, u32[]{:S(2)}) async-start(bf16[8,128,256]{1,2,0:T(8,128)(2,1)} %copy.106), calls=%async_computation.1 | async-start | bytes 1048576 | tf_op jit(solution)/shard_map/all_to_all | solution.py:181
  67.2 6.7 %collective-permute-start.2 = (f32[2,2,16,128]{3,2,1,0:T(8,128)S(1)}, f32[2,2,16,128]{3,2,1,0:T(8,128)S(1)}, u32[]{:S(2)}, u32[]{:S(2)}) collective-permute-start(f32[2,2,16,128]{3,2,1,0:T(8,128)S(1)} %get-tuple-element.189), channel_id=1, source_target_pairs={{0,1},{1,0},{2,3},{3,2},{4,5},{5,4},{6,7},{7,6},{8,9},{9,8},{10,11... | collective-permute-start | bytes 98312 | tf_op jit(solution)/shard_map/ppermute | solution.py:325
  69.3 6.2 %collective-permute-start.6 = (s32[2,2,32]{2,1,0:T(2,128)S(1)}, s32[2,2,32]{2,1,0:T(2,128)S(1)}, u32[]{:S(2)}, u32[]{:S(2)}) collective-permute-start(s32[2,2,32]{2,1,0:T(2,128)S(1)} %get-tuple-element.195), channel_id=1, source_target_pairs={{0,8},{1,9},{2,10},{3,11},{4,12},{5,13},{6,14},{7,15},{8,0},{9,1},... | collective-permute-start | bytes 1544 | tf_op jit(solution)/shard_map/ppermute | solution.py:325
  73.9 4.3 %collective-permute-start.3 = (f32[2,2,2,16,128]{4,3,2,1,0:T(8,128)S(1)}, f32[2,2,2,16,128]{4,3,2,1,0:T(8,128)S(1)}, u32[]{:S(2)}, u32[]{:S(2)}) collective-permute-start(f32[2,2,2,16,128]{4,3,2,1,0:T(8,128)S(1)} %get-tuple-element.187), channel_id=1, source_target_pairs={{0,16},{1,17},{2,18},{3,19},{4,20},{5,21},{6,22},{7,23},{8,24},{9,... | collective-permute-start | bytes 196616 | tf_op jit(solution)/shard_map/ppermute | solution.py:325
  86.8 12.4 %collective-permute-start.10 = (bf16[128,2048]{1,0:T(8,128)(2,1)S(1)}, bf16[128,2048]{1,0:T(8,128)(2,1)S(1)}, u32[]{:S(2)}, u32[]{:S(2)}) collective-permute-start(bf16[128,2048]{1,0:T(8,128)(2,1)S(1)} %fusion.5), channel_id=1, source_target_pairs={{0,16},{1,17},{2,18},{3,19},{4,20},{5,21},{6,22},{7,23},{8,24},{9,... | collective-permute-start | bytes 1572872 | tf_op jit(solution)/shard_map/ppermute | solution.py:325
  88.4 12.0 %collective-permute-start.7 = (bf16[128,2048]{1,0:T(8,128)(2,1)S(1)}, bf16[128,2048]{1,0:T(8,128)(2,1)S(1)}, u32[]{:S(2)}, u32[]{:S(2)}) collective-permute-start(bf16[128,2048]{1,0:T(8,128)(2,1)S(1)} %fusion.5), channel_id=1, source_target_pairs={{0,2},{1,3},{2,0},{3,1},{4,6},{5,7},{6,4},{7,5},{8,10},{9,11},{10,... | collective-permute-start | bytes 1572872 | tf_op jit(solution)/shard_map/ppermute | solution.py:325
  89.2 11.3 %collective-permute-start.8 = (bf16[128,2048]{1,0:T(8,128)(2,1)S(1)}, bf16[128,2048]{1,0:T(8,128)(2,1)S(1)}, u32[]{:S(2)}, u32[]{:S(2)}) collective-permute-start(bf16[128,2048]{1,0:T(8,128)(2,1)S(1)} %fusion.5), channel_id=1, source_target_pairs={{2,4},{3,5},{4,2},{5,3},{10,12},{11,13},{12,10},{13,11},{18,20},{1... | collective-permute-start | bytes 1572872 | tf_op jit(solution)/shard_map/ppermute | solution.py:325
  89.9 11.6 %collective-permute-start.9 = (bf16[128,2048]{1,0:T(8,128)(2,1)S(1)}, bf16[128,2048]{1,0:T(8,128)(2,1)S(1)}, u32[]{:S(2)}, u32[]{:S(2)}) collective-permute-start(bf16[128,2048]{1,0:T(8,128)(2,1)S(1)} %fusion.5), channel_id=1, source_target_pairs={{0,1},{1,0},{2,3},{3,2},{4,5},{5,4},{6,7},{7,6},{8,9},{9,8},{10,11... | collective-permute-start | bytes 1572872 | tf_op jit(solution)/shard_map/ppermute | solution.py:325
  101.8 19.7 %collective-permute-start.11 = (bf16[192,2048]{1,0:T(8,128)(2,1)S(1)}, bf16[192,2048]{1,0:T(8,128)(2,1)S(1)}, u32[]{:S(2)}, u32[]{:S(2)}) collective-permute-start(bf16[192,2048]{1,0:T(8,128)(2,1)S(1)} %get-tuple-element.183), channel_id=1, source_target_pairs={{0,1},{1,0},{2,3},{3,2},{4,5},{5,4},{6,7},{7,6},{8,9},{9,8},{10,11... | collective-permute-start | bytes 2359304 | tf_op jit(solution)/shard_map/ppermute | solution.py:325
  103.6 17.9 %collective-permute-start.12 = (bf16[192,2048]{1,0:T(8,128)(2,1)S(1)}, bf16[192,2048]{1,0:T(8,128)(2,1)S(1)}, u32[]{:S(2)}, u32[]{:S(2)}) collective-permute-start(bf16[192,2048]{1,0:T(8,128)(2,1)S(1)} %get-tuple-element.182), channel_id=1, source_target_pairs={{0,16},{1,17},{2,18},{3,19},{4,20},{5,21},{6,22},{7,23},{8,24},{9,... | collective-permute-start | bytes 2359304 | tf_op jit(solution)/shard_map/ppermute | solution.py:325
  104.1 4.8 %collective-permute-start.13 = (bf16[128,2048]{1,0:T(8,128)(2,1)S(1)}, bf16[128,2048]{1,0:T(8,128)(2,1)S(1)}, u32[]{:S(2)}, u32[]{:S(2)}) collective-permute-start(bf16[128,2048]{1,0:T(8,128)(2,1)S(1)} %collective-permute-done.7), channel_id=1, source_target_pairs={{2,4},{3,5},{4,2},{5,3},{10,12},{11,13},{12,10},{13,11},{18,20},{1... | collective-permute-start | bytes 1572872 | tf_op jit(solution)/shard_map/ppermute | solution.py:325
  104.8 16.6 %collective-permute-start.14 = (bf16[128,2048]{1,0:T(8,128)(2,1)S(1)}, bf16[128,2048]{1,0:T(8,128)(2,1)S(1)}, u32[]{:S(2)}, u32[]{:S(2)}) collective-permute-start(bf16[128,2048]{1,0:T(8,128)(2,1)S(1)} %collective-permute-done.8), channel_id=1, source_target_pairs={{2,0},{3,1},{4,6},{5,7},{10,8},{11,9},{12,14},{13,15},{18,16},{19,... | collective-permute-start | bytes 1572872 | tf_op jit(solution)/shard_map/ppermute | solution.py:325
  123.2 10.6 %collective-permute-start.18 = (bf16[512,2048]{1,0:T(8,128)(2,1)}, bf16[512,2048]{1,0:T(8,128)(2,1)}, u32[]{:S(2)}, u32[]{:S(2)}) collective-permute-start(bf16[512,2048]{1,0:T(8,128)(2,1)} %get-tuple-element.166.rows_ref), channel_id=1, source_target_pairs={{0,8},{1,9},{2,10},{3,11},{4,12},{5,13},{6,14},{7,15},{8,0},{9,1},... | collective-permute-start | bytes 6291464 | tf_op jit(solution)/shard_map/ppermute | solution.py:325
  126.6 17.4 %collective-permute-start.17 = (bf16[128,2048]{1,0:T(8,128)(2,1)S(1)}, bf16[128,2048]{1,0:T(8,128)(2,1)S(1)}, u32[]{:S(2)}, u32[]{:S(2)}) collective-permute-start(bf16[128,2048]{1,0:T(8,128)(2,1)S(1)} %get-tuple-element.141), channel_id=1, source_target_pairs={{2,0},{3,1},{4,6},{5,7},{10,8},{11,9},{12,14},{13,15},{18,16},{19,... | collective-permute-start | bytes 1572872 | tf_op jit(solution)/shard_map/ppermute | solution.py:325
  128.1 20.0 %collective-permute-start.15 = (bf16[192,2048]{1,0:T(8,128)(2,1)S(1)}, bf16[192,2048]{1,0:T(8,128)(2,1)S(1)}, u32[]{:S(2)}, u32[]{:S(2)}) collective-permute-start(bf16[192,2048]{1,0:T(8,128)(2,1)S(1)} %get-tuple-element.181), channel_id=1, source_target_pairs={{0,1},{1,0},{2,3},{3,2},{4,5},{5,4},{6,7},{7,6},{8,9},{9,8},{10,11... | collective-permute-start | bytes 2359304 | tf_op jit(solution)/shard_map/ppermute | solution.py:325
  128.5 19.6 %collective-permute-start.16 = (bf16[192,2048]{1,0:T(8,128)(2,1)S(1)}, bf16[192,2048]{1,0:T(8,128)(2,1)S(1)}, u32[]{:S(2)}, u32[]{:S(2)}) collective-permute-start(bf16[192,2048]{1,0:T(8,128)(2,1)S(1)} %get-tuple-element.180), channel_id=1, source_target_pairs={{0,16},{1,17},{2,18},{3,19},{4,20},{5,21},{6,22},{7,23},{8,24},{9,... | collective-permute-start | bytes 2359304 | tf_op jit(solution)/shard_map/ppermute | solution.py:325
  148.6 20.0 %collective-permute-start.19 = (bf16[192,2048]{1,0:T(8,128)(2,1)S(1)}, bf16[192,2048]{1,0:T(8,128)(2,1)S(1)}, u32[]{:S(2)}, u32[]{:S(2)}) collective-permute-start(bf16[192,2048]{1,0:T(8,128)(2,1)S(1)} %get-tuple-element.179), channel_id=1, source_target_pairs={{0,1},{1,0},{2,3},{3,2},{4,5},{5,4},{6,7},{7,6},{8,9},{9,8},{10,11... | collective-permute-start | bytes 2359304 | tf_op jit(solution)/shard_map/ppermute | solution.py:325
  150.4 19.7 %collective-permute-start.20 = (bf16[192,2048]{1,0:T(8,128)(2,1)S(1)}, bf16[192,2048]{1,0:T(8,128)(2,1)S(1)}, u32[]{:S(2)}, u32[]{:S(2)}) collective-permute-start(bf16[192,2048]{1,0:T(8,128)(2,1)S(1)} %get-tuple-element.178), channel_id=1, source_target_pairs={{0,16},{1,17},{2,18},{3,19},{4,20},{5,21},{6,22},{7,23},{8,24},{9,... | collective-permute-start | bytes 2359304 | tf_op jit(solution)/shard_map/ppermute | solution.py:325
  170.2 10.4 %collective-permute-start.22 = (bf16[512,2048]{1,0:T(8,128)(2,1)S(1)}, bf16[512,2048]{1,0:T(8,128)(2,1)S(1)}, u32[]{:S(2)}, u32[]{:S(2)}) collective-permute-start(bf16[512,2048]{1,0:T(8,128)(2,1)S(1)} %get-tuple-element.158.rows_ref), channel_id=1, source_target_pairs={{0,8},{1,9},{2,10},{3,11},{4,12},{5,13},{6,14},{7,15},{8,0},{9,1},... | collective-permute-start | bytes 6291464 | tf_op jit(solution)/shard_map/ppermute | solution.py:325
  170.4 10.1 %collective-permute-start.25 = (bf16[384,2048]{1,0:T(8,128)(2,1)S(1)}, bf16[384,2048]{1,0:T(8,128)(2,1)S(1)}, u32[]{:S(2)}, u32[]{:S(2)}) collective-permute-start(bf16[384,2048]{1,0:T(8,128)(2,1)S(1)} %pad_maximum_fusion.rows_ref), channel_id=1, source_target_pairs={{0,8},{1,9},{2,10},{3,11},{4,12},{5,13},{6,14},{7,15},{8,0},{9,1},... | collective-permute-start | bytes 4718600 | tf_op jit(solution)/shard_map/ppermute | solution.py:325
  171.0 8.3 %collective-permute-start.24 = (bf16[64,2048]{1,0:T(8,128)(2,1)S(1)}, bf16[64,2048]{1,0:T(8,128)(2,1)S(1)}, u32[]{:S(2)}, u32[]{:S(2)}) collective-permute-start(bf16[64,2048]{1,0:T(8,128)(2,1)S(1)} %get-tuple-element.159), channel_id=1, source_target_pairs={{0,16},{1,17},{2,18},{3,19},{4,20},{5,21},{6,22},{7,23},{8,24},{9,... | collective-permute-start | bytes 786440 | tf_op jit(solution)/shard_map/ppermute | solution.py:325
  172.5 8.0 %collective-permute-start.23 = (bf16[64,2048]{1,0:T(8,128)(2,1)S(1)}, bf16[64,2048]{1,0:T(8,128)(2,1)S(1)}, u32[]{:S(2)}, u32[]{:S(2)}) collective-permute-start(bf16[64,2048]{1,0:T(8,128)(2,1)S(1)} %get-tuple-element.161), channel_id=1, source_target_pairs={{0,1},{1,0},{2,3},{3,2},{4,5},{5,4},{6,7},{7,6},{8,9},{9,8},{10,11... | collective-permute-start | bytes 786440 | tf_op jit(solution)/shard_map/ppermute | solution.py:325
  180.6 8.3 %collective-permute-start.26 = (bf16[128,2048]{1,0:T(8,128)(2,1)S(1)}, bf16[128,2048]{1,0:T(8,128)(2,1)S(1)}, u32[]{:S(2)}, u32[]{:S(2)}) collective-permute-start(bf16[128,2048]{1,0:T(8,128)(2,1)S(1)} %constant_dynamic-update-slice_fusion.5.rows_ref), channel_id=1, source_target_pairs={{0,8},{1,9},{2,10},{3,11},{4,12},{5,13},{6,14},{7,15},{8,0},{9,1},... | collective-permute-start | bytes 1572872 | tf_op jit(solution)/shard_map/ppermute | solution.py:325
  188.3 19.3 %collective-permute-start.31 = (bf16[512,2048]{1,0:T(8,128)(2,1)S(1)}, bf16[512,2048]{1,0:T(8,128)(2,1)S(1)}, u32[]{:S(2)}, u32[]{:S(2)}) collective-permute-start(bf16[512,2048]{1,0:T(8,128)(2,1)S(1)} %get-tuple-element.109), channel_id=1, source_target_pairs={{0,8},{1,9},{2,10},{3,11},{4,12},{5,13},{6,14},{7,15},{8,0},{9,1},... | collective-permute-start | bytes 6291464 | tf_op jit(solution)/shard_map/ppermute | solution.py:325
  191.4 7.5 %collective-permute-start.27 = (bf16[128,2048]{1,0:T(8,128)(2,1)S(1)}, bf16[128,2048]{1,0:T(8,128)(2,1)S(1)}, u32[]{:S(2)}, u32[]{:S(2)}) collective-permute-start(bf16[128,2048]{1,0:T(8,128)(2,1)S(1)} %get-tuple-element.106), channel_id=1, source_target_pairs={{0,8},{1,9},{2,10},{3,11},{4,12},{5,13},{6,14},{7,15},{8,0},{9,1},... | collective-permute-start | bytes 1572872 | tf_op jit(solution)/shard_map/ppermute | solution.py:325
  198.3 9.3 %collective-permute-start.30 = (bf16[384,2048]{1,0:T(8,128)(2,1)S(1)}, bf16[384,2048]{1,0:T(8,128)(2,1)S(1)}, u32[]{:S(2)}, u32[]{:S(2)}) collective-permute-start(bf16[384,2048]{1,0:T(8,128)(2,1)S(1)} %get-tuple-element.108), channel_id=1, source_target_pairs={{0,8},{1,9},{2,10},{3,11},{4,12},{5,13},{6,14},{7,15},{8,0},{9,1},... | collective-permute-start | bytes 4718600 | tf_op jit(solution)/shard_map/ppermute | solution.py:325
  199.1 8.3 %collective-permute-start.28 = (bf16[64,2048]{1,0:T(8,128)(2,1)S(1)}, bf16[64,2048]{1,0:T(8,128)(2,1)S(1)}, u32[]{:S(2)}, u32[]{:S(2)}) collective-permute-start(bf16[64,2048]{1,0:T(8,128)(2,1)S(1)} %get-tuple-element.177), channel_id=1, source_target_pairs={{0,16},{1,17},{2,18},{3,19},{4,20},{5,21},{6,22},{7,23},{8,24},{9,... | collective-permute-start | bytes 786440 | tf_op jit(solution)/shard_map/ppermute | solution.py:325
  199.6 8.0 %collective-permute-start.29 = (bf16[64,2048]{1,0:T(8,128)(2,1)S(1)}, bf16[64,2048]{1,0:T(8,128)(2,1)S(1)}, u32[]{:S(2)}, u32[]{:S(2)}) collective-permute-start(bf16[64,2048]{1,0:T(8,128)(2,1)S(1)} %get-tuple-element.176), channel_id=1, source_target_pairs={{0,1},{1,0},{2,3},{3,2},{4,5},{5,4},{6,7},{7,6},{8,9},{9,8},{10,11... | collective-permute-start | bytes 786440 | tf_op jit(solution)/shard_map/ppermute | solution.py:325
  200.0 18.6 %collective-permute-start.34 = (bf16[512,2048]{1,0:T(8,128)(2,1)}, bf16[512,2048]{1,0:T(8,128)(2,1)}, u32[]{:S(2)}, u32[]{:S(2)}) collective-permute-start(bf16[512,2048]{1,0:T(8,128)(2,1)} %get-tuple-element.115), channel_id=1, source_target_pairs={{0,8},{1,9},{2,10},{3,11},{4,12},{5,13},{6,14},{7,15},{8,0},{9,1},... | collective-permute-start | bytes 6291464 | tf_op jit(solution)/shard_map/ppermute | solution.py:325
  210.4 18.8 %collective-permute-start.33 = (bf16[192,2048]{1,0:T(8,128)(2,1)}, bf16[192,2048]{1,0:T(8,128)(2,1)}, u32[]{:S(2)}, u32[]{:S(2)}) collective-permute-start(bf16[192,2048]{1,0:T(8,128)(2,1)} %pad_maximum_fusion.8), channel_id=1, source_target_pairs={{0,16},{1,17},{2,18},{3,19},{4,20},{5,21},{6,22},{7,23},{8,24},{9,... | collective-permute-start | bytes 2359304 | tf_op jit(solution)/shard_map/ppermute | solution.py:325
  212.8 18.4 %collective-permute-start.32 = (bf16[192,2048]{1,0:T(8,128)(2,1)}, bf16[192,2048]{1,0:T(8,128)(2,1)}, u32[]{:S(2)}, u32[]{:S(2)}) collective-permute-start(bf16[192,2048]{1,0:T(8,128)(2,1)} %pad_maximum_fusion.7), channel_id=1, source_target_pairs={{0,1},{1,0},{2,3},{3,2},{4,5},{5,4},{6,7},{7,6},{8,9},{9,8},{10,11... | collective-permute-start | bytes 2359304 | tf_op jit(solution)/shard_map/ppermute | solution.py:325
  215.4 30.2 %collective-permute-start.38 = (bf16[512,2048]{1,0:T(8,128)(2,1)}, bf16[512,2048]{1,0:T(8,128)(2,1)}, u32[]{:S(2)}, u32[]{:S(2)}) collective-permute-start(bf16[512,2048]{1,0:T(8,128)(2,1)} %copy-done.21), channel_id=1, source_target_pairs={{0,8},{1,9},{2,10},{3,11},{4,12},{5,13},{6,14},{7,15},{8,0},{9,1},... | collective-permute-start | bytes 6291464 | tf_op jit(solution)/shard_map/ppermute | solution.py:325
  235.0 17.6 %collective-permute-start.36 = (bf16[192,2048]{1,0:T(8,128)(2,1)}, bf16[192,2048]{1,0:T(8,128)(2,1)}, u32[]{:S(2)}, u32[]{:S(2)}) collective-permute-start(bf16[192,2048]{1,0:T(8,128)(2,1)} %pad_maximum_fusion.10), channel_id=1, source_target_pairs={{0,16},{1,17},{2,18},{3,19},{4,20},{5,21},{6,22},{7,23},{8,24},{9,... | collective-permute-start | bytes 2359304 | tf_op jit(solution)/shard_map/ppermute | solution.py:325
  236.6 17.3 %collective-permute-start.35 = (bf16[192,2048]{1,0:T(8,128)(2,1)}, bf16[192,2048]{1,0:T(8,128)(2,1)}, u32[]{:S(2)}, u32[]{:S(2)}) collective-permute-start(bf16[192,2048]{1,0:T(8,128)(2,1)} %pad_maximum_fusion.9), channel_id=1, source_target_pairs={{0,1},{1,0},{2,3},{3,2},{4,5},{5,4},{6,7},{7,6},{8,9},{9,8},{10,11... | collective-permute-start | bytes 2359304 | tf_op jit(solution)/shard_map/ppermute | solution.py:325
  238.6 14.0 %collective-permute-start.37 = (bf16[128,2048]{1,0:T(8,128)(2,1)S(1)}, bf16[128,2048]{1,0:T(8,128)(2,1)}, u32[]{:S(2)}, u32[]{:S(2)}) collective-permute-start(bf16[128,2048]{1,0:T(8,128)(2,1)S(1)} %fusion.7), channel_id=1, source_target_pairs={{0,2},{1,3},{6,4},{7,5},{8,10},{9,11},{14,12},{15,13},{16,18},{17,... | collective-permute-start | bytes 1572872 | tf_op jit(solution)/shard_map/ppermute | solution.py:325
  257.9 20.6 %collective-permute-start.40 = (bf16[192,2048]{1,0:T(8,128)(2,1)}, bf16[192,2048]{1,0:T(8,128)(2,1)S(1)}, u32[]{:S(2)}, u32[]{:S(2)}) collective-permute-start(bf16[192,2048]{1,0:T(8,128)(2,1)} %pad_maximum_fusion.12), channel_id=1, source_target_pairs={{0,16},{1,17},{2,18},{3,19},{4,20},{5,21},{6,22},{7,23},{8,24},{9,... | collective-permute-start | bytes 2359304 | tf_op jit(solution)/shard_map/ppermute | solution.py:325
  260.2 18.3 %collective-permute-start.39 = (bf16[192,2048]{1,0:T(8,128)(2,1)}, bf16[192,2048]{1,0:T(8,128)(2,1)}, u32[]{:S(2)}, u32[]{:S(2)}) collective-permute-start(bf16[192,2048]{1,0:T(8,128)(2,1)} %pad_maximum_fusion.11), channel_id=1, source_target_pairs={{0,1},{1,0},{2,3},{3,2},{4,5},{5,4},{6,7},{7,6},{8,9},{9,8},{10,11... | collective-permute-start | bytes 2359304 | tf_op jit(solution)/shard_map/ppermute | solution.py:325
  263.5 9.0 %collective-permute-start.41 = (bf16[128,2048]{1,0:T(8,128)(2,1)}, bf16[128,2048]{1,0:T(8,128)(2,1)S(1)}, u32[]{:S(2)}, u32[]{:S(2)}) collective-permute-start(bf16[128,2048]{1,0:T(8,128)(2,1)} %add_convert_fusion.2), channel_id=1, source_target_pairs={{2,4},{3,5},{4,2},{5,3},{10,12},{11,13},{12,10},{13,11},{18,20},{1... | collective-permute-start | bytes 1572872 | tf_op jit(solution)/shard_map/ppermute | solution.py:325
  264.2 14.3 %collective-permute-start.42 = (bf16[128,2048]{1,0:T(8,128)(2,1)}, bf16[128,2048]{1,0:T(8,128)(2,1)S(1)}, u32[]{:S(2)}, u32[]{:S(2)}) collective-permute-start(bf16[128,2048]{1,0:T(8,128)(2,1)} %add_convert_fusion.2), channel_id=1, source_target_pairs={{0,2},{1,3},{6,4},{7,5},{8,10},{9,11},{14,12},{15,13},{16,18},{17,... | collective-permute-start | bytes 1572872 | tf_op jit(solution)/shard_map/ppermute | solution.py:325
  280.6 25.8 %collective-permute-start.43 = (bf16[128,2048]{1,0:T(8,128)(2,1)S(1)}, bf16[128,2048]{1,0:T(8,128)(2,1)S(1)}, u32[]{:S(2)}, u32[]{:S(2)}) collective-permute-start(bf16[128,2048]{1,0:T(8,128)(2,1)S(1)} %pad_maximum_fusion.13), channel_id=1, source_target_pairs={{0,1},{1,0},{2,3},{3,2},{4,5},{5,4},{6,7},{7,6},{8,9},{9,8},{10,11... | collective-permute-start | bytes 1572872 | tf_op jit(solution)/shard_map/ppermute | solution.py:325
  282.4 24.0 %collective-permute-start.44 = (bf16[128,2048]{1,0:T(8,128)(2,1)S(1)}, bf16[128,2048]{1,0:T(8,128)(2,1)S(1)}, u32[]{:S(2)}, u32[]{:S(2)}) collective-permute-start(bf16[128,2048]{1,0:T(8,128)(2,1)S(1)} %pad_maximum_fusion.14), channel_id=1, source_target_pairs={{0,16},{1,17},{2,18},{3,19},{4,20},{5,21},{6,22},{7,23},{8,24},{9,... | collective-permute-start | bytes 1572872 | tf_op jit(solution)/shard_map/ppermute | solution.py:325
  285.1 21.3 %collective-permute-start.45 = (bf16[128,2048]{1,0:T(8,128)(2,1)S(1)}, bf16[128,2048]{1,0:T(8,128)(2,1)S(1)}, u32[]{:S(2)}, u32[]{:S(2)}) collective-permute-start(bf16[128,2048]{1,0:T(8,128)(2,1)S(1)} %add_convert_fusion.1), channel_id=1, source_target_pairs={{0,2},{1,3},{2,0},{3,1},{4,6},{5,7},{6,4},{7,5},{8,10},{9,11},{10,... | collective-permute-start | bytes 1572872 | tf_op jit(solution)/shard_map/ppermute | solution.py:325
  289.4 17.1 %collective-permute-start.46 = (bf16[128,2048]{1,0:T(8,128)(2,1)S(1)}, bf16[128,2048]{1,0:T(8,128)(2,1)S(1)}, u32[]{:S(2)}, u32[]{:S(2)}) collective-permute-start(bf16[128,2048]{1,0:T(8,128)(2,1)S(1)} %add_convert_fusion), channel_id=1, source_target_pairs={{2,4},{3,5},{4,2},{5,3},{10,12},{11,13},{12,10},{13,11},{18,20},{1... | collective-permute-start | bytes 1572872 | tf_op jit(solution)/shard_map/ppermute | solution.py:325
  301.5 4.4 %collective-permute-start.51 = (f32[32]{0:T(128)S(1)}, f32[32]{0:T(128)S(1)}, u32[]{:S(2)}, u32[]{:S(2)}) collective-permute-start(f32[32]{0:T(128)S(1)} %add.262), channel_id=1, source_target_pairs={{0,4},{1,5},{2,6},{3,7},{4,0},{5,1},{6,2},{7,3},{8,12},{9,13},{10,... | collective-permute-start | bytes 392 | tf_op jit(solution)/shard_map/ppermute | solution.py:325
  (54 other events, 612.5 us)

commit v3 on v1

--- a/solution.py
+++ b/solution.py
@@ -135,30 +135,28 @@
             out_ref[rows, cols] = (weighted / total).astype(jnp.bfloat16)
 
 
-def column_block(exp_count, part, index):
-    return (0, part * exp_count + index)
-
-
-def pack_kernel(q_ref, k_ref, v_ref, out_ref):
-    out_ref[...] = jnp.concatenate([q_ref[...], k_ref[...], v_ref[...]], axis=1)
-
-
-def attention(qkv, q_gain, k_gain, pages, page_table, doc_len, doc_query):
+def pack_kernel(exp_count, qkv_ref, out_ref):
+    rows = qkv_ref.shape[0]
+    own = qkv_ref.shape[1] // (3 * exp_count)
+    for index in range(exp_count):
+        for part in range(3):
+            at = (part * exp_count + index) * own
+            out_ref[index * rows : (index + 1) * rows, part * own : (part + 1) * own] = qkv_ref[
+                :, at : at + own
+            ]
+
+
+def attention(qkv, q_gain, k_gain, pages, page_table, doc_len, doc_query, tables):
     tok_count, width = qkv.shape[0], qkv.shape[1] // 3
     exp_count = lax.axis_size("exp")
     own = width // exp_count
     tokens = exp_count * tok_count
     parts = pl.pallas_call(
-        pack_kernel,
-        grid=(exp_count,),
+        functools.partial(pack_kernel, exp_count),
         out_shape=jax.ShapeDtypeStruct((tokens, 3 * own), jnp.bfloat16),
-        in_specs=[
-            pl.BlockSpec((tok_count, own), functools.partial(column_block, exp_count, part))
-            for part in range(3)
-        ],
-        out_specs=pl.BlockSpec((tok_count, 3 * own), lambda i: (i, 0)),
+        compiler_params=pltpu.CompilerParams(vmem_limit_bytes=8 * 1024 * 1024),
         name="pack_heads",
-    )(qkv, qkv, qkv)
+    )(qkv)
     group = lax.all_to_all(parts, "exp", split_axis=0, concat_axis=0, tiled=True)
     docs = doc_len.shape[1]
     spare = ((0, 0), (0, LANES - docs))
@@ -169,7 +167,7 @@
             pltpu.VMEM((tokens, own), jnp.bfloat16),
             pltpu.VMEM((tokens, own), jnp.bfloat16),
         ],
-        compiler_params=pltpu.CompilerParams(vmem_limit_bytes=32 * 1024 * 1024),
+        compiler_params=pltpu.CompilerParams(vmem_limit_bytes=14 * 1024 * 1024),
         name="paged_attention",
     )(
         group,
@@ -181,45 +179,114 @@
         k_gain.reshape(1, HD),
         jnp.asarray(rope_table()),
     )
+    out, tables = lax.optimization_barrier((out, tables))
     back = lax.all_to_all(out, "exp", split_axis=0, concat_axis=0, tiled=True)
-    return back.reshape(exp_count, tok_count, own)
-
-
-def expert_kernel(rows_ref, scale_ref, gate_ref, up_ref, down_ref, out_ref):
-    rows = rows_ref[...]
-    gate_act = jnp.dot(rows, gate_ref[0], preferred_element_type=jnp.float32)
-    up_act = jnp.dot(rows, up_ref[0], preferred_element_type=jnp.float32)
-    hidden_act = jax.nn.silu(gate_act) * (up_act * scale_ref[...])
-    out_ref[...] = jnp.dot(
-        hidden_act.astype(jnp.bfloat16), down_ref[0], preferred_element_type=jnp.float32
-    ).astype(jnp.bfloat16)
-
-
-def weighted_piece(rows, scale, gate_weight, up_weight, down_weight):
-    count, width = rows.shape
-    hidden = gate_weight.shape[2]
-    tile = 256
-    once = pl.Buffered(1)
+    return back.reshape(exp_count, tok_count, own), tables
+
+
+def expert_kernel(sides, steps, first, held, *refs):
+    rows_refs, refs = refs[:sides], refs[sides:]
+    scale_ref, relevance_ref, *weight_refs = refs[:5]
+    out_refs, score_ref = refs[5 : 5 + sides], refs[5 + sides]
+    step = pl.program_id(0)
+    per_tile = rows_refs[0].shape[0] // LANES
+    if held:
+        gate, up, down = (ref.at[0] for ref in weight_refs)
+    else:
+        gate, up, down, sems = refs[6 + sides :]
+        copies = [
+            pltpu.make_async_copy(source.at[0], target, sems.at[at])
+            for at, (source, target) in enumerate(zip(weight_refs, (gate, up, down)))
+        ]
+
+    def work(rows_ref, out_ref, arriving):
+        rows = rows_ref[...]
+        if arriving:
+            copies[0].wait()
+        gate_act = jnp.dot(rows, gate[...], preferred_element_type=jnp.float32)
+        if arriving:
+            copies[1].wait()
+        up_act = jnp.dot(rows, up[...], preferred_element_type=jnp.float32)
+        spread = [
+            jnp.broadcast_to(
+                scale_ref[pl.ds(first + step * per_tile + part, 1)], (LANES, LANES)
+            ).T
+            for part in range(per_tile)
+        ]
+        scale = jnp.concatenate(spread, axis=0)
+        scale = jnp.concatenate([scale] * (up_act.shape[1] // LANES), axis=1)
+        hidden_act = (jax.nn.silu(gate_act) * (up_act * scale)).astype(jnp.bfloat16)
+        score = lax.dot_general(
+            relevance_ref[...], hidden_act, (((1,), (1,)), ((), ())),
+            preferred_element_type=jnp.float32,
+        )
+        score = jnp.sum(score, axis=0, keepdims=True)
+        for part in range(per_tile):
+            score_ref[pl.ds(step * per_tile + part, 1)] = score[
+                :, part * LANES : (part + 1) * LANES
+            ]
+        if arriving:
+            copies[2].wait()
+        out_ref[...] = jnp.dot(
+            hidden_act, down[...], preferred_element_type=jnp.float32
+        ).astype(jnp.bfloat16)
+
+    if not held:
+
+        @pl.when(step == 0)
+        def _():
+            for copy in copies:
+                copy.start()
+            work(rows_refs[0], out_refs[0], True)
+
+    for side in range(sides):
+        mine = step // steps == side
+        if not held and side == 0:
+            mine = mine & (step > 0)
+
+        @pl.when(mine)
+        def _():
+            work(rows_refs[side], out_refs[side], False)
+
+
+def weighted_pieces(rows, scale, first, relevance, weights, held):
+    sides = len(rows)
+    count, width = rows[0].shape
+    hidden = weights[0].shape[2]
+    tile = 256 if count % 256 == 0 else count
+    steps = count // tile
+    space = pltpu.VMEM if held else pltpu.HBM
+    weights = [pltpu.with_memory_space_constraint(weight, space) for weight in weights]
+
+    def rows_of(side):
+        return pl.BlockSpec((tile, width), lambda i: (jnp.clip(i - side * steps, 0, steps - 1), 0))
+
+    fetched = [pltpu.VMEM(weight.shape[1:], jnp.bfloat16) for weight in weights]
+    kept = pltpu.HBM if held else jax.ShapeDtypeStruct
     return pl.pallas_call(
-        expert_kernel,
-        grid=(count // tile,),
-        out_shape=jax.ShapeDtypeStruct(rows.shape, jnp.bfloat16),
-        in_specs=[
-            pl.BlockSpec((tile, width), lambda i: (i, 0)),
-            pl.BlockSpec((tile, 1), lambda i: (i, 0)),
-            pl.BlockSpec((1, width, hidden), lambda i: (0, 0, 0), pipeline_mode=once),
-            pl.BlockSpec((1, width, hidden), lambda i: (0, 0, 0), pipeline_mode=once),
-            pl.BlockSpec((1, hidden, width), lambda i: (0, 0, 0), pipeline_mode=once),
-        ],
-        out_specs=pl.BlockSpec((tile, width), lambda i: (i, 0)),
-        compiler_params=pltpu.CompilerParams(vmem_limit_bytes=24 * 1024 * 1024),
+        functools.partial(expert_kernel, sides, steps, first, held),
+        grid=(sides * steps,),
+        out_shape=[kept((count, width), jnp.bfloat16)] * sides
+        + [jax.ShapeDtypeStruct((sides * count // LANES, LANES), jnp.float32)],
+        in_specs=[rows_of(side) for side in range(sides)]
+        + [
+            pl.BlockSpec(scale.shape, lambda i: (0, 0)),
+            pl.BlockSpec(relevance.shape, lambda i: (0, 0)),
+        ]
+        + [pl.BlockSpec(memory_space=space)] * 3,
+        out_specs=[rows_of(side) for side in range(sides)]
+        + [pl.BlockSpec((sides * count // LANES, LANES), lambda i: (0, 0))],
+        scratch_shapes=[] if held else fetched + [pltpu.SemaphoreType.DMA((3,))],
+        compiler_params=pltpu.CompilerParams(
+            vmem_limit_bytes=((14 if tile <= 256 else 19) + (0 if held else 7)) * 1024 * 1024
+        ),
         cost_estimate=pl.CostEstimate(
-            flops=6 * count * width * hidden,
-            bytes_accessed=4 * count * width + 6 * width * hidden,
-            transcendentals=count * hidden,
+            flops=6 * sides * count * width * hidden,
+            bytes_accessed=4 * sides * count * width + 6 * width * hidden,
+            transcendentals=sides * count * hidden,
         ),
         name="expert_half",
-    )(rows, scale, gate_weight, up_weight, down_weight)
+    )(*rows, scale, relevance, *weights)
 
 
 def expert_piece(rows, gate_weight, up_weight, down_weight):
@@ -322,71 +389,296 @@
     return (x, y, {0: 1, 3: 2}[z], core) if z in (0, 3) else None
 
 
-def experts_dense(normed, routes, route_weight, gate_weight, up_weight, down_weight):
-    f32 = jnp.float32
-    tok_count = normed.shape[0]
-    req, exp = lax.axis_index("req"), lax.axis_index("exp")
-    z = exp // GRID[0]
-    devices = lax.axis_size("req") * lax.axis_size("exp")
-    experts = devices // 2
+def together(*values):
+    return lax.optimization_barrier(values)
+
+
+def start_tables(routes, route_weight):
+    experts = lax.axis_size("req") * lax.axis_size("exp") // 2
     chosen = routes.T[None] == jnp.arange(experts, dtype=jnp.int32)[:, None, None]
     dense = jnp.sum(jnp.where(chosen, route_weight.T[None], 0.0), axis=1)
-    for target in (z_pair, z_far, over_x, over_y, over_core):
+    for target in (z_pair, z_far):
         dense = jnp.stack([dense, move(dense, target)])
-    own_expert = (req * lax.axis_size("exp") + exp) // 2
+    return dense
+
+
+def finish_tables(dense, doc_len):
+    tok_count = dense.shape[-1]
+    for target in (over_x, over_y, over_core):
+        dense = jnp.stack([dense, move(dense, target)])
+    exp = lax.axis_index("exp")
+    own_expert = (lax.axis_index("req") * lax.axis_size("exp") + exp) // 2
     weights = lax.dynamic_index_in_dim(dense, own_expert, 5, False)
-
-    is_middle = (z == 1) | (z == 2)
-    slot_0 = normed
-    slot_1 = move(slot_0, z_pair)
-    middle = move(slot_0, z_middle)
-    slot_2 = jnp.where(is_middle, move(slot_1, z_middle), move(middle, z_outward))
-    slot_3 = jnp.where(is_middle, middle, move(slot_2, z_outward))
-
-    partials = []
-    for low, near, far in ((0, slot_0, slot_1), (2, slot_2, slot_3)):
-        own = jnp.concatenate([near, far], axis=0)
-        by_x = move(own, over_x)
-        by_y = move(own, over_y)
-        diagonal_near = move(by_x[:tok_count], over_y)
-        diagonal_far = move(by_y[tok_count:], over_x)
-        rows = jnp.concatenate([own, by_x, by_y, diagonal_near, diagonal_far], axis=0)
-        other_rows = move(rows, over_core)
-        results = []
-        for side, held in ((1, other_rows), (0, rows)):
-            scale = weights[side, :, :, low // 2].reshape(-1, 1)
-            results.append(weighted_piece(held, scale, gate_weight, up_weight, down_weight))
-        partials.append(results)
-
-    def total(*terms):
-        result = terms[0].astype(f32)
-        for term in terms[1:]:
-            result = result + term.astype(f32)
-        return result
-
-    def to_wire(value):
-        return value.astype(jnp.bfloat16)
-
-    sums = {}
-    n = tok_count
-    for low, (theirs, mine) in ((2, partials[1]), (0, partials[0])):
-        came = move(theirs, over_core)
-
-        def both(first, last):
-            return total(mine[first * n : last * n], came[first * n : last * n])
-
-        from_y = move(to_wire(both(6, 7)), over_y)
-        from_x = move(to_wire(both(7, 8)), over_x)
-        to_x = jnp.concatenate([to_wire(both(2, 3) + total(from_y)), to_wire(both(3, 4))], axis=0)
-        to_y = jnp.concatenate([to_wire(both(4, 5)), to_wire(both(5, 6) + total(from_x))], axis=0)
-        back_x, back_y = move(to_x, over_x), move(to_y, over_y)
-        own = both(0, 2) + total(back_x) + total(back_y)
-        sums[low], sums[low + 1] = own[:n], own[n:]
-
-    sum_2 = sums[2] + total(move(to_wire(sums[3]), z_inward))
-    sum_3 = sums[3] + total(move(to_wire(sums[2]), z_inward))
-    sum_1 = sums[1] + total(move(to_wire(sum_2), z_middle))
-    return sums[0] + total(move(to_wire(sum_3), z_middle)) + total(move(to_wire(sum_1), z_pair))
+    ends = jnp.cumsum(doc_len, dtype=jnp.int32)
+    bounds = jnp.stack([ends - doc_len, ends])
+    for target in (over_y, over_core):
+        bounds = jnp.stack([bounds, move(bounds, target)])
+    flips = np.array([[[k1 * 4 + k0 * 2 + dx for k0 in (0, 1)] for k1 in (0, 1)] for dx in (0, 1)])
+    blocks = jnp.bitwise_xor(exp, jnp.asarray(flips, jnp.int32))
+    position = blocks[..., None] * tok_count + jnp.arange(tok_count, dtype=jnp.int32)
+    position = position[None, None, ..., None, :]
+
+    def spread(side):
+        return bounds[:, :, side][:, :, None, None, None, :, None]
+
+    return weights, ((position >= spread(0)) & (position < spread(1))).astype(jnp.float32)
+
+
+def hold_kernel(*refs):
+    count = (len(refs) - 1) // 2
+    copies = [
+        pltpu.make_async_copy(refs[at], refs[count + at], refs[-1].at[at]) for at in range(count)
+    ]
+    for copy in copies:
+        copy.start()
+    for copy in copies:
+        copy.wait()
+
+
+def hold(*arrays):
+    return pl.pallas_call(
+        hold_kernel,
+        out_shape=[pltpu.VMEM(array.shape, array.dtype) for array in arrays],
+        in_specs=[pl.BlockSpec(memory_space=pltpu.HBM)] * len(arrays),
+        out_specs=[pl.BlockSpec(memory_space=pltpu.VMEM)] * len(arrays),
+        scratch_shapes=[pltpu.SemaphoreType.DMA((len(arrays),))],
+        compiler_params=pltpu.CompilerParams(vmem_limit_bytes=1024 * 1024),
+        cost_estimate=pl.CostEstimate(
+            flops=0, bytes_accessed=4 * sum(array.size for array in arrays), transcendentals=0
+        ),
+        name="hold_weights",
+    )(*[pltpu.with_memory_space_constraint(array, pltpu.HBM) for array in arrays])
+
+
+def assemble_kernel(plan, *refs):
+    flag_ref, refs = refs[0], refs[1:]
+    outs = refs[sum(len(places) for pieces in plan for _, _, places in pieces) :]
+    at = 0
+    for out_ref, pieces in zip(outs, plan):
+        first = 0
+        for size, pick, places in pieces:
+            held = [refs[at + index][...] for index in range(len(places))]
+            at += len(places)
+            if pick:
+                value = jnp.where(flag_ref[0] == 1, held[0], held[1])
+            else:
+                value = held[0]
+                if len(held) > 1:
+                    value = value.astype(jnp.float32)
+                    for term in held[1:]:
+                        value = value + term.astype(jnp.float32)
+            out_ref[first : first + size] = value.astype(out_ref.dtype)
+            first += size
+
+
+def assemble(flag, *outputs):
+    width = outputs[0][0][2][0][0].shape[1]
+    wide = width // 2
+    operands, specs = [], []
+
+    def block(row):
+        return lambda j: (row, j)
+
+    for pieces in outputs:
+        for size, _, terms in pieces:
+            for array, first in terms:
+                operands.append(array)
+                specs.append(pl.BlockSpec((size, wide), block(first // size)))
+    rows = [sum(size for size, _, _ in pieces) for pieces in outputs]
+    return pl.pallas_call(
+        functools.partial(assemble_kernel, outputs_plan(outputs)),
+        grid=(2,),
+        out_shape=[jax.ShapeDtypeStruct((count, width), jnp.bfloat16) for count in rows],
+        in_specs=[pl.BlockSpec(memory_space=pltpu.SMEM)] + specs,
+        out_specs=[pl.BlockSpec((count, wide), lambda j: (0, j)) for count in rows],
+        compiler_params=pltpu.CompilerParams(vmem_limit_bytes=12 * 1024 * 1024),
+        cost_estimate=pl.CostEstimate(
+            flops=2 * sum(rows) * width, bytes_accessed=8 * sum(rows) * width, transcendentals=0
+        ),
+        name="assemble",
+    )(flag, *operands)
+
+
+def outputs_plan(outputs):
+    return [[(size, pick, [None] * len(terms)) for size, pick, terms in out] for out in outputs]
+
+
+def experts_dense(resid, normed, weights, member, gate_weight, up_weight, down_weight, score_weight):
+    f32 = jnp.float32
+    n = normed.shape[0]
+    h = n // 2
+    z = lax.axis_index("exp") // GRID[0]
+    middle = ((z == 1) | (z == 2)).astype(jnp.int32)[None]
+    rest = jnp.dot(down_weight[0].astype(f32), score_weight, precision=lax.Precision.HIGHEST)
+    terms = []
+    for _ in range(3):
+        terms.append(rest.astype(jnp.bfloat16))
+        rest = rest - terms[-1].astype(f32)
+    relevance = jnp.pad(jnp.stack(terms), ((0, 13), (0, 0)))
+    calls = {
+        "0": [(0, i) for i in range(4)],
+        "p": [(1, i) for i in range(3)],
+        "q": [(2, i) for i in range(3)],
+        "r": [(3, i) for i in range(3)],
+        "e": [(3, 3), (2, 3), (1, 3)],
+    }
+    order = [
+        (name, slot, side, i)
+        for name, blocks in calls.items()
+        for side in (1, 0)
+        for slot, i in blocks
+    ]
+    own_score = jnp.dot(resid.astype(f32), score_weight, precision=lax.Precision.HIGHEST)
+    by_slot = weights.transpose(3, 4, 0, 1, 2, 5).reshape(4, 2, 4, n)
+    scale = jnp.stack([by_slot[slot, side, i] for _, slot, side, i in order])
+    own_sums = jnp.sum(member[0, 0, 0, 0, 0] * own_score[None], axis=1)
+    experts = (gate_weight, up_weight, down_weight)
+    normed, scale, member, relevance = together(normed, scale, member, relevance)
+
+    def join(*blocks):
+        return jnp.concatenate(blocks, axis=0)
+
+    def work(held, name, *rows, side=1):
+        first = [entry[0] for entry in order].index(name) + (1 - side) * len(calls[name])
+        return weighted_pieces(rows, scale, first, relevance, held or experts, bool(held))
+
+    def swap(rows):
+        return move(rows, over_core)
+
+    def keep(size, array, first=0):
+        return (size, False, [(array, first)])
+
+    p, m = move(normed, z_pair), move(normed, z_middle)
+    x0, y0 = move(normed, over_x), move(normed, over_y)
+    p, m, x0, y0, experts = together(p, m, x0, y0, experts)
+    held = hold(*experts)
+
+    to_x, to_y = assemble(
+        middle, [keep(n, p), keep(h, y0, h)], [keep(n, p), keep(h, x0)]
+    )
+    px, py = move(to_x, over_x), move(to_y, over_y)
+    q_middle, q_end = move(p, z_middle), move(m, z_outward)
+    px, py, q_middle, q_end, held = together(px, py, q_middle, q_end, held)
+
+    (q,) = assemble(middle, [(n, True, [(q_middle, 0), (q_end, 0)])])
+    qx, qy = move(q, over_x), move(q, over_y)
+    r_end = move(q, z_outward)
+    d0 = join(py[n:], px[n:])
+    rows_0 = join(normed, x0, y0, d0)
+    out_0 = work(held, "0", swap(rows_0), rows_0)
+    qx, qy, r_end, out_0 = together(qx, qy, r_end, out_0)
+
+    pick = (n, True, [(m, 0), (r_end, 0)])
+    to_x, to_y, r = assemble(middle, [pick, keep(h, qy, h)], [pick, keep(h, qx)], [pick])
+    rx, ry = move(to_x, over_x), move(to_y, over_y)
+    dp = move(d0, z_pair)
+    rows_p = join(p, px[:n], py[:n])
+    rows_q = join(q, qx, qy)
+    other_q = swap(rows_q)
+    out_p = work(held, "p", swap(rows_p), rows_p)
+    out_q = work(held, "q", other_q, rows_q)
+    rx, ry, dp, out_p, out_q = together(rx, ry, dp, out_p, out_q)
+
+    by_x, by_y = move(ry[h:n], over_x), move(rx[:h], over_y)
+    rows_r = join(r, rx[:n], ry[:n])
+    other_r, came_p = swap(rows_r), swap(out_p[0])
+    mine_r = work(held, "r", rows_r, side=0)
+    by_x, by_y, other_r, mine_r, came_p, out_0, out_q = together(
+        by_x, by_y, other_r, mine_r, came_p, out_0, out_q
+    )
+
+    rows_e = join(by_y, by_x, ry[n:], rx[n:], dp)
+    other_e = swap(rows_e)
+    def far(array):
+        return pltpu.with_memory_space_constraint(array, pltpu.HBM)
+
+    def both(size, out, came, first, *more):
+        return (size, False, [(far(out[1]), first), (far(came), first), *more])
+
+    def of_x(out, came, more):
+        return [both(h, out, came, n, more), both(h, out, came, n + h)]
+
+    def of_y(out, came, more):
+        return [both(h, out, came, 2 * n), both(h, out, came, 2 * n + h, more)]
+
+    def own(out, came, *more):
+        return [both(n, out, came, 0, *[(array, 0) for array in more])]
+
+    to_x, to_y = assemble(middle, [both(n, out_p, came_p, n)], [both(n, out_p, came_p, 2 * n)])
+    px, py = move(to_x, over_x), move(to_y, over_y)
+    came_0 = swap(out_0[0])
+    out_e = work(held, "e", other_e, rows_e)
+    came_e = swap(out_e[0])
+    other_r, out_e, px, py = together(other_r, out_e, px, py)
+    theirs_r = work(held, "r", other_r, side=1)
+    out_r = (theirs_r[0], mine_r[0], jnp.concatenate([theirs_r[1], mine_r[1]], axis=0))
+    came_r = swap(theirs_r[0])
+    to_y, to_x = assemble(middle, [both(h, out_e, came_e, 0)], [both(h, out_e, came_e, h)])
+    from_y, from_x = move(to_y, over_y), move(to_x, over_x)
+    outs = {"0": out_0, "p": out_p, "q": out_q, "r": out_r, "e": out_e}
+    rows = join(*[outs[name][2] for name in calls])
+    from_y, from_x, came_0, came_r, out_q, rows = together(
+        from_y, from_x, came_0, came_r, out_q, rows
+    )
+    found = {(slot, side, i): at for at, (_, slot, side, i) in enumerate(order)}
+    scores = jnp.stack(
+        [rows[found[slot, side, i]] for side in (0, 1) for i in range(4) for slot in range(4)]
+    ).reshape(2, 2, 2, 2, 2, n)
+    doc_sums = jnp.sum(member * scores[..., None, :], axis=(2, 3, 4, 6))
+    doc_sums = doc_sums.at[0, 0].add(own_sums)
+    req = lax.axis_index("req")
+    doc_sums = jnp.where(req % 2 == 1, doc_sums[::-1], doc_sums)
+    doc_sums = jnp.where(req // 2 == 1, doc_sums[:, ::-1], doc_sums)
+    doc_sums = jnp.broadcast_to(
+        doc_sums.transpose(1, 0, 2)[:, :, None], (2, 2, lax.axis_size("exp"), doc_sums.shape[2])
+    ).reshape(-1, doc_sums.shape[2])
+    to_x, to_y, to_pair = assemble(
+        middle,
+        of_x(out_r, came_r, (from_y, 0)) + [both(h, out_e, came_e, n + h)],
+        of_y(out_r, came_r, (from_x, 0)) + [both(h, out_e, came_e, n)],
+        [both(n, out_e, came_e, 2 * n)],
+    )
+    rx, ry = move(to_x, over_x), move(to_y, over_y)
+    d_more = move(to_pair, z_pair)
+    came_q = swap(out_q[0])
+    doc_sums = lax.all_to_all(doc_sums, ALL, split_axis=0, concat_axis=0, tiled=True)
+    rx, ry, d_more, doc_sums, came_q = together(rx, ry, d_more, doc_sums, came_q)
+
+    to_x, to_y, sum_r = assemble(
+        middle,
+        of_x(out_q, came_q, (ry, n)),
+        of_y(out_q, came_q, (rx, n)),
+        own(out_r, came_r, rx, ry),
+    )
+    qx, qy = move(to_x, over_x), move(to_y, over_y)
+    q_more = move(sum_r, z_inward)
+    qx, qy, q_more = together(qx, qy, q_more)
+
+    to_x, to_y, sum_q = assemble(
+        middle,
+        [both(h, out_0, came_0, 3 * n + h, (d_more, h))],
+        [both(h, out_0, came_0, 3 * n, (d_more, 0))],
+        own(out_q, came_q, qx, qy, q_more),
+    )
+    d_x, d_y = move(to_x, over_x), move(to_y, over_y)
+    p_more, r_more = move(sum_q, z_middle), move(sum_q, z_inward)
+    d_x, d_y, p_more, r_more = together(d_x, d_y, p_more, r_more)
+
+    to_x, to_y, sum_p, sum_r = assemble(
+        middle,
+        of_x(out_0, came_0, (d_y, 0)),
+        of_y(out_0, came_0, (d_x, 0)),
+        own(out_p, came_p, px, py, p_more),
+        own(out_r, came_r, rx, ry, r_more),
+    )
+    x0, y0 = move(to_x, over_x), move(to_y, over_y)
+    from_p, from_r = move(sum_p, z_pair), move(sum_r, z_middle)
+    (layer_out,) = assemble(middle, own(out_0, came_0, x0, y0, from_p, from_r, resid))
+    return layer_out, jnp.sum(doc_sums, axis=0)
+
+
+def is_small():
+    return (lax.axis_size("req"), lax.axis_size("exp")) == (2 * GRID[1], GRID[0] * GRID[2])
 
 
 def local(
@@ -409,19 +701,35 @@
 ):
     tok_count = hidden_in.shape[0]
     exp_index = lax.axis_index("exp")
-    attn = attention(qkv, q_gain, k_gain, query_pages, page_table, doc_lengths, doc_query)
+    doc_len = doc_lengths[0]
+    tables = start_tables(routes, route_weight) if is_small() else doc_len
+    attn, tables = attention(
+        qkv, q_gain, k_gain, query_pages, page_table, doc_lengths, doc_query, tables
+    )
     attn = attn.transpose(1, 0, 2).reshape(hidden_in.shape)
     mixed = jnp.dot(attn, out_weight, preferred_element_type=jnp.float32)
     resid = (hidden_in.astype(jnp.float32) + mixed).astype(jnp.bfloat16)
     normed = rms_scale(resid.astype(jnp.float32), moe_gain).astype(jnp.bfloat16)
-    is_small = (lax.axis_size("req"), lax.axis_size("exp")) == (2 * GRID[1], GRID[0] * GRID[2])
-    moe = experts_dense if is_small else experts_by_slots
-    combined = moe(normed, routes, route_weight, gate_weight, up_weight, down_weight)
+    if is_small():
+        weights, member = finish_tables(tables, doc_len)
+        layer_out, doc_sums = experts_dense(
+            resid,
+            normed,
+            weights,
+            member,
+            gate_weight,
+            up_weight,
+            down_weight,
+            score_weight,
+        )
+        return (layer_out, (doc_sums / doc_len.astype(jnp.float32))[None, :])
+    combined = experts_by_slots(
+        normed, routes, route_weight, gate_weight, up_weight, down_weight
+    )
     layer_out = (resid.astype(jnp.float32) + combined).astype(jnp.bfloat16)
     token_score = jnp.dot(
         layer_out.astype(jnp.float32), score_weight, precision=lax.Precision.HIGHEST
     )
-    doc_len = doc_lengths[0]
     doc_ends = jnp.cumsum(doc_len, dtype=jnp.int32)
     own_pos = exp_index * tok_count + jnp.arange(tok_count, dtype=jnp.int32)
     member = (own_pos[:, None] < doc_ends[None, :]) & (

time: 406 us -> 292 us (0.72)
  waiting for transfers between devices: 209 us -> 114 us
  blocking collectives: 38.5 us -> 15.5 us
  Pallas kernels: 54.2 us -> 73.5 us
  other arithmetic: 20.5 us -> 4.56 us
  local copies, waits for them, and re-layouts: 21.4 us -> 6.83 us
  starting transfers between devices: 54.8 us -> 66.1 us
    ppermute x35 -> x51, waiting for transfers between devices: 172 us -> 105 us  [move(): return lax.ppermute(block, ALL, pairs(target))]
    all_to_all x1, waiting for transfers between devices: 36.9 us -> 0.01 us  [attention(): lax.all_to_all(parts, 'exp', split_axis=0, concat_axis=0, tiled=True)]
    psum x1 -> x0, blocking collectives: 20.4 us -> none  [local(): doc_sums = lax.psum(doc_partial, 'exp')]
    pallas_call x5 -> x18, Pallas kernels: 42.7 us -> 62 us  [the longest x6 39.8 us: weighted_pieces(): pl.pallas_call(functools.partial(expert_kernel, sides, steps, first, held...]
    unnamed x49 -> x45, local copies, waits for them, and re-layouts: 18 us -> 4.97 us
    convert_element_type x9 -> x4, other arithmetic: 12.8 us -> 1.16 us  [the longest x1 0.95 us: finish_tables(): ((position >= spread(0)) & (position < spread(1))).astype(jnp.float32)]
    all_to_all x0 -> x1, waiting for transfers between devices: none -> 9.21 us  [attention(): back = lax.all_to_all(out, 'exp', split_axis=0, concat_axis=0, tiled=True)]
    ppermute x35 -> x51, starting transfers between devices: 47.5 us -> 55.2 us  [move(): return lax.ppermute(block, ALL, pairs(target))]
  transfers between devices with their start and end apart: 36 -> 53, of which waited for: 21 -> 30; matrix products, arithmetic and copies ran while one was open for 6% -> 3% of each run, Pallas kernels for 9% -> 21%
where the time goes in v3:
time: 292 us; the launch traced here: 291 us
  waiting for transfers between devices  114 us (39%)
  Pallas kernels  73.5 us (25%)
  starting transfers between devices  66.1 us (23%)
  blocking collectives  15.5 us (5%)
  matrix products  8.6 us (3%)
  local copies, waits for them, and re-layouts  6.83 us (2%)
  other arithmetic  4.56 us (2%)
    ppermute x51, waiting for transfers between devices, move(): return lax.ppermute(block, ALL, pairs(target))  105 us
    ppermute x51, starting transfers between devices, move(): return lax.ppermute(block, ALL, pairs(target))  55.2 us
    pallas_call x6, Pallas kernels, weighted_pieces(): pl.pallas_call(functools.partial(expert_kernel, sides, steps, first, held...  39.8 us
    pallas_call x10, Pallas kernels, assemble(): pl.pallas_call(functools.partial(assemble_kernel, outputs_plan(outputs)),...  18 us
    all_to_all x1, blocking collectives, experts_dense(): lax.all_to_all(doc_sums, ALL, split_axis=0, concat_axis=0, tiled=True)  15.5 us
    pallas_call x1, Pallas kernels, attention(): pl.pallas_call(attention_kernel, out_shape=jax.ShapeDtypeStruct((tokens,...  11.6 us
    all_to_all x1, waiting for transfers between devices, attention(): back = lax.all_to_all(out, 'exp', split_axis=0, concat_axis=0, tiled=True)  9.21 us
    all_to_all x1, starting transfers between devices, attention(): lax.all_to_all(parts, 'exp', split_axis=0, concat_axis=0, tiled=True)  7.4 us
  transfers between devices with their start and end apart: 53, of which 30 were waited for; matrix products, arithmetic and copies ran while one was open for 3% of the time, Pallas kernels for 21%

profile of v3, /device:TPU:0, one launch (start us, length us, event | category | flops | bytes accessed | tf_op | source)
XLA Modules:
  0.0 290.9 jit_solution(2288463561866406995)
XLA Ops:
  3.3 7.4 %all-to-all-start = ((bf16[8,128,768]{2,1,0:T(8,128)(2,1)}), bf16[8,128,768]{2,1,0:T(8,128)(2,1)S(1)}, u32[]{:S(2)}, u32[]{:S(2)}) async-start(bf16[8,128,768]{2,1,0:T(8,128)(2,1)} %bitcast.1), calls=%async_computation | async-start | bytes 3145728 | tf_op jit(solution)/shard_map/all_to_all | solution.py:160
  10.8 2.1 collective-permute-start
  13.1 1.6 collective-permute-start.5
  14.8 3.3 %fusion.1 = f32[1,512]{1,0:T(1,128)S(1)} fusion(f32[2048,1]{0,1:T(1,128)S(1)} %bitcast.195, bf16[1,512,2048]{2,1,0:T(8,128)(2,1)} %refs_2_), kind=kOutput, calls=%fused_computation.2 | convolution fusion | flops 12582912 | bytes 2107392 | tf_op jit(solution)/shard_map/dot_general | solution.py:512
  18.2 19.0 %collective-permute-done = f32[16,128]{1,0:T(8,128)S(1)} collective-permute-done((f32[16,128]{1,0:T(8,128)S(1)}, f32[16,128]{1,0:T(8,128)S(1)}, u32[]{:S(2)}, u32[]{:S(2)}) %collective-permute-start) | collective-permute-done | bytes 8224 | tf_op jit(solution)/shard_map/ppermute | solution.py:357
  37.1 3.9 %collective-permute-start.1 = (f32[2,16,128]{2,1,0:T(8,128)S(1)}, f32[2,16,128]{2,1,0:T(8,128)S(1)}, u32[]{:S(2)}, u32[]{:S(2)}) collective-permute-start(f32[2,16,128]{2,1,0:T(8,128)S(1)} %get-tuple-element.311), channel_id=1, source_target_pairs={{0,4},{1,5},{2,6},{3,7},{4,0},{5,1},{6,2},{7,3},{8,12},{9,13},{10,... | collective-permute-start | bytes 49160 | tf_op jit(solution)/shard_map/ppermute | solution.py:357
  41.2 7.2 %collective-permute-done.1 = f32[2,16,128]{2,1,0:T(8,128)S(1)} collective-permute-done((f32[2,16,128]{2,1,0:T(8,128)S(1)}, f32[2,16,128]{2,1,0:T(8,128)S(1)}, u32[]{:S(2)}, u32[]{:S(2)}) %collective-permute-start.1) | collective-permute-done | bytes 16416 | tf_op jit(solution)/shard_map/ppermute | solution.py:357
  48.5 11.6 %paged_attention.1 = bf16[1024,256]{1,0:T(8,128)(2,1)S(1)} custom-call(bf16[1024,768]{1,0:T(8,128)(2,1)S(1)} %bitcast.197, bf16[1024,512]{1,0:T(8,128)(2,1)S(1)} %bitcast.199, s32[1,128]{1,0:T(1,128)S(1)} %pad.14.len_ref, s32[1,128]{1,0:T(1,128)S(1)} %pad.15.query_ref, s32[8,1]{1,0:T(8,128)S(1)} %copy.46.table_ref, f32[1,128]{1,0:T(1,128)S(1)} %bitcast.200, ...), custom_call_target="tpu_custom_call" | custom-call | tf_op jit(solution)/shard_map/paged_attention/pallas_call | solution.py:163
  62.6 3.5 %all-to-all-start.1 = ((bf16[8,128,256]{1,2,0:T(8,128)(2,1)}), bf16[8,128,256]{1,2,0:T(8,128)(2,1)S(1)}, u32[]{:S(2)}, u32[]{:S(2)}) async-start(bf16[8,128,256]{1,2,0:T(8,128)(2,1)} %copy.47), calls=%async_computation.1 | async-start | bytes 1048576 | tf_op jit(solution)/shard_map/all_to_all | solution.py:183
  66.2 1.6 collective-permute-start.3
  67.8 3.0 %collective-permute-done.3 = f32[2,2,2,16,128]{4,3,2,1,0:T(8,128)S(1)} collective-permute-done((f32[2,2,2,16,128]{4,3,2,1,0:T(8,128)S(1)}, f32[2,2,2,16,128]{4,3,2,1,0:T(8,128)S(1)}, u32[]{:S(2)}, u32[]{:S(2)}) %collective-permute-start.3) | collective-permute-done | bytes 65568 | tf_op jit(solution)/shard_map/ppermute | solution.py:357
  72.3 9.2 %all-to-all-done.1 = bf16[8,128,256]{1,2,0:T(8,128)(2,1)S(1)} async-done(((bf16[8,128,256]{1,2,0:T(8,128)(2,1)}), bf16[8,128,256]{1,2,0:T(8,128)(2,1)S(1)}, u32[]{:S(2)}, u32[]{:S(2)}) %all-to-all-start.1) | async-done | bytes 524320 | tf_op jit(solution)/shard_map/all_to_all | solution.py:183
  81.5 4.8 %fusion.3 = (f32[128]{0:T(128)S(1)}, bf16[128,2048]{1,0:T(8,128)(2,1)S(1)}) fusion(bf16[128,2048]{0,1:T(8,128)(2,1)S(1)} %bitcast.202, bf16[2048,2048]{1,0:T(8,128)(2,1)} %param.28, bf16[128,2048]{1,0:T(8,128)(2,1)S(1)} %copy-done.10), kind=kOutput, calls=%fused_computation.10 | convolution fusion | flops 1075314560 | bytes 9961984 | tf_op jit(solution)/shard_map/dot_general | solution.py:710
  88.8 1.5 collective-permute-start.10
  90.3 9.8 %collective-permute-done.7.refs_1_.refs_3_ = bf16[128,2048]{1,0:T(8,128)(2,1)S(1)} collective-permute-done((bf16[128,2048]{1,0:T(8,128)(2,1)S(1)}, bf16[128,2048]{1,0:T(8,128)(2,1)S(1)}, u32[]{:S(2)}, u32[]{:S(2)}) %collective-permute-start.7) | collective-permute-done | bytes 524320 | tf_op jit(solution)/shard_map/ppermute | solution.py:357
  103.1 1.5 collective-permute-start.12
  106.7 2.9 hold_weights.1
  109.6 12.0 %collective-permute-done.14.refs_2_ = bf16[128,2048]{1,0:T(8,128)(2,1)S(1)} collective-permute-done((bf16[128,2048]{1,0:T(8,128)(2,1)S(1)}, bf16[128,2048]{1,0:T(8,128)(2,1)S(1)}, u32[]{:S(2)}, u32[]{:S(2)}) %collective-permute-start.14) | collective-permute-done | bytes 524320 | tf_op jit(solution)/shard_map/ppermute | solution.py:357
  126.0 9.4 %expert_half.6 = (bf16[512,2048]{1,0:T(8,128)(2,1)}, bf16[512,2048]{1,0:T(8,128)(2,1)}, f32[8,128]{1,0:T(8,128)S(1)}) custom-call(bf16[512,2048]{1,0:T(8,128)(2,1)S(1)} %collective-permute-done.18.refs_0_, bf16[512,2048]{1,0:T(8,128)(2,1)S(1)} %get-tuple-element.241.refs_1_, f32[32,128]{1,0:T(8,128)S(1)} %stack.101.refs_2_.refs_1_, ...), custom_call_target="tpu_custom_call" | custom-call | flops 6442450944 | bytes 14680064 | tf_op jit(solution)/shard_map/expert_half/pallas_call | solution.py:266
  137.6 3.3 %collective-permute-done.17.refs_2_.refs_5_.refs_8_ = bf16[128,2048]{1,0:T(8,128)(2,1)S(1)} collective-permute-done((bf16[128,2048]{1,0:T(8,128)(2,1)S(1)}, bf16[128,2048]{1,0:T(8,128)(2,1)S(1)}, u32[]{:S(2)}, u32[]{:S(2)}) %collective-permute-start.17) | collective-permute-done | bytes 524320 | tf_op jit(solution)/shard_map/ppermute | solution.py:357
  143.3 7.5 %expert_half.7 = (bf16[384,2048]{1,0:T(8,128)(2,1)}, bf16[384,2048]{1,0:T(8,128)(2,1)}, f32[6,128]{1,0:T(8,128)S(1)}) custom-call(bf16[384,2048]{1,0:T(8,128)(2,1)S(1)} %collective-permute-done.22.refs_0_, bf16[384,2048]{1,0:T(8,128)(2,1)S(1)} %pad_maximum_fusion.refs_1_, f32[32,128]{1,0:T(8,128)S(1)} %stack.101.refs_2_.refs_1_, ...), custom_call_target="tpu_custom_call" | custom-call | flops 4831838208 | bytes 12582912 | tf_op jit(solution)/shard_map/expert_half/pallas_call | solution.py:266
  150.8 7.4 %expert_half.8 = (bf16[384,2048]{1,0:T(8,128)(2,1)}, bf16[384,2048]{1,0:T(8,128)(2,1)}, f32[6,128]{1,0:T(8,128)S(1)}) custom-call(bf16[384,2048]{1,0:T(8,128)(2,1)S(1)} %collective-permute-done.23.refs_0_, bf16[384,2048]{1,0:T(8,128)(2,1)S(1)} %pad_maximum_fusion.1.refs_1_, f32[32,128]{1,0:T(8,128)S(1)} %stack.101.refs_2_.refs_1_, ...), custom_call_target="tpu_custom_call" | custom-call | flops 4831838208 | bytes 12582912 | tf_op jit(solution)/shard_map/expert_half/pallas_call | solution.py:266
  158.2 3.7 %collective-permute-done.19 = bf16[192,2048]{1,0:T(8,128)(2,1)S(1)} collective-permute-done((bf16[192,2048]{1,0:T(8,128)(2,1)S(1)}, bf16[192,2048]{1,0:T(8,128)(2,1)S(1)}, u32[]{:S(2)}, u32[]{:S(2)}) %collective-permute-start.19) | collective-permute-done | bytes 786464 | tf_op jit(solution)/shard_map/ppermute | solution.py:357
  163.8 1.5 collective-permute-start.24
  165.8 4.0 %expert_half.9 = (bf16[384,2048]{1,0:T(8,128)(2,1)}, f32[3,128]{1,0:T(4,128)S(1)}) custom-call(bf16[384,2048]{1,0:T(8,128)(2,1)S(1)} %pad_maximum_fusion.2.refs_0_, f32[32,128]{1,0:T(8,128)S(1)} %stack.101.refs_2_.refs_1_, bf16[16,512]{1,0:T(8,128)(2,1)S(1)} %fusion.11.refs_3_.refs_2_, bf16[1,2048,512]{2,1,0:T(8,128)(2,1)S(1)} %get-tuple-element.147.refs_4_.refs_3_, ...), custom_call_target="tpu_custom_call" | custom-call | flops 2415919104 | bytes 9437184 | tf_op jit(solution)/shard_map/expert_half/pallas_call | solution.py:266
  169.8 2.8 collective-permute-done.24
  174.9 1.7 assemble.13
  178.3 7.4 %expert_half.10 = (bf16[384,2048]{1,0:T(8,128)(2,1)}, bf16[384,2048]{1,0:T(8,128)(2,1)}, f32[6,128]{1,0:T(8,128)S(1)}) custom-call(bf16[384,2048]{1,0:T(8,128)(2,1)S(1)} %collective-permute-done.28.refs_0_, bf16[384,2048]{1,0:T(8,128)(2,1)S(1)} %constant_dynamic-update-slice_fusion.5.refs_1_, f32[32,128]{1,0:T(8,128)S(1)} %stack.101.refs_2_.refs_1_, ...), custom_call_target="tpu_custom_call" | custom-call | flops 4831838208 | bytes 12582912 | tf_op jit(solution)/shard_map/expert_half/pallas_call | solution.py:266
  185.9 5.1 %collective-permute-done.29.refs_13_ = bf16[128,2048]{1,0:T(8,128)(2,1)S(1)} collective-permute-done((bf16[128,2048]{1,0:T(8,128)(2,1)S(1)}, bf16[128,2048]{1,0:T(8,128)(2,1)S(1)}, u32[]{:S(2)}, u32[]{:S(2)}) %collective-permute-start.29) | collective-permute-done | bytes 524320 | tf_op jit(solution)/shard_map/ppermute | solution.py:357
  191.3 4.0 %expert_half.11 = (bf16[384,2048]{1,0:T(8,128)(2,1)}, f32[3,128]{1,0:T(4,128)S(1)}) custom-call(bf16[384,2048]{1,0:T(8,128)(2,1)S(1)} %collective-permute-done.26.refs_0_, f32[32,128]{1,0:T(8,128)S(1)} %stack.101.refs_2_.refs_1_, bf16[16,512]{1,0:T(8,128)(2,1)S(1)} %fusion.11.refs_3_.refs_2_, bf16[1,2048,512]{2,1,0:T(8,128)(2,1)S(1)} %get-tuple-element.147.refs_4_.refs_3_, ...), custom_call_target="tpu_custom_call" | custom-call | flops 2415919104 | bytes 9437184 | tf_op jit(solution)/shard_map/expert_half/pallas_call | solution.py:266
  200.0 6.6 %collective-permute-done.32.refs_3_ = bf16[64,2048]{1,0:T(8,128)(2,1)S(1)} collective-permute-done((bf16[64,2048]{1,0:T(8,128)(2,1)S(1)}, bf16[64,2048]{1,0:T(8,128)(2,1)S(1)}, u32[]{:S(2)}, u32[]{:S(2)}) %collective-permute-start.32) | collective-permute-done | bytes 262176 | tf_op jit(solution)/shard_map/ppermute | solution.py:357
  208.2 3.5 %assemble.15 = (bf16[192,2048]{1,0:T(8,128)(2,1)}, bf16[192,2048]{1,0:T(8,128)(2,1)}, bf16[128,2048]{1,0:T(8,128)(2,1)}) custom-call(s32[1]{0:T(128)} %bitcast.refs_0_, bf16[384,2048]{1,0:T(8,128)(2,1)} %get-tuple-element.203.refs_1_.refs_4_.refs_8_.refs_10_.refs_11_.refs_16_, ...), custom_call_target="tpu_custom_call" | custom-call | flops 2097152 | bytes 8388608 | tf_op jit(solution)/shard_map/assemble/pallas_call | solution.py:488
  211.6 1.5 collective-permute-start.36
  214.7 1.7 collective-permute-start.38
  217.8 15.5 %all_to_all.32 = f32[32,1,32]{2,1,0:T(1,128)S(1)} all-to-all(f32[32,1,32]{2,1,0:T(1,128)S(1)} %bitcast.209), channel_id=1, replica_groups=mesh['req'=4,'exp'=8] {'req','exp'}, dimensions={0} | all-to-all | bytes 8192 | tf_op jit(solution)/shard_map/all_to_all | solution.py:644
  233.3 2.3 assemble.16
  237.8 3.8 %collective-permute-start.42 = (bf16[128,2048]{1,0:T(8,128)(2,1)S(1)}, bf16[128,2048]{1,0:T(8,128)(2,1)S(1)}, u32[]{:S(2)}, u32[]{:S(2)}) collective-permute-start(bf16[128,2048]{1,0:T(8,128)(2,1)S(1)} %get-tuple-element.220), channel_id=1, source_target_pairs={{0,2},{1,3},{6,4},{7,5},{8,10},{9,11},{14,12},{15,13},{16,18},{17,... | collective-permute-start | bytes 1572872 | tf_op jit(solution)/shard_map/ppermute | solution.py:357
  241.6 8.0 %collective-permute-done.40.refs_9_ = bf16[128,2048]{1,0:T(8,128)(2,1)S(1)} collective-permute-done((bf16[128,2048]{1,0:T(8,128)(2,1)S(1)}, bf16[128,2048]{1,0:T(8,128)(2,1)S(1)}, u32[]{:S(2)}, u32[]{:S(2)}) %collective-permute-start.40) | collective-permute-done | bytes 524320 | tf_op jit(solution)/shard_map/ppermute | solution.py:357
  250.2 2.1 collective-permute-done.42.refs_11_
  252.3 2.0 assemble.17
  255.0 6.4 %collective-permute-start.46 = (bf16[128,2048]{1,0:T(8,128)(2,1)S(1)}, bf16[128,2048]{1,0:T(8,128)(2,1)S(1)}, u32[]{:S(2)}, u32[]{:S(2)}) collective-permute-start(bf16[128,2048]{1,0:T(8,128)(2,1)S(1)} %get-tuple-element.226), channel_id=1, source_target_pairs={{0,2},{1,3},{6,4},{7,5},{8,10},{9,11},{14,12},{15,13},{16,18},{17,... | collective-permute-start | bytes 1572872 | tf_op jit(solution)/shard_map/ppermute | solution.py:357
  263.8 4.0 %collective-permute-done.43.refs_10_ = bf16[64,2048]{1,0:T(8,128)(2,1)S(1)} collective-permute-done((bf16[64,2048]{1,0:T(8,128)(2,1)S(1)}, bf16[64,2048]{1,0:T(8,128)(2,1)S(1)}, u32[]{:S(2)}, u32[]{:S(2)}) %collective-permute-start.43) | collective-permute-done | bytes 262176 | tf_op jit(solution)/shard_map/ppermute | solution.py:357
  269.3 1.7 collective-permute-done.46.refs_20_
  270.9 3.7 %assemble.18 = (bf16[128,2048]{1,0:T(8,128)(2,1)}, bf16[128,2048]{1,0:T(8,128)(2,1)}, bf16[128,2048]{1,0:T(8,128)(2,1)}, bf16[128,2048]{1,0:T(8,128)(2,1)}) custom-call(s32[1]{0:T(128)} %bitcast.refs_0_, bf16[512,2048]{1,0:T(8,128)(2,1)} %get-tuple-element.176.refs_1_.refs_4_.refs_6_.refs_8_, ...), custom_call_target="tpu_custom_call" | custom-call | flops 2097152 | bytes 8388608 | tf_op jit(solution)/shard_map/assemble/pallas_call | solution.py:488
  274.6 1.5 collective-permute-start.47
  277.1 2.5 collective-permute-start.49
  280.8 5.2 %collective-permute-done.47.refs_3_ = bf16[128,2048]{1,0:T(8,128)(2,1)S(1)} collective-permute-done((bf16[128,2048]{1,0:T(8,128)(2,1)}, bf16[128,2048]{1,0:T(8,128)(2,1)S(1)}, u32[]{:S(2)}, u32[]{:S(2)}) %collective-permute-start.47) | collective-permute-done | bytes 524320 | tf_op jit(solution)/shard_map/ppermute | solution.py:357
  288.7 2.2 assemble.19
  (183 shorter events, 51.9 us)
Async XLA Ops:
  3.3 45.1 %all-to-all-start = ((bf16[8,128,768]{2,1,0:T(8,128)(2,1)}), bf16[8,128,768]{2,1,0:T(8,128)(2,1)S(1)}, u32[]{:S(2)}, u32[]{:S(2)}) async-start(bf16[8,128,768]{2,1,0:T(8,128)(2,1)} %bitcast.1), calls=%async_computation | async-start | bytes 3145728 | tf_op jit(solution)/shard_map/all_to_all | solution.py:160
  10.8 26.3 %collective-permute-start = (f32[16,128]{1,0:T(8,128)S(1)}, f32[16,128]{1,0:T(8,128)S(1)}, u32[]{:S(2)}, u32[]{:S(2)}) collective-permute-start(f32[16,128]{1,0:T(8,128)S(1)} %select_reduce_fusion), channel_id=1, source_target_pairs={{0,2},{1,3},{2,0},{3,1},{4,6},{5,7},{6,4},{7,5},{8,10},{9,11},{10,... | collective-permute-start | bytes 24584 | tf_op jit(solution)/shard_map/ppermute | solution.py:357
  13.1 48.4 %collective-permute-start.5 = (s32[2,32]{1,0:T(2,128)S(1)}, s32[2,32]{1,0:T(2,128)S(1)}, u32[]{:S(2)}, u32[]{:S(2)}) collective-permute-start(s32[2,32]{1,0:T(2,128)S(1)} %get-tuple-element.319), channel_id=1, source_target_pairs={{0,16},{1,17},{2,18},{3,19},{4,20},{5,21},{6,22},{7,23},{8,24},{9,... | collective-permute-start | bytes 776 | tf_op jit(solution)/shard_map/ppermute | solution.py:357
  37.1 11.3 %collective-permute-start.1 = (f32[2,16,128]{2,1,0:T(8,128)S(1)}, f32[2,16,128]{2,1,0:T(8,128)S(1)}, u32[]{:S(2)}, u32[]{:S(2)}) collective-permute-start(f32[2,16,128]{2,1,0:T(8,128)S(1)} %get-tuple-element.311), channel_id=1, source_target_pairs={{0,4},{1,5},{2,6},{3,7},{4,0},{5,1},{6,2},{7,3},{8,12},{9,13},{10,... | collective-permute-start | bytes 49160 | tf_op jit(solution)/shard_map/ppermute | solution.py:357
  60.0 6.1 %collective-permute-start.2 = (f32[2,2,16,128]{3,2,1,0:T(8,128)S(1)}, f32[2,2,16,128]{3,2,1,0:T(8,128)S(1)}, u32[]{:S(2)}, u32[]{:S(2)}) collective-permute-start(f32[2,2,16,128]{3,2,1,0:T(8,128)S(1)} %pad_maximum_fusion.6), channel_id=1, source_target_pairs={{0,1},{1,0},{2,3},{3,2},{4,5},{5,4},{6,7},{7,6},{8,9},{9,8},{10,11... | collective-permute-start | bytes 98312 | tf_op jit(solution)/shard_map/ppermute | solution.py:357
  61.5 6.2 %collective-permute-start.6 = (s32[2,2,32]{2,1,0:T(2,128)S(1)}, s32[2,2,32]{2,1,0:T(2,128)S(1)}, u32[]{:S(2)}, u32[]{:S(2)}) collective-permute-start(s32[2,2,32]{2,1,0:T(2,128)S(1)} %get-tuple-element.317), channel_id=1, source_target_pairs={{0,8},{1,9},{2,10},{3,11},{4,12},{5,13},{6,14},{7,15},{8,0},{9,1},... | collective-permute-start | bytes 1544 | tf_op jit(solution)/shard_map/ppermute | solution.py:357
  62.6 18.9 %all-to-all-start.1 = ((bf16[8,128,256]{1,2,0:T(8,128)(2,1)}), bf16[8,128,256]{1,2,0:T(8,128)(2,1)S(1)}, u32[]{:S(2)}, u32[]{:S(2)}) async-start(bf16[8,128,256]{1,2,0:T(8,128)(2,1)} %copy.47), calls=%async_computation.1 | async-start | bytes 1048576 | tf_op jit(solution)/shard_map/all_to_all | solution.py:183
  86.5 13.6 %collective-permute-start.7 = (bf16[128,2048]{1,0:T(8,128)(2,1)S(1)}, bf16[128,2048]{1,0:T(8,128)(2,1)S(1)}, u32[]{:S(2)}, u32[]{:S(2)}) collective-permute-start(bf16[128,2048]{1,0:T(8,128)(2,1)S(1)} %fusion.5), channel_id=1, source_target_pairs={{0,2},{1,3},{2,0},{3,1},{4,6},{5,7},{6,4},{7,5},{8,10},{9,11},{10,... | collective-permute-start | bytes 1572872 | tf_op jit(solution)/shard_map/ppermute | solution.py:357
  87.0 13.1 %collective-permute-start.8 = (bf16[128,2048]{1,0:T(8,128)(2,1)S(1)}, bf16[128,2048]{1,0:T(8,128)(2,1)S(1)}, u32[]{:S(2)}, u32[]{:S(2)}) collective-permute-start(bf16[128,2048]{1,0:T(8,128)(2,1)S(1)} %fusion.5), channel_id=1, source_target_pairs={{2,4},{3,5},{4,2},{5,3},{10,12},{11,13},{12,10},{13,11},{18,20},{1... | collective-permute-start | bytes 1572872 | tf_op jit(solution)/shard_map/ppermute | solution.py:357
  87.7 13.2 %collective-permute-start.9 = (bf16[128,2048]{1,0:T(8,128)(2,1)S(1)}, bf16[128,2048]{1,0:T(8,128)(2,1)S(1)}, u32[]{:S(2)}, u32[]{:S(2)}) collective-permute-start(bf16[128,2048]{1,0:T(8,128)(2,1)S(1)} %fusion.5), channel_id=1, source_target_pairs={{0,1},{1,0},{2,3},{3,2},{4,5},{5,4},{6,7},{7,6},{8,9},{9,8},{10,11... | collective-permute-start | bytes 1572872 | tf_op jit(solution)/shard_map/ppermute | solution.py:357
  88.8 13.3 %collective-permute-start.10 = (bf16[128,2048]{1,0:T(8,128)(2,1)S(1)}, bf16[128,2048]{1,0:T(8,128)(2,1)S(1)}, u32[]{:S(2)}, u32[]{:S(2)}) collective-permute-start(bf16[128,2048]{1,0:T(8,128)(2,1)S(1)} %fusion.5), channel_id=1, source_target_pairs={{0,16},{1,17},{2,18},{3,19},{4,20},{5,21},{6,22},{7,23},{8,24},{9,... | collective-permute-start | bytes 1572872 | tf_op jit(solution)/shard_map/ppermute | solution.py:357
  102.4 19.2 %collective-permute-start.11 = (bf16[192,2048]{1,0:T(8,128)(2,1)S(1)}, bf16[192,2048]{1,0:T(8,128)(2,1)S(1)}, u32[]{:S(2)}, u32[]{:S(2)}) collective-permute-start(bf16[192,2048]{1,0:T(8,128)(2,1)S(1)} %get-tuple-element.133), channel_id=1, source_target_pairs={{0,1},{1,0},{2,3},{3,2},{4,5},{5,4},{6,7},{7,6},{8,9},{9,8},{10,11... | collective-permute-start | bytes 2359304 | tf_op jit(solution)/shard_map/ppermute | solution.py:357
  103.1 18.6 %collective-permute-start.12 = (bf16[192,2048]{1,0:T(8,128)(2,1)S(1)}, bf16[192,2048]{1,0:T(8,128)(2,1)S(1)}, u32[]{:S(2)}, u32[]{:S(2)}) collective-permute-start(bf16[192,2048]{1,0:T(8,128)(2,1)S(1)} %get-tuple-element.134), channel_id=1, source_target_pairs={{0,16},{1,17},{2,18},{3,19},{4,20},{5,21},{6,22},{7,23},{8,24},{9,... | collective-permute-start | bytes 2359304 | tf_op jit(solution)/shard_map/ppermute | solution.py:357
  104.6 5.0 %collective-permute-start.13 = (bf16[128,2048]{1,0:T(8,128)(2,1)S(1)}, bf16[128,2048]{1,0:T(8,128)(2,1)S(1)}, u32[]{:S(2)}, u32[]{:S(2)}) collective-permute-start(bf16[128,2048]{1,0:T(8,128)(2,1)S(1)} %collective-permute-done.7.refs_1_.refs_3_), channel_id=1, source_target_pairs={{2,4},{3,5},{4,2},{5,3},{10,12},{11,13},{12,10},{13,11},{18,20},{1... | collective-permute-start | bytes 1572872 | tf_op jit(solution)/shard_map/ppermute | solution.py:357
  105.3 16.4 %collective-permute-start.14 = (bf16[128,2048]{1,0:T(8,128)(2,1)S(1)}, bf16[128,2048]{1,0:T(8,128)(2,1)S(1)}, u32[]{:S(2)}, u32[]{:S(2)}) collective-permute-start(bf16[128,2048]{1,0:T(8,128)(2,1)S(1)} %collective-permute-done.8.refs_1_.refs_4_.refs_7_), channel_id=1, source_target_pairs={{2,0},{3,1},{4,6},{5,7},{10,8},{11,9},{12,14},{13,15},{18,16},{19,... | collective-permute-start | bytes 1572872 | tf_op jit(solution)/shard_map/ppermute | solution.py:357
  122.1 14.4 %collective-permute-start.15 = (bf16[128,2048]{1,0:T(8,128)(2,1)S(1)}, bf16[128,2048]{1,0:T(8,128)(2,1)S(1)}, u32[]{:S(2)}, u32[]{:S(2)}) collective-permute-start(bf16[128,2048]{1,0:T(8,128)(2,1)S(1)} %assemble.11), channel_id=1, source_target_pairs={{0,1},{1,0},{2,3},{3,2},{4,5},{5,4},{6,7},{7,6},{8,9},{9,8},{10,11... | collective-permute-start | bytes 1572872 | tf_op jit(solution)/shard_map/ppermute | solution.py:357
  123.6 14.0 %collective-permute-start.16 = (bf16[128,2048]{1,0:T(8,128)(2,1)S(1)}, bf16[128,2048]{1,0:T(8,128)(2,1)S(1)}, u32[]{:S(2)}, u32[]{:S(2)}) collective-permute-start(bf16[128,2048]{1,0:T(8,128)(2,1)S(1)} %assemble.11), channel_id=1, source_target_pairs={{0,16},{1,17},{2,18},{3,19},{4,20},{5,21},{6,22},{7,23},{8,24},{9,... | collective-permute-start | bytes 1572872 | tf_op jit(solution)/shard_map/ppermute | solution.py:357
  124.2 16.7 %collective-permute-start.17 = (bf16[128,2048]{1,0:T(8,128)(2,1)S(1)}, bf16[128,2048]{1,0:T(8,128)(2,1)S(1)}, u32[]{:S(2)}, u32[]{:S(2)}) collective-permute-start(bf16[128,2048]{1,0:T(8,128)(2,1)S(1)} %assemble.11), channel_id=1, source_target_pairs={{2,0},{3,1},{4,6},{5,7},{10,8},{11,9},{12,14},{13,15},{18,16},{19,... | collective-permute-start | bytes 1572872 | tf_op jit(solution)/shard_map/ppermute | solution.py:357
  125.9 17.4 %collective-permute-start.22 = (bf16[384,2048]{1,0:T(8,128)(2,1)S(1)}, bf16[384,2048]{1,0:T(8,128)(2,1)S(1)}, u32[]{:S(2)}, u32[]{:S(2)}) collective-permute-start(bf16[384,2048]{1,0:T(8,128)(2,1)S(1)} %pad_maximum_fusion.refs_1_), channel_id=1, source_target_pairs={{0,8},{1,9},{2,10},{3,11},{4,12},{5,13},{6,14},{7,15},{8,0},{9,1},... | collective-permute-start | bytes 4718600 | tf_op jit(solution)/shard_map/ppermute | solution.py:357
  141.0 9.8 %collective-permute-start.23 = (bf16[384,2048]{1,0:T(8,128)(2,1)S(1)}, bf16[384,2048]{1,0:T(8,128)(2,1)S(1)}, u32[]{:S(2)}, u32[]{:S(2)}) collective-permute-start(bf16[384,2048]{1,0:T(8,128)(2,1)S(1)} %pad_maximum_fusion.1.refs_1_), channel_id=1, source_target_pairs={{0,8},{1,9},{2,10},{3,11},{4,12},{5,13},{6,14},{7,15},{8,0},{9,1},... | collective-permute-start | bytes 4718600 | tf_op jit(solution)/shard_map/ppermute | solution.py:357
  141.2 17.0 %collective-permute-start.21 = (bf16[128,2048]{1,0:T(8,128)(2,1)S(1)}, bf16[128,2048]{1,0:T(8,128)(2,1)S(1)}, u32[]{:S(2)}, u32[]{:S(2)}) collective-permute-start(bf16[128,2048]{1,0:T(8,128)(2,1)S(1)} %pad_maximum_fusion.3), channel_id=1, source_target_pairs={{0,2},{1,3},{2,0},{3,1},{4,6},{5,7},{6,4},{7,5},{8,10},{9,11},{10,... | collective-permute-start | bytes 1572872 | tf_op jit(solution)/shard_map/ppermute | solution.py:357
  141.9 20.0 %collective-permute-start.19 = (bf16[192,2048]{1,0:T(8,128)(2,1)S(1)}, bf16[192,2048]{1,0:T(8,128)(2,1)S(1)}, u32[]{:S(2)}, u32[]{:S(2)}) collective-permute-start(bf16[192,2048]{1,0:T(8,128)(2,1)S(1)} %get-tuple-element.156), channel_id=1, source_target_pairs={{0,1},{1,0},{2,3},{3,2},{4,5},{5,4},{6,7},{7,6},{8,9},{9,8},{10,11... | collective-permute-start | bytes 2359304 | tf_op jit(solution)/shard_map/ppermute | solution.py:357
  142.6 19.7 %collective-permute-start.20 = (bf16[192,2048]{1,0:T(8,128)(2,1)S(1)}, bf16[192,2048]{1,0:T(8,128)(2,1)S(1)}, u32[]{:S(2)}, u32[]{:S(2)}) collective-permute-start(bf16[192,2048]{1,0:T(8,128)(2,1)S(1)} %get-tuple-element.157), channel_id=1, source_target_pairs={{0,16},{1,17},{2,18},{3,19},{4,20},{5,21},{6,22},{7,23},{8,24},{9,... | collective-permute-start | bytes 2359304 | tf_op jit(solution)/shard_map/ppermute | solution.py:357
  162.4 11.3 %collective-permute-start.26 = (bf16[384,2048]{1,0:T(8,128)(2,1)S(1)}, bf16[384,2048]{1,0:T(8,128)(2,1)S(1)}, u32[]{:S(2)}, u32[]{:S(2)}) collective-permute-start(bf16[384,2048]{1,0:T(8,128)(2,1)S(1)} %pad_maximum_fusion.2.refs_0_), channel_id=1, source_target_pairs={{0,8},{1,9},{2,10},{3,11},{4,12},{5,13},{6,14},{7,15},{8,0},{9,1},... | collective-permute-start | bytes 4718600 | tf_op jit(solution)/shard_map/ppermute | solution.py:357
  163.7 10.0 %collective-permute-start.27 = (bf16[384,2048]{1,0:T(8,128)(2,1)S(1)}, bf16[384,2048]{1,0:T(8,128)(2,1)S(1)}, u32[]{:S(2)}, u32[]{:S(2)}) collective-permute-start(bf16[384,2048]{1,0:T(8,128)(2,1)S(1)} %copy-done.16), channel_id=1, source_target_pairs={{0,8},{1,9},{2,10},{3,11},{4,12},{5,13},{6,14},{7,15},{8,0},{9,1},... | collective-permute-start | bytes 4718600 | tf_op jit(solution)/shard_map/ppermute | solution.py:357
  163.8 8.8 %collective-permute-start.24 = (bf16[64,2048]{1,0:T(8,128)(2,1)S(1)}, bf16[64,2048]{1,0:T(8,128)(2,1)S(1)}, u32[]{:S(2)}, u32[]{:S(2)}) collective-permute-start(bf16[64,2048]{1,0:T(8,128)(2,1)S(1)} %slice.291), channel_id=1, source_target_pairs={{0,1},{1,0},{2,3},{3,2},{4,5},{5,4},{6,7},{7,6},{8,9},{9,8},{10,11... | collective-permute-start | bytes 786440 | tf_op jit(solution)/shard_map/ppermute | solution.py:357
  165.3 8.4 %collective-permute-start.25 = (bf16[64,2048]{1,0:T(8,128)(2,1)S(1)}, bf16[64,2048]{1,0:T(8,128)(2,1)S(1)}, u32[]{:S(2)}, u32[]{:S(2)}) collective-permute-start(bf16[64,2048]{1,0:T(8,128)(2,1)S(1)} %slice.292), channel_id=1, source_target_pairs={{0,16},{1,17},{2,18},{3,19},{4,20},{5,21},{6,22},{7,23},{8,24},{9,... | collective-permute-start | bytes 786440 | tf_op jit(solution)/shard_map/ppermute | solution.py:357
  176.6 14.4 %collective-permute-start.29 = (bf16[128,2048]{1,0:T(8,128)(2,1)S(1)}, bf16[128,2048]{1,0:T(8,128)(2,1)S(1)}, u32[]{:S(2)}, u32[]{:S(2)}) collective-permute-start(bf16[128,2048]{1,0:T(8,128)(2,1)S(1)} %get-tuple-element.186), channel_id=1, source_target_pairs={{0,1},{1,0},{2,3},{3,2},{4,5},{5,4},{6,7},{7,6},{8,9},{9,8},{10,11... | collective-permute-start | bytes 1572872 | tf_op jit(solution)/shard_map/ppermute | solution.py:357
  177.2 14.1 %collective-permute-start.30 = (bf16[128,2048]{1,0:T(8,128)(2,1)S(1)}, bf16[128,2048]{1,0:T(8,128)(2,1)S(1)}, u32[]{:S(2)}, u32[]{:S(2)}) collective-permute-start(bf16[128,2048]{1,0:T(8,128)(2,1)S(1)} %get-tuple-element.187), channel_id=1, source_target_pairs={{0,16},{1,17},{2,18},{3,19},{4,20},{5,21},{6,22},{7,23},{8,24},{9,... | collective-permute-start | bytes 1572872 | tf_op jit(solution)/shard_map/ppermute | solution.py:357
  177.7 22.3 %collective-permute-start.34 = (bf16[512,2048]{1,0:T(8,128)(2,1)}, bf16[512,2048]{1,0:T(8,128)(2,1)}, u32[]{:S(2)}, u32[]{:S(2)}) collective-permute-start(bf16[512,2048]{1,0:T(8,128)(2,1)} %get-tuple-element.191), channel_id=1, source_target_pairs={{0,8},{1,9},{2,10},{3,11},{4,12},{5,13},{6,14},{7,15},{8,0},{9,1},... | collective-permute-start | bytes 6291464 | tf_op jit(solution)/shard_map/ppermute | solution.py:357
  185.7 9.6 %collective-permute-start.31 = (bf16[384,2048]{1,0:T(8,128)(2,1)}, bf16[384,2048]{1,0:T(8,128)(2,1)S(1)}, u32[]{:S(2)}, u32[]{:S(2)}) collective-permute-start(bf16[384,2048]{1,0:T(8,128)(2,1)} %get-tuple-element.181), channel_id=1, source_target_pairs={{0,8},{1,9},{2,10},{3,11},{4,12},{5,13},{6,14},{7,15},{8,0},{9,1},... | collective-permute-start | bytes 4718600 | tf_op jit(solution)/shard_map/ppermute | solution.py:357
  197.8 8.8 %collective-permute-start.32 = (bf16[64,2048]{1,0:T(8,128)(2,1)S(1)}, bf16[64,2048]{1,0:T(8,128)(2,1)S(1)}, u32[]{:S(2)}, u32[]{:S(2)}) collective-permute-start(bf16[64,2048]{1,0:T(8,128)(2,1)S(1)} %get-tuple-element.189), channel_id=1, source_target_pairs={{0,16},{1,17},{2,18},{3,19},{4,20},{5,21},{6,22},{7,23},{8,24},{9,... | collective-permute-start | bytes 786440 | tf_op jit(solution)/shard_map/ppermute | solution.py:357
  198.4 8.4 %collective-permute-start.33 = (bf16[64,2048]{1,0:T(8,128)(2,1)S(1)}, bf16[64,2048]{1,0:T(8,128)(2,1)S(1)}, u32[]{:S(2)}, u32[]{:S(2)}) collective-permute-start(bf16[64,2048]{1,0:T(8,128)(2,1)S(1)} %get-tuple-element.190), channel_id=1, source_target_pairs={{0,1},{1,0},{2,3},{3,2},{4,5},{5,4},{6,7},{7,6},{8,9},{9,8},{10,11... | collective-permute-start | bytes 786440 | tf_op jit(solution)/shard_map/ppermute | solution.py:357
  206.8 26.5 %collective-permute-start.39 = (bf16[384,2048]{1,0:T(8,128)(2,1)}, bf16[384,2048]{1,0:T(8,128)(2,1)}, u32[]{:S(2)}, u32[]{:S(2)}) collective-permute-start(bf16[384,2048]{1,0:T(8,128)(2,1)} %get-tuple-element.212), channel_id=1, source_target_pairs={{0,8},{1,9},{2,10},{3,11},{4,12},{5,13},{6,14},{7,15},{8,0},{9,1},... | collective-permute-start | bytes 4718600 | tf_op jit(solution)/shard_map/ppermute | solution.py:357
  211.6 21.6 %collective-permute-start.36 = (bf16[192,2048]{1,0:T(8,128)(2,1)}, bf16[192,2048]{1,0:T(8,128)(2,1)S(1)}, u32[]{:S(2)}, u32[]{:S(2)}) collective-permute-start(bf16[192,2048]{1,0:T(8,128)(2,1)} %get-tuple-element.207), channel_id=1, source_target_pairs={{0,1},{1,0},{2,3},{3,2},{4,5},{5,4},{6,7},{7,6},{8,9},{9,8},{10,11... | collective-permute-start | bytes 2359304 | tf_op jit(solution)/shard_map/ppermute | solution.py:357
  213.2 20.1 %collective-permute-start.37 = (bf16[192,2048]{1,0:T(8,128)(2,1)}, bf16[192,2048]{1,0:T(8,128)(2,1)S(1)}, u32[]{:S(2)}, u32[]{:S(2)}) collective-permute-start(bf16[192,2048]{1,0:T(8,128)(2,1)} %get-tuple-element.208), channel_id=1, source_target_pairs={{0,16},{1,17},{2,18},{3,19},{4,20},{5,21},{6,22},{7,23},{8,24},{9,... | collective-permute-start | bytes 2359304 | tf_op jit(solution)/shard_map/ppermute | solution.py:357
  214.7 18.6 %collective-permute-start.38 = (bf16[128,2048]{1,0:T(8,128)(2,1)}, bf16[128,2048]{1,0:T(8,128)(2,1)S(1)}, u32[]{:S(2)}, u32[]{:S(2)}) collective-permute-start(bf16[128,2048]{1,0:T(8,128)(2,1)} %get-tuple-element.209), channel_id=1, source_target_pairs={{0,2},{1,3},{2,0},{3,1},{4,6},{5,7},{6,4},{7,5},{8,10},{9,11},{10,... | collective-permute-start | bytes 1572872 | tf_op jit(solution)/shard_map/ppermute | solution.py:357
  235.6 13.9 %collective-permute-start.40 = (bf16[128,2048]{1,0:T(8,128)(2,1)S(1)}, bf16[128,2048]{1,0:T(8,128)(2,1)S(1)}, u32[]{:S(2)}, u32[]{:S(2)}) collective-permute-start(bf16[128,2048]{1,0:T(8,128)(2,1)S(1)} %get-tuple-element.218), channel_id=1, source_target_pairs={{0,1},{1,0},{2,3},{3,2},{4,5},{5,4},{6,7},{7,6},{8,9},{9,8},{10,11... | collective-permute-start | bytes 1572872 | tf_op jit(solution)/shard_map/ppermute | solution.py:357
  236.9 13.4 %collective-permute-start.41 = (bf16[128,2048]{1,0:T(8,128)(2,1)S(1)}, bf16[128,2048]{1,0:T(8,128)(2,1)S(1)}, u32[]{:S(2)}, u32[]{:S(2)}) collective-permute-start(bf16[128,2048]{1,0:T(8,128)(2,1)S(1)} %get-tuple-element.219), channel_id=1, source_target_pairs={{0,16},{1,17},{2,18},{3,19},{4,20},{5,21},{6,22},{7,23},{8,24},{9,... | collective-permute-start | bytes 1572872 | tf_op jit(solution)/shard_map/ppermute | solution.py:357
  237.8 14.5 %collective-permute-start.42 = (bf16[128,2048]{1,0:T(8,128)(2,1)S(1)}, bf16[128,2048]{1,0:T(8,128)(2,1)S(1)}, u32[]{:S(2)}, u32[]{:S(2)}) collective-permute-start(bf16[128,2048]{1,0:T(8,128)(2,1)S(1)} %get-tuple-element.220), channel_id=1, source_target_pairs={{0,2},{1,3},{6,4},{7,5},{8,10},{9,11},{14,12},{15,13},{16,18},{17,... | collective-permute-start | bytes 1572872 | tf_op jit(solution)/shard_map/ppermute | solution.py:357
  254.3 15.0 %collective-permute-start.45 = (bf16[128,2048]{1,0:T(8,128)(2,1)S(1)}, bf16[128,2048]{1,0:T(8,128)(2,1)S(1)}, u32[]{:S(2)}, u32[]{:S(2)}) collective-permute-start(bf16[128,2048]{1,0:T(8,128)(2,1)S(1)} %get-tuple-element.226), channel_id=1, source_target_pairs={{2,4},{3,5},{4,2},{5,3},{10,12},{11,13},{12,10},{13,11},{18,20},{1... | collective-permute-start | bytes 1572872 | tf_op jit(solution)/shard_map/ppermute | solution.py:357
  255.0 15.9 %collective-permute-start.46 = (bf16[128,2048]{1,0:T(8,128)(2,1)S(1)}, bf16[128,2048]{1,0:T(8,128)(2,1)S(1)}, u32[]{:S(2)}, u32[]{:S(2)}) collective-permute-start(bf16[128,2048]{1,0:T(8,128)(2,1)S(1)} %get-tuple-element.226), channel_id=1, source_target_pairs={{0,2},{1,3},{6,4},{7,5},{8,10},{9,11},{14,12},{15,13},{16,18},{17,... | collective-permute-start | bytes 1572872 | tf_op jit(solution)/shard_map/ppermute | solution.py:357
  261.4 6.4 %collective-permute-start.43 = (bf16[64,2048]{1,0:T(8,128)(2,1)S(1)}, bf16[64,2048]{1,0:T(8,128)(2,1)S(1)}, u32[]{:S(2)}, u32[]{:S(2)}) collective-permute-start(bf16[64,2048]{1,0:T(8,128)(2,1)S(1)} %get-tuple-element.224), channel_id=1, source_target_pairs={{0,1},{1,0},{2,3},{3,2},{4,5},{5,4},{6,7},{7,6},{8,9},{9,8},{10,11... | collective-permute-start | bytes 786440 | tf_op jit(solution)/shard_map/ppermute | solution.py:357
  262.9 6.4 %collective-permute-start.44 = (bf16[64,2048]{1,0:T(8,128)(2,1)S(1)}, bf16[64,2048]{1,0:T(8,128)(2,1)S(1)}, u32[]{:S(2)}, u32[]{:S(2)}) collective-permute-start(bf16[64,2048]{1,0:T(8,128)(2,1)S(1)} %get-tuple-element.225), channel_id=1, source_target_pairs={{0,16},{1,17},{2,18},{3,19},{4,20},{5,21},{6,22},{7,23},{8,24},{9,... | collective-permute-start | bytes 786440 | tf_op jit(solution)/shard_map/ppermute | solution.py:357
  274.6 11.4 %collective-permute-start.47 = (bf16[128,2048]{1,0:T(8,128)(2,1)}, bf16[128,2048]{1,0:T(8,128)(2,1)S(1)}, u32[]{:S(2)}, u32[]{:S(2)}) collective-permute-start(bf16[128,2048]{1,0:T(8,128)(2,1)} %get-tuple-element.233), channel_id=1, source_target_pairs={{0,1},{1,0},{2,3},{3,2},{4,5},{5,4},{6,7},{7,6},{8,9},{9,8},{10,11... | collective-permute-start | bytes 1572872 | tf_op jit(solution)/shard_map/ppermute | solution.py:357
  276.2 11.1 %collective-permute-start.48 = (bf16[128,2048]{1,0:T(8,128)(2,1)}, bf16[128,2048]{1,0:T(8,128)(2,1)S(1)}, u32[]{:S(2)}, u32[]{:S(2)}) collective-permute-start(bf16[128,2048]{1,0:T(8,128)(2,1)} %get-tuple-element.234), channel_id=1, source_target_pairs={{0,16},{1,17},{2,18},{3,19},{4,20},{5,21},{6,22},{7,23},{8,24},{9,... | collective-permute-start | bytes 1572872 | tf_op jit(solution)/shard_map/ppermute | solution.py:357
  277.1 11.6 %collective-permute-start.49 = (bf16[128,2048]{1,0:T(8,128)(2,1)}, bf16[128,2048]{1,0:T(8,128)(2,1)S(1)}, u32[]{:S(2)}, u32[]{:S(2)}) collective-permute-start(bf16[128,2048]{1,0:T(8,128)(2,1)} %get-tuple-element.235), channel_id=1, source_target_pairs={{0,2},{1,3},{2,0},{3,1},{4,6},{5,7},{6,4},{7,5},{8,10},{9,11},{10,... | collective-permute-start | bytes 1572872 | tf_op jit(solution)/shard_map/ppermute | solution.py:357
  279.6 9.1 %collective-permute-start.50 = (bf16[128,2048]{1,0:T(8,128)(2,1)}, bf16[128,2048]{1,0:T(8,128)(2,1)S(1)}, u32[]{:S(2)}, u32[]{:S(2)}) collective-permute-start(bf16[128,2048]{1,0:T(8,128)(2,1)} %get-tuple-element.236), channel_id=1, source_target_pairs={{2,4},{3,5},{4,2},{5,3},{10,12},{11,13},{12,10},{13,11},{18,20},{1... | collective-permute-start | bytes 1572872 | tf_op jit(solution)/shard_map/ppermute | solution.py:357
  (24 other events, 347.0 us)

commit v4 on v3

--- a/solution.py
+++ b/solution.py
@@ -89,18 +89,22 @@
                     values * cosine + swapped * sine
                 ).astype(jnp.bfloat16)
 
+    many = 2 * LANES
     page_of_key = (
-        lax.broadcasted_iota(jnp.int32, (LANES, keys), 1) // PAGE
+        lax.broadcasted_iota(jnp.int32, (many, keys), 1) // PAGE
     ).astype(jnp.float32)
-    wide = 3 * LANES
-    key_at = lax.broadcasted_iota(jnp.int32, (LANES, wide), 1)
-
-    @pl.loop(0, blocks)
+    wide = 4 * LANES
+    key_at = lax.broadcasted_iota(jnp.int32, (many, wide), 1)
+
+    @pl.loop(0, blocks // 2)
     def _(block):
-        rows = pl.ds(pl.multiple_of(block * LANES, LANES), LANES)
-        first = pl.multiple_of(jnp.clip(block - 1, 0, blocks - 3) * LANES, LANES)
+        rows = pl.ds(pl.multiple_of(block * many, many), many)
+        first = pl.multiple_of(jnp.clip(2 * block - 1, 0, blocks - 4) * LANES, LANES)
         window = pl.ds(first, wide)
-        _, start, stop, page = places(block)
+        upper_half, lower_half = places(2 * block), places(2 * block + 1)
+        start, stop, page = (
+            jnp.concatenate(pair, axis=0) for pair in zip(upper_half[1:], lower_half[1:])
+        )
         position = (key_at + first).astype(jnp.float32)
         in_page = page_of_key == page
         in_doc = (position >= start) & (position < stop)
@@ -262,11 +266,11 @@
         return pl.BlockSpec((tile, width), lambda i: (jnp.clip(i - side * steps, 0, steps - 1), 0))
 
     fetched = [pltpu.VMEM(weight.shape[1:], jnp.bfloat16) for weight in weights]
-    kept = pltpu.HBM if held else jax.ShapeDtypeStruct
+    kept = [jax.ShapeDtypeStruct, pltpu.HBM][-sides:]
     return pl.pallas_call(
         functools.partial(expert_kernel, sides, steps, first, held),
         grid=(sides * steps,),
-        out_shape=[kept((count, width), jnp.bfloat16)] * sides
+        out_shape=[make((count, width), jnp.bfloat16) for make in kept]
         + [jax.ShapeDtypeStruct((sides * count // LANES, LANES), jnp.float32)],
         in_specs=[rows_of(side) for side in range(sides)]
         + [
@@ -471,9 +475,9 @@
             first += size
 
 
-def assemble(flag, *outputs):
+def assemble(flag, *outputs, steps=2):
     width = outputs[0][0][2][0][0].shape[1]
-    wide = width // 2
+    wide = width // steps
     operands, specs = [], []
 
     def block(row):
@@ -487,11 +491,11 @@
     rows = [sum(size for size, _, _ in pieces) for pieces in outputs]
     return pl.pallas_call(
         functools.partial(assemble_kernel, outputs_plan(outputs)),
-        grid=(2,),
+        grid=(steps,),
         out_shape=[jax.ShapeDtypeStruct((count, width), jnp.bfloat16) for count in rows],
         in_specs=[pl.BlockSpec(memory_space=pltpu.SMEM)] + specs,
         out_specs=[pl.BlockSpec((count, wide), lambda j: (0, j)) for count in rows],
-        compiler_params=pltpu.CompilerParams(vmem_limit_bytes=12 * 1024 * 1024),
+        compiler_params=pltpu.CompilerParams(vmem_limit_bytes=16 * 1024 * 1024),
         cost_estimate=pl.CostEstimate(
             flops=2 * sum(rows) * width, bytes_accessed=8 * sum(rows) * width, transcendentals=0
         ),
@@ -554,13 +558,13 @@
     held = hold(*experts)
 
     to_x, to_y = assemble(
-        middle, [keep(n, p), keep(h, y0, h)], [keep(n, p), keep(h, x0)]
+        middle, [keep(n, p), keep(h, y0, h)], [keep(n, p), keep(h, x0)], steps=1
     )
     px, py = move(to_x, over_x), move(to_y, over_y)
     q_middle, q_end = move(p, z_middle), move(m, z_outward)
     px, py, q_middle, q_end, held = together(px, py, q_middle, q_end, held)
 
-    (q,) = assemble(middle, [(n, True, [(q_middle, 0), (q_end, 0)])])
+    (q,) = assemble(middle, [(n, True, [(q_middle, 0), (q_end, 0)])], steps=1)
     qx, qy = move(q, over_x), move(q, over_y)
     r_end = move(q, z_outward)
     d0 = join(py[n:], px[n:])
@@ -569,7 +573,9 @@
     qx, qy, r_end, out_0 = together(qx, qy, r_end, out_0)
 
     pick = (n, True, [(m, 0), (r_end, 0)])
-    to_x, to_y, r = assemble(middle, [pick, keep(h, qy, h)], [pick, keep(h, qx)], [pick])
+    to_x, to_y, r = assemble(
+        middle, [pick, keep(h, qy, h)], [pick, keep(h, qx)], [pick], steps=1
+    )
     rx, ry = move(to_x, over_x), move(to_y, over_y)
     dp = move(d0, z_pair)
     rows_p = join(p, px[:n], py[:n])

time: 292 us -> 289 us (0.990)
  transfers between devices with their start and end apart: 53 -> 53, of which waited for: 30 -> 31; matrix products, arithmetic and copies ran while one was open for 3% -> 3% of each run, Pallas kernels for 21% -> 20%
where the time goes in v4:
time: 289 us; the launch traced here: 288 us
  waiting for transfers between devices  115 us (40%)
  Pallas kernels  70.6 us (24%)
  starting transfers between devices  66.6 us (23%)
  blocking collectives  15.5 us (5%)
  matrix products  8.61 us (3%)
  local copies, waits for them, and re-layouts  5.63 us (2%)
  other arithmetic  4.63 us (2%)
    ppermute x51, waiting for transfers between devices, move(): return lax.ppermute(block, ALL, pairs(target))  106 us
    ppermute x51, starting transfers between devices, move(): return lax.ppermute(block, ALL, pairs(target))  55.7 us
    pallas_call x6, Pallas kernels, weighted_pieces(): pl.pallas_call(functools.partial(expert_kernel, sides, steps, first, held...  38.7 us
    pallas_call x10, Pallas kernels, assemble(): pl.pallas_call(functools.partial(assemble_kernel, outputs_plan(outputs)),...  17.1 us
    all_to_all x1, blocking collectives, experts_dense(): lax.all_to_all(doc_sums, ALL, split_axis=0, concat_axis=0, tiled=True)  15.5 us
    pallas_call x1, Pallas kernels, attention(): pl.pallas_call(attention_kernel, out_shape=jax.ShapeDtypeStruct((tokens,...  10.6 us
    all_to_all x1, waiting for transfers between devices, attention(): back = lax.all_to_all(out, 'exp', split_axis=0, concat_axis=0, tiled=True)  9.21 us
    all_to_all x1, starting transfers between devices, attention(): lax.all_to_all(parts, 'exp', split_axis=0, concat_axis=0, tiled=True)  7.4 us
  transfers between devices with their start and end apart: 53, of which 31 were waited for; matrix products, arithmetic and copies ran while one was open for 3% of the time, Pallas kernels for 20%

profile of v4, /device:TPU:0, one launch (start us, length us, event | category | flops | bytes accessed | tf_op | source)
XLA Modules:
  0.0 288.0 jit_solution(6589435030945844211)
XLA Ops:
  3.3 7.4 %all-to-all-start = ((bf16[8,128,768]{2,1,0:T(8,128)(2,1)}), bf16[8,128,768]{2,1,0:T(8,128)(2,1)S(1)}, u32[]{:S(2)}, u32[]{:S(2)}) async-start(bf16[8,128,768]{2,1,0:T(8,128)(2,1)} %bitcast.1), calls=%async_computation | async-start | bytes 3145728 | tf_op jit(solution)/shard_map/all_to_all | solution.py:164
  10.8 2.1 collective-permute-start
  13.1 1.6 collective-permute-start.5
  14.8 3.3 %fusion.1 = f32[1,512]{1,0:T(1,128)S(1)} fusion(f32[2048,1]{0,1:T(1,128)S(1)} %bitcast.195, bf16[1,512,2048]{2,1,0:T(8,128)(2,1)} %refs_2_), kind=kOutput, calls=%fused_computation.2 | convolution fusion | flops 12582912 | bytes 2107392 | tf_op jit(solution)/shard_map/dot_general | solution.py:516
  18.2 19.0 %collective-permute-done = f32[16,128]{1,0:T(8,128)S(1)} collective-permute-done((f32[16,128]{1,0:T(8,128)S(1)}, f32[16,128]{1,0:T(8,128)S(1)}, u32[]{:S(2)}, u32[]{:S(2)}) %collective-permute-start) | collective-permute-done | bytes 8224 | tf_op jit(solution)/shard_map/ppermute | solution.py:361
  37.2 3.9 %collective-permute-start.1 = (f32[2,16,128]{2,1,0:T(8,128)S(1)}, f32[2,16,128]{2,1,0:T(8,128)S(1)}, u32[]{:S(2)}, u32[]{:S(2)}) collective-permute-start(f32[2,16,128]{2,1,0:T(8,128)S(1)} %get-tuple-element.311), channel_id=1, source_target_pairs={{0,4},{1,5},{2,6},{3,7},{4,0},{5,1},{6,2},{7,3},{8,12},{9,13},{10,... | collective-permute-start | bytes 49160 | tf_op jit(solution)/shard_map/ppermute | solution.py:361
  41.2 7.2 %collective-permute-done.1 = f32[2,16,128]{2,1,0:T(8,128)S(1)} collective-permute-done((f32[2,16,128]{2,1,0:T(8,128)S(1)}, f32[2,16,128]{2,1,0:T(8,128)S(1)}, u32[]{:S(2)}, u32[]{:S(2)}) %collective-permute-start.1) | collective-permute-done | bytes 16416 | tf_op jit(solution)/shard_map/ppermute | solution.py:361
  48.5 10.6 %paged_attention.1 = bf16[1024,256]{1,0:T(8,128)(2,1)S(1)} custom-call(bf16[1024,768]{1,0:T(8,128)(2,1)S(1)} %bitcast.197, bf16[1024,512]{1,0:T(8,128)(2,1)S(1)} %bitcast.199, s32[1,128]{1,0:T(1,128)S(1)} %pad.14.len_ref, s32[1,128]{1,0:T(1,128)S(1)} %pad.15.query_ref, s32[8,1]{1,0:T(8,128)S(1)} %copy.46.table_ref, f32[1,128]{1,0:T(1,128)S(1)} %bitcast.200, ...), custom_call_target="tpu_custom_call" | custom-call | tf_op jit(solution)/shard_map/paged_attention/pallas_call | solution.py:167
  61.7 3.5 %all-to-all-start.1 = ((bf16[8,128,256]{1,2,0:T(8,128)(2,1)}), bf16[8,128,256]{1,2,0:T(8,128)(2,1)S(1)}, u32[]{:S(2)}, u32[]{:S(2)}) async-start(bf16[8,128,256]{1,2,0:T(8,128)(2,1)} %copy.47), calls=%async_computation.1 | async-start | bytes 1048576 | tf_op jit(solution)/shard_map/all_to_all | solution.py:187
  65.2 1.6 collective-permute-start.3
  66.8 3.0 %collective-permute-done.3 = f32[2,2,2,16,128]{4,3,2,1,0:T(8,128)S(1)} collective-permute-done((f32[2,2,2,16,128]{4,3,2,1,0:T(8,128)S(1)}, f32[2,2,2,16,128]{4,3,2,1,0:T(8,128)S(1)}, u32[]{:S(2)}, u32[]{:S(2)}) %collective-permute-start.3) | collective-permute-done | bytes 65568 | tf_op jit(solution)/shard_map/ppermute | solution.py:361
  71.3 9.2 %all-to-all-done.1 = bf16[8,128,256]{1,2,0:T(8,128)(2,1)S(1)} async-done(((bf16[8,128,256]{1,2,0:T(8,128)(2,1)}), bf16[8,128,256]{1,2,0:T(8,128)(2,1)S(1)}, u32[]{:S(2)}, u32[]{:S(2)}) %all-to-all-start.1) | async-done | bytes 524320 | tf_op jit(solution)/shard_map/all_to_all | solution.py:187
  80.6 4.8 %fusion.3 = (f32[128]{0:T(128)S(1)}, bf16[128,2048]{1,0:T(8,128)(2,1)S(1)}) fusion(bf16[128,2048]{0,1:T(8,128)(2,1)S(1)} %bitcast.202, bf16[2048,2048]{1,0:T(8,128)(2,1)} %param.28, bf16[128,2048]{1,0:T(8,128)(2,1)S(1)} %copy-done.10), kind=kOutput, calls=%fused_computation.10 | convolution fusion | flops 1075314560 | bytes 9961984 | tf_op jit(solution)/shard_map/dot_general | solution.py:716
  87.8 1.5 collective-permute-start.10
  89.4 9.8 %collective-permute-done.7.refs_1_.refs_3_ = bf16[128,2048]{1,0:T(8,128)(2,1)S(1)} collective-permute-done((bf16[128,2048]{1,0:T(8,128)(2,1)S(1)}, bf16[128,2048]{1,0:T(8,128)(2,1)S(1)}, u32[]{:S(2)}, u32[]{:S(2)}) %collective-permute-start.7) | collective-permute-done | bytes 524320 | tf_op jit(solution)/shard_map/ppermute | solution.py:361
  101.9 1.5 collective-permute-start.12
  105.4 2.9 %hold_weights.1 = (bf16[1,2048,512]{2,1,0:T(8,128)(2,1)S(1)}, bf16[1,2048,512]{2,1,0:T(8,128)(2,1)S(1)}, bf16[1,512,2048]{2,1,0:T(8,128)(2,1)S(1)}) custom-call(bf16[1,2048,512]{2,1,0:T(8,128)(2,1)} %refs_0_, bf16[1,2048,512]{2,1,0:T(8,128)(2,1)} %refs_1_, bf16[1,512,2048]{2,1,0:T(8,128)(2,1)} %refs_2_), custom_call_target="tpu_custom_call" | custom-call | bytes 12582912 | tf_op jit(solution)/shard_map/hold_weights/pallas_call | solution.py:443
  108.4 12.0 %collective-permute-done.14.refs_2_ = bf16[128,2048]{1,0:T(8,128)(2,1)S(1)} collective-permute-done((bf16[128,2048]{1,0:T(8,128)(2,1)S(1)}, bf16[128,2048]{1,0:T(8,128)(2,1)S(1)}, u32[]{:S(2)}, u32[]{:S(2)}) %collective-permute-start.14) | collective-permute-done | bytes 524320 | tf_op jit(solution)/shard_map/ppermute | solution.py:361
  124.8 9.4 %expert_half.6 = (bf16[512,2048]{1,0:T(8,128)(2,1)}, bf16[512,2048]{1,0:T(8,128)(2,1)}, f32[8,128]{1,0:T(8,128)S(1)}) custom-call(bf16[512,2048]{1,0:T(8,128)(2,1)S(1)} %collective-permute-done.18.refs_0_, bf16[512,2048]{1,0:T(8,128)(2,1)S(1)} %get-tuple-element.241.refs_1_, f32[32,128]{1,0:T(8,128)S(1)} %stack.101.refs_2_.refs_1_, ...), custom_call_target="tpu_custom_call" | custom-call | flops 6442450944 | bytes 14680064 | tf_op jit(solution)/shard_map/expert_half/pallas_call | solution.py:270
  136.2 3.3 %collective-permute-done.17.refs_2_.refs_5_.refs_8_ = bf16[128,2048]{1,0:T(8,128)(2,1)S(1)} collective-permute-done((bf16[128,2048]{1,0:T(8,128)(2,1)S(1)}, bf16[128,2048]{1,0:T(8,128)(2,1)S(1)}, u32[]{:S(2)}, u32[]{:S(2)}) %collective-permute-start.17) | collective-permute-done | bytes 524320 | tf_op jit(solution)/shard_map/ppermute | solution.py:361
  141.4 6.9 %expert_half.7 = (bf16[384,2048]{1,0:T(8,128)(2,1)S(1)}, bf16[384,2048]{1,0:T(8,128)(2,1)}, f32[6,128]{1,0:T(8,128)S(1)}) custom-call(bf16[384,2048]{1,0:T(8,128)(2,1)S(1)} %collective-permute-done.22.refs_0_, bf16[384,2048]{1,0:T(8,128)(2,1)S(1)} %pad_maximum_fusion.refs_1_, f32[32,128]{1,0:T(8,128)S(1)} %stack.101.refs_2_.refs_1_, ...), custom_call_target="tpu_custom_call" | custom-call | flops 4831838208 | bytes 12582912 | tf_op jit(solution)/shard_map/expert_half/pallas_call | solution.py:270
  148.4 7.3 %expert_half.8 = (bf16[384,2048]{1,0:T(8,128)(2,1)}, bf16[384,2048]{1,0:T(8,128)(2,1)}, f32[6,128]{1,0:T(8,128)S(1)}) custom-call(bf16[384,2048]{1,0:T(8,128)(2,1)S(1)} %collective-permute-done.23.refs_0_, bf16[384,2048]{1,0:T(8,128)(2,1)S(1)} %pad_maximum_fusion.1.refs_1_, f32[32,128]{1,0:T(8,128)S(1)} %stack.101.refs_2_.refs_1_, ...), custom_call_target="tpu_custom_call" | custom-call | flops 4831838208 | bytes 12582912 | tf_op jit(solution)/shard_map/expert_half/pallas_call | solution.py:270
  155.7 4.3 %collective-permute-done.19 = bf16[192,2048]{1,0:T(8,128)(2,1)S(1)} collective-permute-done((bf16[192,2048]{1,0:T(8,128)(2,1)S(1)}, bf16[192,2048]{1,0:T(8,128)(2,1)S(1)}, u32[]{:S(2)}, u32[]{:S(2)}) %collective-permute-start.19) | collective-permute-done | bytes 786464 | tf_op jit(solution)/shard_map/ppermute | solution.py:361
  161.2 1.5 collective-permute-start.24
  163.2 4.0 %expert_half.9 = (bf16[384,2048]{1,0:T(8,128)(2,1)}, f32[3,128]{1,0:T(4,128)S(1)}) custom-call(bf16[384,2048]{1,0:T(8,128)(2,1)S(1)} %pad_maximum_fusion.2.refs_0_, f32[32,128]{1,0:T(8,128)S(1)} %stack.101.refs_2_.refs_1_, bf16[16,512]{1,0:T(8,128)(2,1)S(1)} %fusion.11.refs_3_.refs_2_, bf16[1,2048,512]{2,1,0:T(8,128)(2,1)S(1)} %get-tuple-element.147.refs_4_.refs_3_, ...), custom_call_target="tpu_custom_call" | custom-call | flops 2415919104 | bytes 9437184 | tf_op jit(solution)/shard_map/expert_half/pallas_call | solution.py:270
  167.2 2.3 collective-permute-done.24
  171.9 1.7 assemble.13
  175.3 7.0 %expert_half.10 = (bf16[384,2048]{1,0:T(8,128)(2,1)S(1)}, bf16[384,2048]{1,0:T(8,128)(2,1)}, f32[6,128]{1,0:T(8,128)S(1)}) custom-call(bf16[384,2048]{1,0:T(8,128)(2,1)S(1)} %collective-permute-done.28.refs_0_, bf16[384,2048]{1,0:T(8,128)(2,1)S(1)} %constant_dynamic-update-slice_fusion.5.refs_1_, f32[32,128]{1,0:T(8,128)S(1)} %stack.101.refs_2_.refs_1_, ...), custom_call_target="tpu_custom_call" | custom-call | flops 4831838208 | bytes 12582912 | tf_op jit(solution)/shard_map/expert_half/pallas_call | solution.py:270
  182.4 5.6 %collective-permute-done.29.refs_13_ = bf16[128,2048]{1,0:T(8,128)(2,1)S(1)} collective-permute-done((bf16[128,2048]{1,0:T(8,128)(2,1)S(1)}, bf16[128,2048]{1,0:T(8,128)(2,1)S(1)}, u32[]{:S(2)}, u32[]{:S(2)}) %collective-permute-start.29) | collective-permute-done | bytes 524320 | tf_op jit(solution)/shard_map/ppermute | solution.py:361
  188.2 4.0 %expert_half.11 = (bf16[384,2048]{1,0:T(8,128)(2,1)}, f32[3,128]{1,0:T(4,128)S(1)}) custom-call(bf16[384,2048]{1,0:T(8,128)(2,1)S(1)} %collective-permute-done.26.refs_0_, f32[32,128]{1,0:T(8,128)S(1)} %stack.101.refs_2_.refs_1_, bf16[16,512]{1,0:T(8,128)(2,1)S(1)} %fusion.11.refs_3_.refs_2_, bf16[1,2048,512]{2,1,0:T(8,128)(2,1)S(1)} %get-tuple-element.147.refs_4_.refs_3_, ...), custom_call_target="tpu_custom_call" | custom-call | flops 2415919104 | bytes 9437184 | tf_op jit(solution)/shard_map/expert_half/pallas_call | solution.py:270
  197.0 6.6 %collective-permute-done.32.refs_3_ = bf16[64,2048]{1,0:T(8,128)(2,1)S(1)} collective-permute-done((bf16[64,2048]{1,0:T(8,128)(2,1)S(1)}, bf16[64,2048]{1,0:T(8,128)(2,1)S(1)}, u32[]{:S(2)}, u32[]{:S(2)}) %collective-permute-start.32) | collective-permute-done | bytes 262176 | tf_op jit(solution)/shard_map/ppermute | solution.py:361
  205.2 3.5 %assemble.15 = (bf16[192,2048]{1,0:T(8,128)(2,1)}, bf16[192,2048]{1,0:T(8,128)(2,1)}, bf16[128,2048]{1,0:T(8,128)(2,1)}) custom-call(s32[1]{0:T(128)} %bitcast.refs_0_, bf16[384,2048]{1,0:T(8,128)(2,1)} %get-tuple-element.203.refs_1_.refs_4_.refs_8_.refs_10_.refs_11_.refs_16_, ...), custom_call_target="tpu_custom_call" | custom-call | flops 2097152 | bytes 8388608 | tf_op jit(solution)/shard_map/assemble/pallas_call | solution.py:492
  208.7 1.5 collective-permute-start.36
  210.2 1.5 collective-permute-start.37
  211.7 1.7 collective-permute-start.38
  214.8 15.5 %all_to_all.32 = f32[32,1,32]{2,1,0:T(1,128)S(1)} all-to-all(f32[32,1,32]{2,1,0:T(1,128)S(1)} %bitcast.209), channel_id=1, replica_groups=mesh['req'=4,'exp'=8] {'req','exp'}, dimensions={0} | all-to-all | bytes 8192 | tf_op jit(solution)/shard_map/all_to_all | solution.py:650
  230.3 2.3 assemble.16
  234.8 3.8 %collective-permute-start.42 = (bf16[128,2048]{1,0:T(8,128)(2,1)S(1)}, bf16[128,2048]{1,0:T(8,128)(2,1)S(1)}, u32[]{:S(2)}, u32[]{:S(2)}) collective-permute-start(bf16[128,2048]{1,0:T(8,128)(2,1)S(1)} %get-tuple-element.220), channel_id=1, source_target_pairs={{0,2},{1,3},{6,4},{7,5},{8,10},{9,11},{14,12},{15,13},{16,18},{17,... | collective-permute-start | bytes 1572872 | tf_op jit(solution)/shard_map/ppermute | solution.py:361
  238.6 8.0 %collective-permute-done.40.refs_9_ = bf16[128,2048]{1,0:T(8,128)(2,1)S(1)} collective-permute-done((bf16[128,2048]{1,0:T(8,128)(2,1)S(1)}, bf16[128,2048]{1,0:T(8,128)(2,1)S(1)}, u32[]{:S(2)}, u32[]{:S(2)}) %collective-permute-start.40) | collective-permute-done | bytes 524320 | tf_op jit(solution)/shard_map/ppermute | solution.py:361
  247.2 2.1 collective-permute-done.42.refs_11_
  249.4 2.0 assemble.17
  252.0 6.4 %collective-permute-start.46 = (bf16[128,2048]{1,0:T(8,128)(2,1)S(1)}, bf16[128,2048]{1,0:T(8,128)(2,1)S(1)}, u32[]{:S(2)}, u32[]{:S(2)}) collective-permute-start(bf16[128,2048]{1,0:T(8,128)(2,1)S(1)} %get-tuple-element.226), channel_id=1, source_target_pairs={{0,2},{1,3},{6,4},{7,5},{8,10},{9,11},{14,12},{15,13},{16,18},{17,... | collective-permute-start | bytes 1572872 | tf_op jit(solution)/shard_map/ppermute | solution.py:361
  260.9 4.0 %collective-permute-done.43.refs_10_ = bf16[64,2048]{1,0:T(8,128)(2,1)S(1)} collective-permute-done((bf16[64,2048]{1,0:T(8,128)(2,1)S(1)}, bf16[64,2048]{1,0:T(8,128)(2,1)S(1)}, u32[]{:S(2)}, u32[]{:S(2)}) %collective-permute-start.43) | collective-permute-done | bytes 262176 | tf_op jit(solution)/shard_map/ppermute | solution.py:361
  266.3 1.7 collective-permute-done.46.refs_20_
  267.9 3.7 %assemble.18 = (bf16[128,2048]{1,0:T(8,128)(2,1)}, bf16[128,2048]{1,0:T(8,128)(2,1)}, bf16[128,2048]{1,0:T(8,128)(2,1)}, bf16[128,2048]{1,0:T(8,128)(2,1)}) custom-call(s32[1]{0:T(128)} %bitcast.refs_0_, bf16[512,2048]{1,0:T(8,128)(2,1)} %get-tuple-element.176.refs_1_.refs_4_.refs_6_.refs_8_, ...), custom_call_target="tpu_custom_call" | custom-call | flops 2097152 | bytes 8388608 | tf_op jit(solution)/shard_map/assemble/pallas_call | solution.py:492
  274.2 2.5 collective-permute-start.49
  277.9 5.2 %collective-permute-done.47.refs_3_ = bf16[128,2048]{1,0:T(8,128)(2,1)S(1)} collective-permute-done((bf16[128,2048]{1,0:T(8,128)(2,1)}, bf16[128,2048]{1,0:T(8,128)(2,1)S(1)}, u32[]{:S(2)}, u32[]{:S(2)}) %collective-permute-start.47) | collective-permute-done | bytes 524320 | tf_op jit(solution)/shard_map/ppermute | solution.py:361
  285.7 2.2 assemble.19
  (181 shorter events, 50.2 us)
Async XLA Ops:
  3.3 45.1 %all-to-all-start = ((bf16[8,128,768]{2,1,0:T(8,128)(2,1)}), bf16[8,128,768]{2,1,0:T(8,128)(2,1)S(1)}, u32[]{:S(2)}, u32[]{:S(2)}) async-start(bf16[8,128,768]{2,1,0:T(8,128)(2,1)} %bitcast.1), calls=%async_computation | async-start | bytes 3145728 | tf_op jit(solution)/shard_map/all_to_all | solution.py:164
  10.8 26.3 %collective-permute-start = (f32[16,128]{1,0:T(8,128)S(1)}, f32[16,128]{1,0:T(8,128)S(1)}, u32[]{:S(2)}, u32[]{:S(2)}) collective-permute-start(f32[16,128]{1,0:T(8,128)S(1)} %select_reduce_fusion), channel_id=1, source_target_pairs={{0,2},{1,3},{2,0},{3,1},{4,6},{5,7},{6,4},{7,5},{8,10},{9,11},{10,... | collective-permute-start | bytes 24584 | tf_op jit(solution)/shard_map/ppermute | solution.py:361
  13.1 47.4 %collective-permute-start.5 = (s32[2,32]{1,0:T(2,128)S(1)}, s32[2,32]{1,0:T(2,128)S(1)}, u32[]{:S(2)}, u32[]{:S(2)}) collective-permute-start(s32[2,32]{1,0:T(2,128)S(1)} %get-tuple-element.319), channel_id=1, source_target_pairs={{0,16},{1,17},{2,18},{3,19},{4,20},{5,21},{6,22},{7,23},{8,24},{9,... | collective-permute-start | bytes 776 | tf_op jit(solution)/shard_map/ppermute | solution.py:361
  37.2 11.3 %collective-permute-start.1 = (f32[2,16,128]{2,1,0:T(8,128)S(1)}, f32[2,16,128]{2,1,0:T(8,128)S(1)}, u32[]{:S(2)}, u32[]{:S(2)}) collective-permute-start(f32[2,16,128]{2,1,0:T(8,128)S(1)} %get-tuple-element.311), channel_id=1, source_target_pairs={{0,4},{1,5},{2,6},{3,7},{4,0},{5,1},{6,2},{7,3},{8,12},{9,13},{10,... | collective-permute-start | bytes 49160 | tf_op jit(solution)/shard_map/ppermute | solution.py:361
  59.1 6.1 %collective-permute-start.2 = (f32[2,2,16,128]{3,2,1,0:T(8,128)S(1)}, f32[2,2,16,128]{3,2,1,0:T(8,128)S(1)}, u32[]{:S(2)}, u32[]{:S(2)}) collective-permute-start(f32[2,2,16,128]{3,2,1,0:T(8,128)S(1)} %pad_maximum_fusion.6), channel_id=1, source_target_pairs={{0,1},{1,0},{2,3},{3,2},{4,5},{5,4},{6,7},{7,6},{8,9},{9,8},{10,11... | collective-permute-start | bytes 98312 | tf_op jit(solution)/shard_map/ppermute | solution.py:361
  60.6 6.2 %collective-permute-start.6 = (s32[2,2,32]{2,1,0:T(2,128)S(1)}, s32[2,2,32]{2,1,0:T(2,128)S(1)}, u32[]{:S(2)}, u32[]{:S(2)}) collective-permute-start(s32[2,2,32]{2,1,0:T(2,128)S(1)} %get-tuple-element.317), channel_id=1, source_target_pairs={{0,8},{1,9},{2,10},{3,11},{4,12},{5,13},{6,14},{7,15},{8,0},{9,1},... | collective-permute-start | bytes 1544 | tf_op jit(solution)/shard_map/ppermute | solution.py:361
  61.7 18.9 %all-to-all-start.1 = ((bf16[8,128,256]{1,2,0:T(8,128)(2,1)}), bf16[8,128,256]{1,2,0:T(8,128)(2,1)S(1)}, u32[]{:S(2)}, u32[]{:S(2)}) async-start(bf16[8,128,256]{1,2,0:T(8,128)(2,1)} %copy.47), calls=%async_computation.1 | async-start | bytes 1048576 | tf_op jit(solution)/shard_map/all_to_all | solution.py:187
  85.6 13.6 %collective-permute-start.7 = (bf16[128,2048]{1,0:T(8,128)(2,1)S(1)}, bf16[128,2048]{1,0:T(8,128)(2,1)S(1)}, u32[]{:S(2)}, u32[]{:S(2)}) collective-permute-start(bf16[128,2048]{1,0:T(8,128)(2,1)S(1)} %fusion.5), channel_id=1, source_target_pairs={{0,2},{1,3},{2,0},{3,1},{4,6},{5,7},{6,4},{7,5},{8,10},{9,11},{10,... | collective-permute-start | bytes 1572872 | tf_op jit(solution)/shard_map/ppermute | solution.py:361
  86.1 13.1 %collective-permute-start.8 = (bf16[128,2048]{1,0:T(8,128)(2,1)S(1)}, bf16[128,2048]{1,0:T(8,128)(2,1)S(1)}, u32[]{:S(2)}, u32[]{:S(2)}) collective-permute-start(bf16[128,2048]{1,0:T(8,128)(2,1)S(1)} %fusion.5), channel_id=1, source_target_pairs={{2,4},{3,5},{4,2},{5,3},{10,12},{11,13},{12,10},{13,11},{18,20},{1... | collective-permute-start | bytes 1572872 | tf_op jit(solution)/shard_map/ppermute | solution.py:361
  86.8 13.2 %collective-permute-start.9 = (bf16[128,2048]{1,0:T(8,128)(2,1)S(1)}, bf16[128,2048]{1,0:T(8,128)(2,1)S(1)}, u32[]{:S(2)}, u32[]{:S(2)}) collective-permute-start(bf16[128,2048]{1,0:T(8,128)(2,1)S(1)} %fusion.5), channel_id=1, source_target_pairs={{0,1},{1,0},{2,3},{3,2},{4,5},{5,4},{6,7},{7,6},{8,9},{9,8},{10,11... | collective-permute-start | bytes 1572872 | tf_op jit(solution)/shard_map/ppermute | solution.py:361
  87.8 13.3 %collective-permute-start.10 = (bf16[128,2048]{1,0:T(8,128)(2,1)S(1)}, bf16[128,2048]{1,0:T(8,128)(2,1)S(1)}, u32[]{:S(2)}, u32[]{:S(2)}) collective-permute-start(bf16[128,2048]{1,0:T(8,128)(2,1)S(1)} %fusion.5), channel_id=1, source_target_pairs={{0,16},{1,17},{2,18},{3,19},{4,20},{5,21},{6,22},{7,23},{8,24},{9,... | collective-permute-start | bytes 1572872 | tf_op jit(solution)/shard_map/ppermute | solution.py:361
  101.2 19.2 %collective-permute-start.11 = (bf16[192,2048]{1,0:T(8,128)(2,1)S(1)}, bf16[192,2048]{1,0:T(8,128)(2,1)S(1)}, u32[]{:S(2)}, u32[]{:S(2)}) collective-permute-start(bf16[192,2048]{1,0:T(8,128)(2,1)S(1)} %get-tuple-element.133), channel_id=1, source_target_pairs={{0,1},{1,0},{2,3},{3,2},{4,5},{5,4},{6,7},{7,6},{8,9},{9,8},{10,11... | collective-permute-start | bytes 2359304 | tf_op jit(solution)/shard_map/ppermute | solution.py:361
  101.9 18.6 %collective-permute-start.12 = (bf16[192,2048]{1,0:T(8,128)(2,1)S(1)}, bf16[192,2048]{1,0:T(8,128)(2,1)S(1)}, u32[]{:S(2)}, u32[]{:S(2)}) collective-permute-start(bf16[192,2048]{1,0:T(8,128)(2,1)S(1)} %get-tuple-element.134), channel_id=1, source_target_pairs={{0,16},{1,17},{2,18},{3,19},{4,20},{5,21},{6,22},{7,23},{8,24},{9,... | collective-permute-start | bytes 2359304 | tf_op jit(solution)/shard_map/ppermute | solution.py:361
  103.4 5.0 %collective-permute-start.13 = (bf16[128,2048]{1,0:T(8,128)(2,1)S(1)}, bf16[128,2048]{1,0:T(8,128)(2,1)S(1)}, u32[]{:S(2)}, u32[]{:S(2)}) collective-permute-start(bf16[128,2048]{1,0:T(8,128)(2,1)S(1)} %collective-permute-done.7.refs_1_.refs_3_), channel_id=1, source_target_pairs={{2,4},{3,5},{4,2},{5,3},{10,12},{11,13},{12,10},{13,11},{18,20},{1... | collective-permute-start | bytes 1572872 | tf_op jit(solution)/shard_map/ppermute | solution.py:361
  104.1 16.4 %collective-permute-start.14 = (bf16[128,2048]{1,0:T(8,128)(2,1)S(1)}, bf16[128,2048]{1,0:T(8,128)(2,1)S(1)}, u32[]{:S(2)}, u32[]{:S(2)}) collective-permute-start(bf16[128,2048]{1,0:T(8,128)(2,1)S(1)} %collective-permute-done.8.refs_1_.refs_4_.refs_7_), channel_id=1, source_target_pairs={{2,0},{3,1},{4,6},{5,7},{10,8},{11,9},{12,14},{13,15},{18,16},{19,... | collective-permute-start | bytes 1572872 | tf_op jit(solution)/shard_map/ppermute | solution.py:361
  120.7 14.4 %collective-permute-start.15 = (bf16[128,2048]{1,0:T(8,128)(2,1)S(1)}, bf16[128,2048]{1,0:T(8,128)(2,1)S(1)}, u32[]{:S(2)}, u32[]{:S(2)}) collective-permute-start(bf16[128,2048]{1,0:T(8,128)(2,1)S(1)} %assemble.11), channel_id=1, source_target_pairs={{0,1},{1,0},{2,3},{3,2},{4,5},{5,4},{6,7},{7,6},{8,9},{9,8},{10,11... | collective-permute-start | bytes 1572872 | tf_op jit(solution)/shard_map/ppermute | solution.py:361
  122.2 14.0 %collective-permute-start.16 = (bf16[128,2048]{1,0:T(8,128)(2,1)S(1)}, bf16[128,2048]{1,0:T(8,128)(2,1)S(1)}, u32[]{:S(2)}, u32[]{:S(2)}) collective-permute-start(bf16[128,2048]{1,0:T(8,128)(2,1)S(1)} %assemble.11), channel_id=1, source_target_pairs={{0,16},{1,17},{2,18},{3,19},{4,20},{5,21},{6,22},{7,23},{8,24},{9,... | collective-permute-start | bytes 1572872 | tf_op jit(solution)/shard_map/ppermute | solution.py:361
  122.8 16.7 %collective-permute-start.17 = (bf16[128,2048]{1,0:T(8,128)(2,1)S(1)}, bf16[128,2048]{1,0:T(8,128)(2,1)S(1)}, u32[]{:S(2)}, u32[]{:S(2)}) collective-permute-start(bf16[128,2048]{1,0:T(8,128)(2,1)S(1)} %assemble.11), channel_id=1, source_target_pairs={{2,0},{3,1},{4,6},{5,7},{10,8},{11,9},{12,14},{13,15},{18,16},{19,... | collective-permute-start | bytes 1572872 | tf_op jit(solution)/shard_map/ppermute | solution.py:361
  124.5 16.9 %collective-permute-start.22 = (bf16[384,2048]{1,0:T(8,128)(2,1)S(1)}, bf16[384,2048]{1,0:T(8,128)(2,1)S(1)}, u32[]{:S(2)}, u32[]{:S(2)}) collective-permute-start(bf16[384,2048]{1,0:T(8,128)(2,1)S(1)} %pad_maximum_fusion.refs_1_), channel_id=1, source_target_pairs={{0,8},{1,9},{2,10},{3,11},{4,12},{5,13},{6,14},{7,15},{8,0},{9,1},... | collective-permute-start | bytes 4718600 | tf_op jit(solution)/shard_map/ppermute | solution.py:361
  139.7 8.7 %collective-permute-start.23 = (bf16[384,2048]{1,0:T(8,128)(2,1)S(1)}, bf16[384,2048]{1,0:T(8,128)(2,1)S(1)}, u32[]{:S(2)}, u32[]{:S(2)}) collective-permute-start(bf16[384,2048]{1,0:T(8,128)(2,1)S(1)} %pad_maximum_fusion.1.refs_1_), channel_id=1, source_target_pairs={{0,8},{1,9},{2,10},{3,11},{4,12},{5,13},{6,14},{7,15},{8,0},{9,1},... | collective-permute-start | bytes 4718600 | tf_op jit(solution)/shard_map/ppermute | solution.py:361
  139.8 15.9 %collective-permute-start.21 = (bf16[128,2048]{1,0:T(8,128)(2,1)S(1)}, bf16[128,2048]{1,0:T(8,128)(2,1)S(1)}, u32[]{:S(2)}, u32[]{:S(2)}) collective-permute-start(bf16[128,2048]{1,0:T(8,128)(2,1)S(1)} %pad_maximum_fusion.3), channel_id=1, source_target_pairs={{0,2},{1,3},{2,0},{3,1},{4,6},{5,7},{6,4},{7,5},{8,10},{9,11},{10,... | collective-permute-start | bytes 1572872 | tf_op jit(solution)/shard_map/ppermute | solution.py:361
  140.1 20.0 %collective-permute-start.19 = (bf16[192,2048]{1,0:T(8,128)(2,1)S(1)}, bf16[192,2048]{1,0:T(8,128)(2,1)S(1)}, u32[]{:S(2)}, u32[]{:S(2)}) collective-permute-start(bf16[192,2048]{1,0:T(8,128)(2,1)S(1)} %get-tuple-element.156), channel_id=1, source_target_pairs={{0,1},{1,0},{2,3},{3,2},{4,5},{5,4},{6,7},{7,6},{8,9},{9,8},{10,11... | collective-permute-start | bytes 2359304 | tf_op jit(solution)/shard_map/ppermute | solution.py:361
  140.7 19.7 %collective-permute-start.20 = (bf16[192,2048]{1,0:T(8,128)(2,1)S(1)}, bf16[192,2048]{1,0:T(8,128)(2,1)S(1)}, u32[]{:S(2)}, u32[]{:S(2)}) collective-permute-start(bf16[192,2048]{1,0:T(8,128)(2,1)S(1)} %get-tuple-element.157), channel_id=1, source_target_pairs={{0,16},{1,17},{2,18},{3,19},{4,20},{5,21},{6,22},{7,23},{8,24},{9,... | collective-permute-start | bytes 2359304 | tf_op jit(solution)/shard_map/ppermute | solution.py:361
  160.6 10.2 %collective-permute-start.26 = (bf16[384,2048]{1,0:T(8,128)(2,1)S(1)}, bf16[384,2048]{1,0:T(8,128)(2,1)S(1)}, u32[]{:S(2)}, u32[]{:S(2)}) collective-permute-start(bf16[384,2048]{1,0:T(8,128)(2,1)S(1)} %pad_maximum_fusion.2.refs_0_), channel_id=1, source_target_pairs={{0,8},{1,9},{2,10},{3,11},{4,12},{5,13},{6,14},{7,15},{8,0},{9,1},... | collective-permute-start | bytes 4718600 | tf_op jit(solution)/shard_map/ppermute | solution.py:361
  160.6 10.1 %collective-permute-start.27 = (bf16[384,2048]{1,0:T(8,128)(2,1)S(1)}, bf16[384,2048]{1,0:T(8,128)(2,1)S(1)}, u32[]{:S(2)}, u32[]{:S(2)}) collective-permute-start(bf16[384,2048]{1,0:T(8,128)(2,1)S(1)} %get-tuple-element.169), channel_id=1, source_target_pairs={{0,8},{1,9},{2,10},{3,11},{4,12},{5,13},{6,14},{7,15},{8,0},{9,1},... | collective-permute-start | bytes 4718600 | tf_op jit(solution)/shard_map/ppermute | solution.py:361
  161.2 8.4 %collective-permute-start.24 = (bf16[64,2048]{1,0:T(8,128)(2,1)S(1)}, bf16[64,2048]{1,0:T(8,128)(2,1)S(1)}, u32[]{:S(2)}, u32[]{:S(2)}) collective-permute-start(bf16[64,2048]{1,0:T(8,128)(2,1)S(1)} %slice.291), channel_id=1, source_target_pairs={{0,1},{1,0},{2,3},{3,2},{4,5},{5,4},{6,7},{7,6},{8,9},{9,8},{10,11... | collective-permute-start | bytes 786440 | tf_op jit(solution)/shard_map/ppermute | solution.py:361
  162.7 8.0 %collective-permute-start.25 = (bf16[64,2048]{1,0:T(8,128)(2,1)S(1)}, bf16[64,2048]{1,0:T(8,128)(2,1)S(1)}, u32[]{:S(2)}, u32[]{:S(2)}) collective-permute-start(bf16[64,2048]{1,0:T(8,128)(2,1)S(1)} %slice.292), channel_id=1, source_target_pairs={{0,16},{1,17},{2,18},{3,19},{4,20},{5,21},{6,22},{7,23},{8,24},{9,... | collective-permute-start | bytes 786440 | tf_op jit(solution)/shard_map/ppermute | solution.py:361
  173.6 14.4 %collective-permute-start.29 = (bf16[128,2048]{1,0:T(8,128)(2,1)S(1)}, bf16[128,2048]{1,0:T(8,128)(2,1)S(1)}, u32[]{:S(2)}, u32[]{:S(2)}) collective-permute-start(bf16[128,2048]{1,0:T(8,128)(2,1)S(1)} %get-tuple-element.186), channel_id=1, source_target_pairs={{0,1},{1,0},{2,3},{3,2},{4,5},{5,4},{6,7},{7,6},{8,9},{9,8},{10,11... | collective-permute-start | bytes 1572872 | tf_op jit(solution)/shard_map/ppermute | solution.py:361
  174.2 14.1 %collective-permute-start.30 = (bf16[128,2048]{1,0:T(8,128)(2,1)S(1)}, bf16[128,2048]{1,0:T(8,128)(2,1)S(1)}, u32[]{:S(2)}, u32[]{:S(2)}) collective-permute-start(bf16[128,2048]{1,0:T(8,128)(2,1)S(1)} %get-tuple-element.187), channel_id=1, source_target_pairs={{0,16},{1,17},{2,18},{3,19},{4,20},{5,21},{6,22},{7,23},{8,24},{9,... | collective-permute-start | bytes 1572872 | tf_op jit(solution)/shard_map/ppermute | solution.py:361
  174.7 22.3 %collective-permute-start.34 = (bf16[512,2048]{1,0:T(8,128)(2,1)}, bf16[512,2048]{1,0:T(8,128)(2,1)}, u32[]{:S(2)}, u32[]{:S(2)}) collective-permute-start(bf16[512,2048]{1,0:T(8,128)(2,1)} %get-tuple-element.191), channel_id=1, source_target_pairs={{0,8},{1,9},{2,10},{3,11},{4,12},{5,13},{6,14},{7,15},{8,0},{9,1},... | collective-permute-start | bytes 6291464 | tf_op jit(solution)/shard_map/ppermute | solution.py:361
  182.2 10.1 %collective-permute-start.31 = (bf16[384,2048]{1,0:T(8,128)(2,1)S(1)}, bf16[384,2048]{1,0:T(8,128)(2,1)S(1)}, u32[]{:S(2)}, u32[]{:S(2)}) collective-permute-start(bf16[384,2048]{1,0:T(8,128)(2,1)S(1)} %get-tuple-element.181), channel_id=1, source_target_pairs={{0,8},{1,9},{2,10},{3,11},{4,12},{5,13},{6,14},{7,15},{8,0},{9,1},... | collective-permute-start | bytes 4718600 | tf_op jit(solution)/shard_map/ppermute | solution.py:361
  194.8 8.8 %collective-permute-start.32 = (bf16[64,2048]{1,0:T(8,128)(2,1)S(1)}, bf16[64,2048]{1,0:T(8,128)(2,1)S(1)}, u32[]{:S(2)}, u32[]{:S(2)}) collective-permute-start(bf16[64,2048]{1,0:T(8,128)(2,1)S(1)} %get-tuple-element.189), channel_id=1, source_target_pairs={{0,16},{1,17},{2,18},{3,19},{4,20},{5,21},{6,22},{7,23},{8,24},{9,... | collective-permute-start | bytes 786440 | tf_op jit(solution)/shard_map/ppermute | solution.py:361
  195.4 8.4 %collective-permute-start.33 = (bf16[64,2048]{1,0:T(8,128)(2,1)S(1)}, bf16[64,2048]{1,0:T(8,128)(2,1)S(1)}, u32[]{:S(2)}, u32[]{:S(2)}) collective-permute-start(bf16[64,2048]{1,0:T(8,128)(2,1)S(1)} %get-tuple-element.190), channel_id=1, source_target_pairs={{0,1},{1,0},{2,3},{3,2},{4,5},{5,4},{6,7},{7,6},{8,9},{9,8},{10,11... | collective-permute-start | bytes 786440 | tf_op jit(solution)/shard_map/ppermute | solution.py:361
  203.8 26.5 %collective-permute-start.39 = (bf16[384,2048]{1,0:T(8,128)(2,1)}, bf16[384,2048]{1,0:T(8,128)(2,1)}, u32[]{:S(2)}, u32[]{:S(2)}) collective-permute-start(bf16[384,2048]{1,0:T(8,128)(2,1)} %get-tuple-element.212), channel_id=1, source_target_pairs={{0,8},{1,9},{2,10},{3,11},{4,12},{5,13},{6,14},{7,15},{8,0},{9,1},... | collective-permute-start | bytes 4718600 | tf_op jit(solution)/shard_map/ppermute | solution.py:361
  208.7 21.6 %collective-permute-start.36 = (bf16[192,2048]{1,0:T(8,128)(2,1)}, bf16[192,2048]{1,0:T(8,128)(2,1)S(1)}, u32[]{:S(2)}, u32[]{:S(2)}) collective-permute-start(bf16[192,2048]{1,0:T(8,128)(2,1)} %get-tuple-element.207), channel_id=1, source_target_pairs={{0,1},{1,0},{2,3},{3,2},{4,5},{5,4},{6,7},{7,6},{8,9},{9,8},{10,11... | collective-permute-start | bytes 2359304 | tf_op jit(solution)/shard_map/ppermute | solution.py:361
  210.2 20.1 %collective-permute-start.37 = (bf16[192,2048]{1,0:T(8,128)(2,1)}, bf16[192,2048]{1,0:T(8,128)(2,1)S(1)}, u32[]{:S(2)}, u32[]{:S(2)}) collective-permute-start(bf16[192,2048]{1,0:T(8,128)(2,1)} %get-tuple-element.208), channel_id=1, source_target_pairs={{0,16},{1,17},{2,18},{3,19},{4,20},{5,21},{6,22},{7,23},{8,24},{9,... | collective-permute-start | bytes 2359304 | tf_op jit(solution)/shard_map/ppermute | solution.py:361
  211.7 18.6 %collective-permute-start.38 = (bf16[128,2048]{1,0:T(8,128)(2,1)}, bf16[128,2048]{1,0:T(8,128)(2,1)S(1)}, u32[]{:S(2)}, u32[]{:S(2)}) collective-permute-start(bf16[128,2048]{1,0:T(8,128)(2,1)} %get-tuple-element.209), channel_id=1, source_target_pairs={{0,2},{1,3},{2,0},{3,1},{4,6},{5,7},{6,4},{7,5},{8,10},{9,11},{10,... | collective-permute-start | bytes 1572872 | tf_op jit(solution)/shard_map/ppermute | solution.py:361
  232.7 13.9 %collective-permute-start.40 = (bf16[128,2048]{1,0:T(8,128)(2,1)S(1)}, bf16[128,2048]{1,0:T(8,128)(2,1)S(1)}, u32[]{:S(2)}, u32[]{:S(2)}) collective-permute-start(bf16[128,2048]{1,0:T(8,128)(2,1)S(1)} %get-tuple-element.218), channel_id=1, source_target_pairs={{0,1},{1,0},{2,3},{3,2},{4,5},{5,4},{6,7},{7,6},{8,9},{9,8},{10,11... | collective-permute-start | bytes 1572872 | tf_op jit(solution)/shard_map/ppermute | solution.py:361
  233.9 13.4 %collective-permute-start.41 = (bf16[128,2048]{1,0:T(8,128)(2,1)S(1)}, bf16[128,2048]{1,0:T(8,128)(2,1)S(1)}, u32[]{:S(2)}, u32[]{:S(2)}) collective-permute-start(bf16[128,2048]{1,0:T(8,128)(2,1)S(1)} %get-tuple-element.219), channel_id=1, source_target_pairs={{0,16},{1,17},{2,18},{3,19},{4,20},{5,21},{6,22},{7,23},{8,24},{9,... | collective-permute-start | bytes 1572872 | tf_op jit(solution)/shard_map/ppermute | solution.py:361
  234.8 14.5 %collective-permute-start.42 = (bf16[128,2048]{1,0:T(8,128)(2,1)S(1)}, bf16[128,2048]{1,0:T(8,128)(2,1)S(1)}, u32[]{:S(2)}, u32[]{:S(2)}) collective-permute-start(bf16[128,2048]{1,0:T(8,128)(2,1)S(1)} %get-tuple-element.220), channel_id=1, source_target_pairs={{0,2},{1,3},{6,4},{7,5},{8,10},{9,11},{14,12},{15,13},{16,18},{17,... | collective-permute-start | bytes 1572872 | tf_op jit(solution)/shard_map/ppermute | solution.py:361
  251.3 14.9 %collective-permute-start.45 = (bf16[128,2048]{1,0:T(8,128)(2,1)S(1)}, bf16[128,2048]{1,0:T(8,128)(2,1)S(1)}, u32[]{:S(2)}, u32[]{:S(2)}) collective-permute-start(bf16[128,2048]{1,0:T(8,128)(2,1)S(1)} %get-tuple-element.226), channel_id=1, source_target_pairs={{2,4},{3,5},{4,2},{5,3},{10,12},{11,13},{12,10},{13,11},{18,20},{1... | collective-permute-start | bytes 1572872 | tf_op jit(solution)/shard_map/ppermute | solution.py:361
  252.0 15.9 %collective-permute-start.46 = (bf16[128,2048]{1,0:T(8,128)(2,1)S(1)}, bf16[128,2048]{1,0:T(8,128)(2,1)S(1)}, u32[]{:S(2)}, u32[]{:S(2)}) collective-permute-start(bf16[128,2048]{1,0:T(8,128)(2,1)S(1)} %get-tuple-element.226), channel_id=1, source_target_pairs={{0,2},{1,3},{6,4},{7,5},{8,10},{9,11},{14,12},{15,13},{16,18},{17,... | collective-permute-start | bytes 1572872 | tf_op jit(solution)/shard_map/ppermute | solution.py:361
  258.4 6.4 %collective-permute-start.43 = (bf16[64,2048]{1,0:T(8,128)(2,1)S(1)}, bf16[64,2048]{1,0:T(8,128)(2,1)S(1)}, u32[]{:S(2)}, u32[]{:S(2)}) collective-permute-start(bf16[64,2048]{1,0:T(8,128)(2,1)S(1)} %get-tuple-element.224), channel_id=1, source_target_pairs={{0,1},{1,0},{2,3},{3,2},{4,5},{5,4},{6,7},{7,6},{8,9},{9,8},{10,11... | collective-permute-start | bytes 786440 | tf_op jit(solution)/shard_map/ppermute | solution.py:361
  259.9 6.4 %collective-permute-start.44 = (bf16[64,2048]{1,0:T(8,128)(2,1)S(1)}, bf16[64,2048]{1,0:T(8,128)(2,1)S(1)}, u32[]{:S(2)}, u32[]{:S(2)}) collective-permute-start(bf16[64,2048]{1,0:T(8,128)(2,1)S(1)} %get-tuple-element.225), channel_id=1, source_target_pairs={{0,16},{1,17},{2,18},{3,19},{4,20},{5,21},{6,22},{7,23},{8,24},{9,... | collective-permute-start | bytes 786440 | tf_op jit(solution)/shard_map/ppermute | solution.py:361
  271.7 11.4 %collective-permute-start.47 = (bf16[128,2048]{1,0:T(8,128)(2,1)}, bf16[128,2048]{1,0:T(8,128)(2,1)S(1)}, u32[]{:S(2)}, u32[]{:S(2)}) collective-permute-start(bf16[128,2048]{1,0:T(8,128)(2,1)} %get-tuple-element.233), channel_id=1, source_target_pairs={{0,1},{1,0},{2,3},{3,2},{4,5},{5,4},{6,7},{7,6},{8,9},{9,8},{10,11... | collective-permute-start | bytes 1572872 | tf_op jit(solution)/shard_map/ppermute | solution.py:361
  273.2 11.1 %collective-permute-start.48 = (bf16[128,2048]{1,0:T(8,128)(2,1)}, bf16[128,2048]{1,0:T(8,128)(2,1)S(1)}, u32[]{:S(2)}, u32[]{:S(2)}) collective-permute-start(bf16[128,2048]{1,0:T(8,128)(2,1)} %get-tuple-element.234), channel_id=1, source_target_pairs={{0,16},{1,17},{2,18},{3,19},{4,20},{5,21},{6,22},{7,23},{8,24},{9,... | collective-permute-start | bytes 1572872 | tf_op jit(solution)/shard_map/ppermute | solution.py:361
  274.2 11.6 %collective-permute-start.49 = (bf16[128,2048]{1,0:T(8,128)(2,1)}, bf16[128,2048]{1,0:T(8,128)(2,1)S(1)}, u32[]{:S(2)}, u32[]{:S(2)}) collective-permute-start(bf16[128,2048]{1,0:T(8,128)(2,1)} %get-tuple-element.235), channel_id=1, source_target_pairs={{0,2},{1,3},{2,0},{3,1},{4,6},{5,7},{6,4},{7,5},{8,10},{9,11},{10,... | collective-permute-start | bytes 1572872 | tf_op jit(solution)/shard_map/ppermute | solution.py:361
  276.6 9.1 %collective-permute-start.50 = (bf16[128,2048]{1,0:T(8,128)(2,1)}, bf16[128,2048]{1,0:T(8,128)(2,1)S(1)}, u32[]{:S(2)}, u32[]{:S(2)}) collective-permute-start(bf16[128,2048]{1,0:T(8,128)(2,1)} %get-tuple-element.236), channel_id=1, source_target_pairs={{2,4},{3,5},{4,2},{5,3},{10,12},{11,13},{12,10},{13,11},{18,20},{1... | collective-permute-start | bytes 1572872 | tf_op jit(solution)/shard_map/ppermute | solution.py:361
  (23 other events, 345.6 us)
